TPU v7x, 32 devices: a whole 2x2x4 slice. The times are simulated.
32 devices in a mesh: rep: 8 (over y, x, core), shard: 4 (over z).
Axes of the slice: x: 2, y: 2, z: 4, core: 2. Of those that a mesh axis runs over, the one named last changes fastest.
Arguments:
- tokens: bfloat16 [32768, 1024], P(('rep', 'shard')), may hold values from -6 to 6
- cotangent: bfloat16 [32768, 1024], P(('rep', 'shard')), may hold values from -6 to 6
- seq_lengths: int32 [64], replicated, may hold values from 256 to 1024, as said below
- deal_order: int32 [64], replicated, may hold values from 0 to 63, as said below
- norm_gain: bfloat16 [1024], P('shard'), may hold values from 0.5 to 1.5
- in_proj: bfloat16 [1024, 4384], P('shard'), may hold values from -0.1875 to 0.1875
- conv_weight: bfloat16 [4, 2304], P(None, 'shard'), may hold values from -3 to 3
- conv_bias: bfloat16 [2304], P('shard'), may hold values from -1.5 to 0.5
- step_bias: bfloat16 [32], P('shard'), may hold values from -4.59375 to -2.296875
- decay_log: bfloat16 [32], P('shard'), may hold values from 0 to 2.078125
- skip_gain: bfloat16 [32], P('shard'), may hold values from 0.5 to 2
- gate_gain: bfloat16 [2048], P('shard'), may hold values from 0.5 to 1.5
- out_proj: bfloat16 [2048, 1024], P('shard'), may hold values from -0.125 to 0.125
Outputs:
- output: bfloat16 [32768, 1024], P(('rep', 'shard'))
- grad_tokens: bfloat16 [32768, 1024], P(('rep', 'shard'))
- grad_norm_gain: float32 [1024], P('shard')
- grad_in_proj: float32 [1024, 4384], P('shard')
- grad_conv_weight: float32 [4, 2304], P(None, 'shard')
- grad_conv_bias: float32 [2304], P('shard')
- grad_step_bias: float32 [32], P('shard')
- grad_decay_log: float32 [32], P('shard')
- grad_skip_gain: float32 [32], P('shard')
- grad_gate_gain: float32 [2048], P('shard')
- grad_out_proj: float32 [2048, 1024], P('shard')
Inputs may be any that keep to these rules, and one draw needn't show every extreme that they name: `seq_lengths`: each length is a multiple of 256. Taken in the order deal_order gives, the sequences fill each device's 1024 tokens exactly, whole sequences only, at most 3 on one device; some device holds a single sequence and some holds 3. `deal_order`: A permutation of the 64 sequence indices; entry j is the initial index of the j-th dealt sequence.
All inputs are finite; a program needn't handle non-finite values.
Results may differ from a plain program's by a relative error of at most 0.0075.
Values may be sent and summed in bfloat16 or wider, within the bound.
No kernel may reach another device: no remote copies, remote signals or barrier semaphores. Data moves between devices by JAX's collectives and lax.ppermute only.
A program may use at most 320 MiB of HBM per device.

v0:
```python
from functools import partial
from math import lcm

import jax
import jax.numpy as jnp
from jax import lax
from jax.experimental import pallas as pl
from jax.experimental.pallas import tpu as pltpu
from jax.sharding import PartitionSpec as P

D = 1024
DI = 2048
H = 32
P_SIZE = 64
NS = 128
CONVW = 4
CH = DI + 2 * NS
L = 256
LANES = 128
TILE = 256
EPSILON = 1e-05
LOG2E = 1.4426950408889634
VMEM = 58 << 20
F32 = jnp.float32
BF = jnp.bfloat16
NN = (((1,), (0,)), ((), ()))
NT = (((1,), (1,)), ((), ()))
TN = (((0,), (0,)), ((), ()))
BOTH = ("rep", "shard")


def dot(a, b, dims=NN):
    return lax.dot_general(a, b, dims, preferred_element_type=F32)


def sigmoid(v):
    return 0.5 * jnp.tanh(0.5 * v) + 0.5


def silu_and_slope(v):
    half = 0.5 * v
    bent = jnp.tanh(half)
    part = half * bent
    return half + part, (0.5 + 0.5 * bent) * (1.0 + half - part)


def split2(v):
    hi = v.astype(BF)
    return jnp.concatenate([hi, (v - hi.astype(F32)).astype(BF)], 1)


def tri_sum(tri, v):
    hi = v.astype(BF)
    rest = v - hi.astype(F32)
    mid = rest.astype(BF)
    low = (rest - mid.astype(F32)).astype(BF)
    got = dot(tri, jnp.concatenate([hi, mid, low], 1))
    return got[:, :LANES] + got[:, LANES : 2 * LANES] + got[:, 2 * LANES :]


def head_spread():
    row = lax.broadcasted_iota(jnp.int32, (2 * LANES, DI), 0)
    col = lax.broadcasted_iota(jnp.int32, (2 * LANES, DI), 1)
    return jnp.where((row % LANES) == col // P_SIZE, 1.0, 0.0).astype(BF)


def head_sum(v, e2, at):
    hi = v.astype(BF)
    low = (v - hi.astype(F32)).astype(BF)
    return dot(hi, e2[0:LANES, at], NT) + dot(low, e2[0:LANES, at], NT)


def triangle(kind, up):
    row = lax.broadcasted_iota(jnp.int32, (L, L), 0)
    col = lax.broadcasted_iota(jnp.int32, (L, L), 1)
    return jnp.where(row <= col if up else row >= col, 1.0, 0.0).astype(kind)


def tile_at(t, size=TILE):
    return pl.ds(pl.multiple_of(t * size, size), size)


def tiles(width, size=TILE):
    return [slice(t, t + size) for t in range(0, width, size)]


STEP = 64


def pieces_of(at):
    for lanes in range(at.start, at.stop, LANES):
        for q in range(0, L, STEP):
            yield slice(q, q + STEP), slice(lanes, lanes + LANES), slice(lanes - at.start, lanes - at.start + LANES)


def fold(v):
    return jnp.sum(v.reshape(STEP // 8, 8, LANES), 0)


def staged(parts, first, then):
    first(0, parts[0])
    for i, part in enumerate(parts):
        if i + 1 < len(parts):
            first(i + 1, parts[i + 1])
        then(i, part)


def slot_of(rep, reps):
    return lax.rem(rep, 2) * (reps // 2) + rep // 2


def span(first, size):
    return pl.ds(pl.multiple_of(first, 16), size)


def features(refs, place, part, shard, rep, reps):
    made = [(refs[0], place.at[shard])]
    for i, ref in enumerate(refs[1:]):
        first = slot_of(rep ^ i, reps) * part
        for k in range(1, ref.shape[0] + 1):
            source = ref.at[k - 1] if part == ref.shape[1] else ref.at[k - 1, pl.ds(0, part)]
            made.append((source, place.at[shard ^ k, span(first, part)]))
    return made


def rows_behind(own, refs, place, skip, shard, rep, reps):
    groups, n, _ = own.shape
    part = n // reps
    made = [(own.at[u], place.at[u, span(shard * n, n)]) for u in range(groups)]
    for i, ref in enumerate(refs):
        first = slot_of(rep ^ i, reps) * part
        for k in range(1, ref.shape[0] + 1):
            for u in range(groups):
                source = ref.at[k - 1, pl.ds(skip + u * part, part)]
                made.append((source, place.at[u, span((shard ^ k) * n + first, part)]))
    return made


def across(a, w, rows):
    m = w.shape[2]
    out = dot(a[:, 0:m], w[0, rows], NT)
    for s in range(1, w.shape[0]):
        out = out + dot(a[:, s * m : (s + 1) * m], w[s, rows], NT)
    return out


def copies_of(made, sems):
    return [pltpu.make_async_copy(source, place, sems.at[i]) for i, (source, place) in enumerate(made)]


def copy_count(reps, shards, each=1):
    return each + reps * (shards - 1) * each


def rms(x, gain):
    xf = x.astype(F32)
    inv = lax.rsqrt(jnp.mean(xf * xf, 1, keepdims=True) + EPSILON)
    return (xf * inv * gain).astype(BF)


def front_kernel(count, cont, x_ref, xh_ref, ng_ref, cw_ref, sp_ref, *rest):
    wrefs = rest[:count]
    (normed_ref, inner_ref, vp_ref, cs_ref, cin_ref, stp_ref, sig_ref, tot_ref, tott_ref, sloc_ref, fin_ref, nh_ref, ch_ref,
     cbuf, state, e2, part, weight, wc, sems) = rest[count:]
    b = pl.program_id(0)
    nb = pl.num_programs(0)
    gain = ng_ref[...]

    @pl.when(b == 0)
    def _():
        loads = copies_of(features(wrefs, wc, wc.shape[1] // (count - 1), cont[nb + 1], cont[nb + 2], count - 1), sems)
        for c in loads:
            c.start()
        e2[...] = head_spread()
        state[...] = jnp.zeros_like(state)
        halo = rms(xh_ref[...], gain)
        nh_ref[...] = jnp.zeros_like(nh_ref)
        nh_ref[0:16] = halo
        for c in loads:
            c.wait()
        for at in tiles(CH):
            c = across(halo, wc, at)[8:16]
            ch_ref[:, at] = c
            for u in range(TILE // LANES):
                cbuf[at.start // LANES + u, 0:8, :] = c[:, u * LANES : (u + 1) * LANES]

    @pl.when(b > 0)
    def _():
        cbuf[:, 0:8, :] = cbuf[:, L : L + 8, :]

    keep = cont[b].astype(F32)
    cbuf[:, 0:8, :] = cbuf[:, 0:8, :] * keep
    normed = rms(x_ref[...], gain)
    normed_ref[...] = normed

    raw = across(normed, wc, slice(CH, CH + LANES)) + sp_ref[0:1, :]
    small = jnp.exp(-jnp.abs(raw))
    series = small * (1.0 - small * (0.5 - small * (1.0 / 3.0)))
    step = jnp.maximum(raw, 0.0) + jnp.where(small < 0.01, series, jnp.log(1.0 + small))
    rate = -sp_ref[1:2, :] * step
    total = tri_sum(triangle(BF, False), rate)
    stp_ref[...] = step
    sig_ref[...] = sigmoid(raw)
    tot_ref[...] = total
    tott_ref[0] = total.T
    last = total[L - 1 : L, :]
    steps = split2(step)
    leaving = split2(jnp.exp(last - total))
    kept = dot(split2(jnp.exp(jnp.broadcast_to(last, (8, LANES)))), e2[...])[0:1]
    state[...] = state[...] * keep
    sloc_ref[0] = state[...].astype(BF)

    def project(i, at):
        c = across(normed, wc, at)
        for u in range(TILE // LANES):
            cbuf[at.start // LANES + u, 8 : L + 8, :] = c[:, u * LANES : (u + 1) * LANES]
        if at.start < DI:
            weight[i % 2, 0] = dot(steps, e2[:, at])
            weight[i % 2, 1] = dot(leaving, e2[:, at])

    def convolve(i, at):
        for rows, lanes, within in pieces_of(at):
            lo = 8 + rows.start
            buf = cbuf.at[lanes.start // LANES]
            here = buf[lo : lo + STEP, :]
            cin_ref[rows, lanes] = here.astype(BF)
            acc = cw_ref[4:5, lanes] + cw_ref[3:4, lanes] * here
            for back in range(1, CONVW):
                acc = acc + cw_ref[3 - back : 4 - back, lanes] * buf[lo - back : lo - back + STEP, :]
            v, slope = silu_and_slope(acc)
            cs_ref[rows, lanes] = slope.astype(BF)
            inner_ref[rows, lanes] = v.astype(BF)
            if at.start < DI:
                v = v * weight[i % 2, 0, rows, within]
                vp_ref[rows, lanes] = v.astype(BF)
                part[rows, lanes] = (v * weight[i % 2, 1, rows, within]).astype(BF)

    staged([slice(DI, CH)] + tiles(DI), project, convolve)
    keys = inner_ref[:, DI : DI + NS].T
    for at in tiles(DI):
        state[:, at] = state[:, at] * kept[:, at] + dot(keys, part[:, at])

    @pl.when(b == nb - 1)
    def _():
        fin_ref[...] = state[...].astype(BF)


def scan_kernel(cont, kq_ref, vp_ref, tot_ref, tott_ref, y_ref, gm):
    total = tot_ref[...] * LOG2E
    keys = kq_ref[:, :NS]
    queries = kq_ref[:, NS:]
    gm[...] = dot(queries, keys, NT) * triangle(F32, False)
    half = L // 2
    lane = lax.broadcasted_iota(jnp.int32, (L, LANES), 1)

    @pl.loop(0, H // 8)
    def _(g):
        cols = pltpu.roll(total, lax.rem(LANES - 8 * g, LANES), 1)
        rows = tott_ref[0, pl.ds(pl.multiple_of(g * 8, 8), 8), :] * LOG2E
        for pair in range(4):
            at = tile_at(g * 4 + pair, LANES)
            both = vp_ref[:, at]
            top, low = 0.0, 0.0
            for odd in range(2):
                i = 2 * pair + odd
                mine = jnp.where((lane >= P_SIZE) == (odd == 1), both, jnp.zeros_like(both))
                col = cols[:, i : i + 1]
                row = rows[i : i + 1, :]
                p0 = jnp.exp2(jnp.minimum(col[:half] - row[:, :half], 0.0)) * gm[:half, :half]
                p1 = jnp.exp2(col[half:] - row[:, :half]) * gm[half:, :half]
                p2 = jnp.exp2(jnp.minimum(col[half:] - row[:, half:], 0.0)) * gm[half:, half:]
                top = top + dot(p0.astype(BF), mine[:half])
                low = low + dot(jnp.concatenate([p1.astype(BF), p2.astype(BF)], 1), mine)
            y_ref[0:half, at] = top
            y_ref[half:L, at] = low


def gate_kernel(
    count, cont, x_ref, dy_ref, normed_ref, inner_ref, y_ref, tot_ref, sloc_ref, sin_ref, gg_ref, sk_ref, *rest
):
    grefs, own_ref = rest[:count], rest[count]
    (out_ref, gn_ref, dgate_ref, dmix_ref, yd_ref, sc_ref, dlead_ref, sums_ref,
     e2, gate, gated, dn, etot, yfull, dlead, lead, wg, wo, gsems, osems) = rest[count + 1 :]
    b = pl.program_id(0)
    nb = pl.num_programs(0)

    @pl.when(b == 0)
    def _():
        place = cont[nb + 1], cont[nb + 2], count - 1
        part = DI // (count - 1)
        loads = copies_of(features(grefs, wg, part, *place), gsems)
        loads += copies_of(rows_behind(own_ref, grefs[1:], wo, part, *place), osems)
        for c in loads:
            c.start()
        e2[...] = head_spread()
        dlead[...] = jnp.zeros_like(dlead)
        sums_ref[...] = jnp.zeros_like(sums_ref)
        lead[...] = jnp.ones_like(lead)
        for c in loads:
            c.wait()

    keep = cont[b].astype(F32)
    first = cont[0].astype(F32)
    lead[...] = lead[...] * jnp.where(b == 0, 1.0, keep)
    normed = normed_ref[...]
    queries = inner_ref[:, DI + NS :]
    reach = split2(jnp.exp(tot_ref[...]))
    square = jnp.zeros((L, TILE), F32)
    for at in tiles(DI):
        g = across(normed, wg, at)
        gate[:, at] = g
        start = (sloc_ref[0, :, at].astype(F32) + (lead[0:1, at] * first) * sin_ref[:, at].astype(F32)).astype(BF)
        sc_ref[0, :, at] = start
        e = dot(reach, e2[:, at])
        etot[:, at] = e
        y = y_ref[:, at] + e * dot(queries, start)
        yfull[:, at] = y
        v = (y + sk_ref[:, at] * inner_ref[:, at].astype(F32)) * silu_and_slope(g)[0]
        gated[:, at] = v
        square = square + v * v
    rinv = lax.rsqrt(jnp.sum(square, 1, keepdims=True) * (1.0 / DI) + EPSILON)
    for at in tiles(DI):
        gn_ref[:, at] = (gated[:, at] * rinv * gg_ref[:, at]).astype(BF)
    dy = dy_ref[...]
    inner_sum = jnp.zeros((L, TILE), F32)
    for at in tiles(DI):
        back = across(dy, wo, at)
        v = gated[:, at]
        sums_ref[0:1, at] += jnp.sum(back * (v * rinv), 0, keepdims=True)
        back = back * gg_ref[:, at]
        dn[:, at] = back
        inner_sum = inner_sum + back * v
    for u, at in enumerate(tiles(D, wo.shape[2])):
        out_ref[:, at] = (x_ref[:, at].astype(F32) + dot(gn_ref[...], wo[u])).astype(BF)
    shared = jnp.sum(inner_sum, 1, keepdims=True) * (1.0 / DI) * (rinv * rinv * rinv)
    turned = queries.T
    yd = jnp.zeros((L, LANES), F32)
    for at in tiles(DI):
        dgated = rinv * dn[:, at] - gated[:, at] * shared
        s, slope = silu_and_slope(gate[:, at])
        y = yfull[:, at]
        v = inner_ref[:, at].astype(F32)
        dgate_ref[:, at] = (dgated * (y + sk_ref[:, at] * v) * slope).astype(BF)
        dmix = (dgated * s).astype(BF)
        dmix_ref[:, at] = dmix
        dmix = dmix.astype(F32)
        sums_ref[1:2, at] += jnp.sum(dmix * v, 0, keepdims=True)
        yd = yd + head_sum(dmix * y, e2, at)
        dlead[:, at] += lead[0:1, at] * dot(turned, (dmix * etot[:, at]).astype(BF))
    yd_ref[...] = yd
    lead[...] = lead[...] * etot[L - 1 : L, :]

    @pl.when(b == nb - 1)
    def _():
        dlead_ref[...] = dlead[...].astype(BF)


def back_kernel(
    cont, kq_ref, vp_ref, cs_ref, cin_ref, stp_ref, sig_ref, tot_ref, tott_ref, sc_ref, dmix_ref, yd_ref, din_ref,
    cw_ref, sp_ref, sk_ref, ch_ref,
    gp_ref, turned_ref, gph_ref, turned_halo_ref, csum_ref, hsum_ref,
    dstate, e2, z, dbuf, gt, dgt, weight, sent, reached, ends, fine,
):
    nb = pl.num_programs(0)
    b = nb - 1 - pl.program_id(0)
    after = cont[b + 1].astype(F32)

    @pl.when(b == nb - 1)
    def _():
        e2[...] = head_spread()
        dstate[...] = din_ref[...].astype(F32)
        csum_ref[...] = jnp.zeros_like(csum_ref)
        hsum_ref[...] = jnp.zeros_like(hsum_ref)
        dbuf[:, L : L + 8, :] = jnp.zeros((CH // LANES, 8, LANES), F32)

    @pl.when(b < nb - 1)
    def _():
        dbuf[:, L : L + 8, :] = dbuf[:, 0:8, :] * after

    dstate[...] = dstate[...] * after
    step = stp_ref[...]
    total = tot_ref[...]
    last = total[L - 1 : L, :]
    keys = kq_ref[:, :NS]
    queries = kq_ref[:, NS:]
    gt[...] = dot(keys, queries, NT) * triangle(F32, True)
    dgt[...] = jnp.zeros_like(dgt)
    steps = split2(step)
    leaving = split2(jnp.exp(last - total))
    reach = split2(jnp.exp(total))
    kept = dot(split2(jnp.exp(jnp.broadcast_to(last, (8, LANES)))), e2[...])[0:1]

    turned = queries.T
    ended = dstate[...].astype(BF)

    def spread(i, at):
        z[:, at] = dot(keys, ended[:, at])
        weight[i % 2, 0] = dot(leaving, e2[:, at])
        weight[i % 2, 1] = dot(reach, e2[:, at])

    def reweigh(i, at):
        for u in range(TILE // LANES):
            summed = jnp.zeros((8, LANES), F32)
            for rows, lanes, _ in pieces_of(slice(at.start + u * LANES, at.start + (u + 1) * LANES)):
                within = slice(u * LANES, (u + 1) * LANES)
                w = weight[i % 2, 0, rows, within]
                scaled = w * z[rows, lanes]
                z[rows, lanes] = scaled
                v = vp_ref[rows, lanes].astype(F32)
                summed = summed + fold(v * scaled)
                sent[rows, lanes] = (v * w).astype(BF)
                reached[rows, lanes] = (dmix_ref[rows, lanes].astype(F32) * weight[i % 2, 1, rows, within]).astype(BF)
            ends[:, lanes] = summed

    staged(tiles(DI), spread, reweigh)
    dk = dot(sent[...], ended, NT)
    dq = dot(reached[...], sc_ref[0], NT)
    for at in tiles(DI):
        old = dstate[:, at] * kept[:, at]
        ends[:, at] += jnp.sum((old * sc_ref[0, :, at].astype(F32)).reshape(NS // 8, 8, TILE), 0)
        dstate[:, at] = old + dot(turned, reached[:, at])
    ends_hi = ends[...].astype(BF)
    ends_lo = (ends[...] - ends_hi.astype(F32)).astype(BF)
    at_end = dot(ends_hi, e2[0:LANES], NT) + dot(ends_lo, e2[0:LANES], NT)
    at_end = jnp.sum(at_end, 0, keepdims=True)
    scaled_total = total * LOG2E

    half = L // 2
    lane = lax.broadcasted_iota(jnp.int32, (L, LANES), 1)

    @pl.loop(0, H // 8)
    def _(g):
        cols = pltpu.roll(scaled_total, lax.rem(LANES - 8 * g, LANES), 1)
        rows = tott_ref[0, pl.ds(pl.multiple_of(g * 8, 8), 8), :] * LOG2E
        for pair in range(4):
            at = tile_at(g * 4 + pair, LANES)
            dy = dmix_ref[:, at]
            v = vp_ref[:, at]
            top = z[0:half, at]
            low = z[half:L, at]
            for odd in range(2):
                i = 2 * pair + odd
                mine = jnp.where((lane >= P_SIZE) == (odd == 1), dy, jnp.zeros_like(dy))
                col = cols[:, i : i + 1]
                row = rows[i : i + 1, :]
                e0 = jnp.exp2(jnp.minimum(row[:, :half] - col[:half], 0.0))
                e1 = jnp.exp2(row[:, half:] - col[:half])
                e2_ = jnp.exp2(jnp.minimum(row[:, half:] - col[half:], 0.0))
                p0 = (e0 * gt[:half, :half]).astype(BF)
                p1 = (e1 * gt[:half, half:]).astype(BF)
                p2 = (e2_ * gt[half:, half:]).astype(BF)
                top = top + dot(jnp.concatenate([p0, p1], 1), mine)
                low = low + dot(p2, mine[half:])
                d = dot(v[:half], mine, NT)
                dgt[:half, :half] += e0 * d[:, :half]
                dgt[:half, half:] += e1 * d[:, half:]
                dgt[half:, half:] += e2_ * dot(v[half:], mine[half:], NT)
            z[0:half, at] = top
            z[half:L, at] = low

    masked = (dgt[...] * triangle(F32, True)).astype(BF)
    dk = dk + dot(masked, queries)
    dq = dq + dot(masked, keys, TN)

    def respread(i, at):
        weight[i % 2, 0] = dot(steps, e2[:, at])

    def unwind(i, at):
        for rows, lanes, within in pieces_of(at):
            dvp = z[rows, lanes]
            p = dvp * vp_ref[rows, lanes].astype(F32)
            hi = p.astype(BF)
            fine[0, rows, lanes] = hi
            fine[1, rows, lanes] = (p - hi.astype(F32)).astype(BF)
            dv = weight[i % 2, 0, rows, within] * dvp + sk_ref[:, lanes] * dmix_ref[rows, lanes].astype(F32)
            dbuf[lanes.start // LANES, rows, :] = dv * cs_ref[rows, lanes].astype(F32)

    staged(tiles(DI), respread, unwind)
    own = dot(fine[0], e2[0:LANES], NT) + dot(fine[1], e2[0:LANES], NT)
    slope = cs_ref[:, DI:].astype(F32)
    dbuf[DI // LANES, 0:L, :] = dk * slope[:, :NS]
    dbuf[DI // LANES + 1, 0:L, :] = dq * slope[:, NS:]

    row = lax.broadcasted_iota(jnp.int32, (L, LANES), 0)
    dtotal = yd_ref[...] - own + jnp.where(row == L - 1, at_end, 0.0)
    drate = tri_sum(triangle(BF, True), dtotal)
    decay = sp_ref[1:2, :]
    dstep = own / jnp.maximum(step, 1e-30) - decay * drate
    draw = jnp.where(lax.broadcasted_iota(jnp.int32, (L, LANES), 1) < H, dstep * sig_ref[...], 0.0)
    gp_ref[:, CH : CH + LANES] = draw.astype(BF)
    turned_ref[CH : CH + LANES, :] = draw.astype(BF).T
    if gp_ref.shape[1] > CH + LANES:
        gp_ref[:, CH + LANES :] = jnp.zeros((L, gp_ref.shape[1] - CH - LANES), BF)
        turned_ref[CH + LANES :, :] = jnp.zeros((gp_ref.shape[1] - CH - LANES, L), BF)
    hsum_ref[0:1, :] += jnp.sum(draw, 0, keepdims=True)
    hsum_ref[1:2, :] += jnp.sum(-decay * step * drate, 0, keepdims=True)

    for lt in range(CH // LANES):
        at = slice(lt * LANES, (lt + 1) * LANES)
        sums = [jnp.zeros((8, LANES), F32) for _ in range(CONVW + 1)]
        made = []
        for q in range(L // 64):
            lo = 64 * q
            here = dbuf[lt, lo : lo + 64, :]
            c = cin_ref[lo : lo + 64, at].astype(F32)
            acc = cw_ref[3:4, at] * here
            sums[3] = sums[3] + jnp.sum((here * c).reshape(8, 8, LANES), 0)
            sums[4] = sums[4] + jnp.sum(here.reshape(8, 8, LANES), 0)
            for ahead in range(1, CONVW):
                there = dbuf[lt, lo + ahead : lo + ahead + 64, :]
                acc = acc + cw_ref[3 - ahead : 4 - ahead, at] * there
                sums[3 - ahead] = sums[3 - ahead] + jnp.sum((there * c).reshape(8, 8, LANES), 0)
            made.append(acc.astype(BF))
            gp_ref[lo : lo + 64, at] = made[-1]
        turned_ref[at, :] = jnp.concatenate(made, 0).T
        for k in range(CONVW + 1):
            csum_ref[k : k + 1, at] += jnp.sum(sums[k], 0, keepdims=True)

    @pl.when(b == 0)
    def _():
        gph_ref[...] = jnp.zeros_like(gph_ref)
        turned_halo_ref[...] = jnp.zeros_like(turned_halo_ref)
        for lt in range(CH // LANES):
            at = slice(lt * LANES, (lt + 1) * LANES)
            d = dbuf[lt, 0:8, :] * cont[0].astype(F32)
            d0, d1, d2 = d[0:1], d[1:2], d[2:3]
            w0, w1, w2 = cw_ref[0:1, at], cw_ref[1:2, at], cw_ref[2:3, at]
            c5, c6, c7 = ch_ref[5:6, at], ch_ref[6:7, at], ch_ref[7:8, at]
            made = [jnp.zeros((13, LANES), F32), w0 * d0, w1 * d0 + w0 * d1, w2 * d0 + w1 * d1 + w0 * d2]
            made = jnp.concatenate(made, 0)
            gph_ref[:, at] = made.astype(BF)
            turned_halo_ref[at, :] = jnp.concatenate([made, jnp.zeros((LANES - 16, LANES), F32)], 0).T.astype(BF)
            csum_ref[0:1, at] += c5 * d0 + c6 * d1 + c7 * d2
            csum_ref[1:2, at] += c6 * d0 + c7 * d1
            csum_ref[2:3, at] += c7 * d0


def wide_grad_kernel(cont, gn_ref, dy_ref, normed_ref, dgate_ref, out_ref, buf, sems):
    k = pl.program_id(0)
    reps, shards, _, m = buf.shape
    o = dot(gn_ref[...], dy_ref[...], TN).astype(BF)
    part = o.shape[0] // reps
    first = D // m * part
    each = reps // shards

    def copies(step):
        made = [(r, step, pl.ds(0, first)) for r in range(reps)]
        made += [(step * each + i, s, pl.ds(first, DI // reps)) for i in range(each) for s in range(shards)]
        return [
            pltpu.make_async_copy(buf.at[at], out_ref.at[at], sems.at[step, i]) for i, at in enumerate(made)
        ]

    for r in range(reps):
        for u in range(D // m):
            buf[r, k, u * part : (u + 1) * part, :] = o[r * part : (r + 1) * part, u * m : (u + 1) * m]
    part = DI // reps
    g = dot(dgate_ref[...], normed_ref[...], TN).astype(BF)
    for i in range(each):
        for s in range(shards):
            buf[k * each + i, s, first:, :] = g[i * part : (i + 1) * part, s * m : (s + 1) * m]
    for c in copies(k):
        c.start()

    @pl.when(k == shards - 1)
    def _():
        for step in range(shards):
            for c in copies(step):
                c.wait()


def conv_grad_kernel(nb, cont, normed_ref, turned_ref, nh_ref, turned_halo_ref, out_ref):
    half, _, part, _ = out_ref.shape
    full = (dot(turned_ref[...], normed_ref[...]) + dot(turned_halo_ref[...], nh_ref[...])).astype(BF)
    for chip in range(half):
        out_ref[(cont[nb + 2] // 2) ^ chip, 0] = full[chip * part : (chip + 1) * part]


def input_grad_kernel(convs, gates, cont, x_ref, dy_ref, gp_ref, dgate_ref, ahead_ref, ng_ref, *rest):
    crefs, grefs = rest[:convs], rest[convs : convs + gates]
    gt_ref, gn_ref, wc, wg, csems, gsems, acc = rest[convs + gates :]
    b = pl.program_id(0)
    nb = pl.num_programs(0)

    @pl.when(b == 0)
    def _():
        place = cont[nb + 1], cont[nb + 2], convs - 1
        loads = copies_of(features(crefs, wc, wc.shape[1] // (convs - 1), *place), csems)
        loads += copies_of(features(grefs, wg, DI // (convs - 1), *place), gsems)
        for c in loads:
            c.start()
        gn_ref[...] = jnp.zeros_like(gn_ref)
        for c in loads:
            c.wait()

    m = wc.shape[2]
    for s, at in enumerate(tiles(D, m)):
        acc[:, at] = dot(gp_ref[...], wc[s]) + dot(dgate_ref[...], wg[s])

    @pl.when(b == nb - 1)
    def _():
        keep = cont[nb].astype(F32)
        for s, at in enumerate(tiles(D, m)):
            acc[L - 16 : L, at] += keep * dot(ahead_ref[...], wc[s])

    for q in range(L // 32):
        rows = slice(32 * q, 32 * q + 32)
        x = x_ref[rows].astype(F32)
        inv = lax.rsqrt(jnp.mean(x * x, 1, keepdims=True) + EPSILON)
        g = acc[rows]
        gn_ref[...] += jnp.sum((g * (x * inv)).reshape(4, 8, D), 0)
        v = g * ng_ref[...]
        mean = jnp.mean(v * x, 1, keepdims=True)
        gt_ref[rows] = (inv * v - x * (inv * inv * inv * mean) + dy_ref[rows].astype(F32)).astype(BF)


def finish_wide_kernel(cont, wide_ref, gin_ref, gout_ref, buf, sem):
    reps, rows, m = wide_ref.shape
    part = DI // reps
    for r in range(reps):
        buf[r * part : (r + 1) * part, :] = wide_ref[r, rows - part :, :].astype(F32)
    copy = pltpu.make_async_copy(buf, gin_ref.at[pl.ds(0, DI)], sem)
    copy.start()
    part = (rows - part) * m // D
    for r in range(reps):
        for u in range(D // m):
            block = wide_ref[r, u * part : (u + 1) * part, :]
            gout_ref[r * part : (r + 1) * part, u * m : (u + 1) * m] = block.astype(F32)
    copy.wait()


def finish_conv_kernel(nb, count, part, cont, *rest):
    pieces = rest[:count]
    gin_ref, small_ref, buf, sem = rest[count + 1 :]
    for i, piece in enumerate(pieces):
        place = slot_of(cont[nb + 2] ^ i, count)
        buf[pl.ds(pl.multiple_of(place * part, 16), part), :] = piece[0:part].astype(F32)
    copy = pltpu.make_async_copy(buf.at[pl.ds(0, CH + H)], gin_ref.at[pl.ds(DI, CH + H)], sem)
    copy.start()
    half = small_ref.shape[0]
    small = jnp.zeros(small_ref.shape, F32)
    for piece in pieces:
        small = small + (piece[part : part + half].astype(F32) + piece[part + half :].astype(F32))
    small_ref[...] = small
    copy.wait()


def rows_of(width, reverse=0, column=0):
    if reverse:
        return pl.BlockSpec((L, width), lambda b, cont: (reverse - 1 - b, column))
    return pl.BlockSpec((L, width), lambda b, cont: (b, column))


def whole(*shape):
    return pl.BlockSpec(shape, lambda b, cont: (0,) * len(shape), pipeline_mode=pl.Buffered(1))


def fixed(*shape):
    return pl.BlockSpec(shape, lambda b, cont: (0,) * len(shape))


def lead_of(reverse, *shape):
    if reverse:
        return pl.BlockSpec((1, *shape), lambda b, cont: (reverse - 1 - b, 0, 0))
    return pl.BlockSpec((1, *shape), lambda b, cont: (b, 0, 0))


def anywhere(count):
    return [pl.BlockSpec(memory_space=pl.ANY)] * count


def call(kernel, grid, in_specs, out_specs, outs, scratch, flops, nbytes, name, aliases=None):
    return pl.pallas_call(
        kernel,
        grid_spec=pltpu.PrefetchScalarGridSpec(
            num_scalar_prefetch=1, grid=(grid,), in_specs=in_specs, out_specs=out_specs, scratch_shapes=scratch
        ),
        out_shape=[jax.ShapeDtypeStruct(s, d) for s, d in outs],
        input_output_aliases=aliases or {},
        compiler_params=pltpu.CompilerParams(vmem_limit_bytes=VMEM),
        cost_estimate=pl.CostEstimate(flops=flops, bytes_accessed=nbytes, transcendentals=0),
        name=name,
    )


def loaded(count, shards, *shape):
    return [pltpu.VMEM(shape, BF), pltpu.SemaphoreType.DMA((copy_count(count - 1, shards),))]


def front(cont, x, xh, ng, wc, cw, sp, shards):
    rows = x.shape[0]
    nb = rows // L
    count = len(wc)
    return call(
        partial(front_kernel, count), nb,
        [rows_of(D), whole(16, D), whole(1, D), whole(8, CH), whole(8, LANES), *anywhere(count)],
        [rows_of(D), rows_of(CH), rows_of(DI), rows_of(CH), rows_of(CH), rows_of(LANES), rows_of(LANES), rows_of(LANES),
         lead_of(0, LANES, L), lead_of(0, NS, DI), fixed(NS, DI), fixed(LANES, D), fixed(8, CH)],
        [((rows, D), BF), ((rows, CH), BF), ((rows, DI), BF), ((rows, CH), BF), ((rows, CH), BF), ((rows, LANES), F32),
         ((rows, LANES), F32), ((rows, LANES), F32), ((nb, LANES, L), F32), ((nb, NS, DI), BF), ((NS, DI), BF),
         ((LANES, D), BF), ((8, CH), F32)],
        [pltpu.VMEM((CH // LANES, L + 8, LANES), F32), pltpu.VMEM((NS, DI), F32), pltpu.VMEM((2 * LANES, DI), BF),
         pltpu.VMEM((L, DI), BF), pltpu.VMEM((2, 2, L, TILE), F32), *loaded(count, shards, shards, *wc[0].shape)],
        1_000_000, 1 << 20, "front",
    )(cont, x, xh, ng, cw, sp, *wc)


def scan(cont, inner, vp, tot, tott):
    rows = inner.shape[0]
    nb = rows // L
    return call(
        scan_kernel, nb,
        [rows_of(2 * NS, 0, DI // (2 * NS)), rows_of(DI), rows_of(LANES), lead_of(0, LANES, L)],
        [rows_of(DI)],
        [((rows, DI), F32)],
        [pltpu.VMEM((L, L), F32)],
        1_000_000, 1 << 20, "scan",
    )(cont, inner, vp, tot, tott)[0]


def gating(cont, x, dy, normed, inner, y, tot, sloc, sin, wg, wo_own, gg, sk, shards):
    rows = x.shape[0]
    nb = rows // L
    count = len(wg)
    wide = pltpu.VMEM((L, DI), F32)
    return call(
        partial(gate_kernel, count), nb,
        [rows_of(D), rows_of(D), rows_of(D), rows_of(CH), rows_of(DI), rows_of(LANES), lead_of(0, NS, DI), whole(NS, DI),
         whole(1, DI), whole(1, DI), *anywhere(count + 1)],
        [rows_of(D), rows_of(DI), rows_of(DI), rows_of(DI), rows_of(LANES), lead_of(0, NS, DI), fixed(NS, DI),
         fixed(8, DI)],
        [((rows, D), BF), ((rows, DI), BF), ((rows, DI), BF), ((rows, DI), BF), ((rows, LANES), F32),
         ((nb, NS, DI), BF), ((NS, DI), BF), ((8, DI), F32)],
        [pltpu.VMEM((2 * LANES, DI), BF), wide, wide, wide, wide, wide,
         pltpu.VMEM((NS, DI), F32), pltpu.VMEM((1, DI), F32), pltpu.VMEM((shards, *wg[0].shape), BF),
         pltpu.VMEM((wo_own.shape[0], DI, wo_own.shape[2]), BF),
         pltpu.SemaphoreType.DMA((copy_count(count - 1, shards),)),
         pltpu.SemaphoreType.DMA((copy_count(count - 1, shards, shards),))],
        35_000_000_000, 40 << 20, "gating",
    )(cont, x, dy, normed, inner, y, tot, sloc, sin, gg, sk, *wg, wo_own)


def back(cont, inner, vp, cs, cin, stp, sig, tot, tott, sc, dmix, yd, din, cw, sp, sk, ch, width):
    rows = inner.shape[0]
    nb = rows // L
    return call(
        back_kernel, nb,
        [rows_of(2 * NS, nb, DI // (2 * NS)), rows_of(DI, nb), rows_of(CH, nb), rows_of(CH, nb), rows_of(LANES, nb),
         rows_of(LANES, nb), rows_of(LANES, nb), lead_of(nb, LANES, L), lead_of(nb, NS, DI), rows_of(DI, nb),
         rows_of(LANES, nb), whole(NS, DI), whole(8, CH), whole(8, LANES), whole(1, DI), whole(8, CH)],
        [rows_of(width, nb), pl.BlockSpec((width, L), lambda b, cont: (0, nb - 1 - b)), fixed(16, width),
         fixed(width, LANES), fixed(8, CH), fixed(8, LANES)],
        [((rows, width), BF), ((width, rows), BF), ((16, width), BF), ((width, LANES), BF), ((8, CH), F32),
         ((8, LANES), F32)],
        [pltpu.VMEM((NS, DI), F32), pltpu.VMEM((2 * LANES, DI), BF), pltpu.VMEM((L, DI), F32),
         pltpu.VMEM((CH // LANES, L + 8, LANES), F32), pltpu.VMEM((L, L), F32), pltpu.VMEM((L, L), F32),
         pltpu.VMEM((2, 2, L, TILE), F32), pltpu.VMEM((L, DI), BF), pltpu.VMEM((L, DI), BF), pltpu.VMEM((8, DI), F32),
         pltpu.VMEM((2, L, DI), BF)],
        60_000_000_000, 30 << 20, "back",
    )(cont, inner, vp, cs, cin, stp, sig, tot, tott, sc, dmix, yd, din, cw, sp, sk, ch)


def wide_grad(cont, gn, dy, normed, dgate, reps, shards):
    rows = dy.shape[0]
    block = DI // shards
    shape = (reps, shards, 2 * DI // reps, D // shards)
    return call(
        wide_grad_kernel, shards,
        [pl.BlockSpec((rows, block), lambda k, c: (0, k)), whole(rows, D), whole(rows, D),
         pl.BlockSpec((rows, block), lambda k, c: (0, k))],
        anywhere(1),
        [(shape, BF)],
        [pltpu.VMEM(shape, BF), pltpu.SemaphoreType.DMA((shards, 2 * reps))], 8_600_000_000, 24 << 20, "wide_grad",
    )(cont, gn, dy, normed, dgate)[0]


def conv_grad(cont, normed, turned, nh, turned_halo, reps, shards, other):
    width, rows = turned.shape
    nb = rows // L
    m = D // shards
    half, part = width // 2, width // reps
    return call(
        partial(conv_grad_kernel, nb), shards,
        [pl.BlockSpec((rows, m), lambda k, c: (0, c[nb + 1] ^ k)),
         pl.BlockSpec((half, rows), lambda k, c: (lax.rem(c[nb + 2], 2) ^ other, 0)),
         pl.BlockSpec((LANES, m), lambda k, c: (0, c[nb + 1] ^ k)),
         pl.BlockSpec((half, LANES), lambda k, c: (lax.rem(c[nb + 2], 2) ^ other, 0))],
        [pl.BlockSpec((reps // 2, 1, part, m), lambda k, c: (0, k, 0, 0))],
        [((reps // 2, shards, part, m), BF)],
        [], 5_000_000_000, 8 << 20, "conv_grad",
    )(cont, normed, turned, nh, turned_halo)[0]


def input_grad(cont, x, dy, gp, dgate, ahead, ng, wc, wg, shards):
    rows, width = gp.shape
    nb = rows // L
    convs, gates = len(wc), len(wg)
    return call(
        partial(input_grad_kernel, convs, gates), nb,
        [rows_of(D), rows_of(D), rows_of(width), rows_of(DI), whole(16, width), whole(1, D), *anywhere(convs + gates)],
        [rows_of(D), fixed(8, D)],
        [((rows, D), BF), ((8, D), F32)],
        [pltpu.VMEM((shards, *wc[0].shape), BF), pltpu.VMEM((shards, *wg[0].shape), BF),
         pltpu.SemaphoreType.DMA((copy_count(convs - 1, shards),)), pltpu.SemaphoreType.DMA((copy_count(gates - 1, shards),)),
         pltpu.VMEM((L, D), F32)],
        10_000_000_000, 24 << 20, "input_grad",
    )(cont, x, dy, gp, dgate, ahead, ng, *wc, *wg)


def finish_wide(cont, wide):
    reps, rows, m = wide.shape
    shards = D // m
    return call(
        finish_wide_kernel, 1,
        [whole(*wide.shape)],
        [pl.BlockSpec(memory_space=pl.ANY), fixed(DI // shards, D)],
        [((DI + CH + H, m), F32), ((DI // shards, D), F32)],
        [pltpu.VMEM((DI, m), F32), pltpu.SemaphoreType.DMA],
        1_000_000, 8 << 20, "finish_wide",
    )(cont, wide)


def finish_conv(cont, nb, pieces, gin, part):
    rows, m = pieces[0].shape
    count = len(pieces)
    return call(
        partial(finish_conv_kernel, nb, count, part), 1,
        [*[whole(rows, m)] * count, pl.BlockSpec(memory_space=pl.ANY)],
        [pl.BlockSpec(memory_space=pl.ANY), fixed((rows - part) // 2, m)],
        [(gin.shape, F32), (((rows - part) // 2, m), F32)],
        [pltpu.VMEM((count * part, m), F32), pltpu.SemaphoreType.DMA],
        1_000_000, 5 << 20, "finish_conv", {1 + count: 0},
    )(cont, *pieces, gin)


def shift(v, by):
    n = lax.axis_size(BOTH)
    return lax.ppermute(v, BOTH, [(i, (i + by) % n) for i in range(n)])


def swap(v, mask):
    n = lax.axis_size(BOTH)
    return lax.ppermute(v, BOTH, [(i, i ^ mask) for i in range(n)])


def part_of(w):
    reps = lax.axis_size("rep")
    part = w.shape[0] // reps
    return lax.dynamic_slice(w, (slot_of(lax.axis_index("rep"), reps) * part, 0), (part, w.shape[1]))


def over_reps(column):
    reps, shards = lax.axis_size("rep"), lax.axis_size("shard")
    return [column] + [swap(column, 2 * shards * j) for j in range(1, reps // 2)]


def over_cores(plane):
    shards = lax.axis_size("shard")
    other = [swap(v, shards) for v in plane]
    return [v for pair in zip(plane, other) for v in pair]


def after(value, *first):
    return lax.optimization_barrier((value, first))[0]


def total_of(first, *others):
    out = first.astype(F32)
    for v in others:
        out = out + v.astype(F32)
    return out.astype(first.dtype)


def two_halves(v, m):
    rows = -(-v.size // (16 * m)) * 16
    v = jnp.pad(v, (0, rows * m - v.size)).reshape(rows, m)
    hi = v.astype(BF)
    return jnp.concatenate([hi, (v - hi.astype(F32)).astype(BF)], 0)


def one_value(v):
    half = v.shape[0] // 2
    return v[:half].astype(F32) + v[half:].astype(F32)


def local(
    tokens, cotangent, seq_lengths, deal_order, norm_gain, in_proj, conv_weight, conv_bias, step_bias, decay_log,
    skip_gain, gate_gain, out_proj,
):
    n = lax.axis_size(BOTH)
    me = lax.axis_index(BOTH)
    reps, shards = lax.axis_size("rep"), lax.axis_size("shard")
    rep, mine = lax.axis_index("rep"), lax.axis_index("shard")
    rows = tokens.shape[0]
    nb = rows // L
    unit = lcm(LANES, 16 * reps)
    width = -(-(CH + LANES) // unit) * unit

    seqs = seq_lengths.shape[0]
    order = jnp.arange(seqs, dtype=jnp.int32)
    starts = jnp.sum(jnp.where(order[None, :] < order[:, None], seq_lengths[None, :], 0), 1)
    edge = (me * nb + jnp.arange(nb + 1, dtype=jnp.int32)) * L
    cont = jnp.where(jnp.any(starts[None, :] == edge[:, None], 1) | (edge >= n * rows), 0, 1)
    cont = jnp.concatenate([cont.astype(jnp.int32), jnp.stack([mine, rep]).astype(jnp.int32)])

    turned = in_proj.T
    wcs = jnp.pad(turned[DI:], ((0, width - CH - H), (0, 0)))
    wgs = turned[:DI]
    m = wcs.shape[1]
    own_small = [*conv_weight, conv_bias, gate_gain, norm_gain, step_bias, decay_log, skip_gain]
    count = sum(v.size for v in own_small)
    extra = -(-count // (16 * m)) * 16
    small, at = jnp.zeros((extra * m,), BF), 0
    for v in own_small:
        small = small + lax.pad(v, jnp.zeros((), BF), [(at, extra * m - at - v.size, 0)])
        at += v.size
    piece = jnp.concatenate([part_of(wcs), small.reshape(extra, m)], 0)
    small = small[:count]
    part = width // reps
    column = [swap(piece, k) for k in range(1, shards)]
    small = jnp.stack([small] + [v[part:].reshape(-1)[:count] for v in column])
    conv_column = jnp.stack(column)
    halo = shift(tokens[rows - 16 :], 1)
    wo_own = jnp.stack([out_proj[:, at] for at in tiles(D, m)])
    out_rows = out_proj.shape[0] // reps
    out_part = lax.dynamic_slice(wo_own, (0, slot_of(rep, reps) * out_rows, 0), (D // m, out_rows, m))
    piece = jnp.concatenate([part_of(wgs), out_part.reshape(-1, m)], 0)
    gate_column = lax.all_gather(piece, "shard", axis=0)
    gate_column = jnp.take(gate_column, mine ^ jnp.arange(1, shards), axis=0)
    small = jnp.take(small, mine ^ jnp.arange(shards), axis=0).astype(F32)
    sizes = [conv_weight.size, conv_bias.size, gate_gain.size, norm_gain.size, step_bias.size, decay_log.size,
             skip_gain.size]
    parts, at = [], 0
    for size in sizes:
        parts.append(small[:, at : at + size])
        at += size
    taps = parts[0].reshape(shards, CONVW, -1).transpose(1, 0, 2).reshape(CONVW, CH)
    cw = jnp.concatenate([taps, parts[1].reshape(1, CH), jnp.zeros((3, CH), F32)], 0)
    gg = parts[2].reshape(1, DI)
    ng = parts[3].reshape(1, D)
    rate_scale = jnp.exp(parts[5].reshape(1, H))
    sp = jnp.pad(jnp.concatenate([parts[4].reshape(1, H), rate_scale], 0), ((0, 6), (0, LANES - H)))
    sk = jnp.repeat(parts[6].reshape(1, H), P_SIZE, axis=1)

    conv_plane = over_reps(conv_column)
    wc = [wcs, *over_cores(conv_plane[:1] + after(conv_plane[1:], gate_column))]
    gate_plane = over_reps(after(gate_column, conv_plane))

    normed, inner, vp, cs, cin, stp, sig, tot, tott, sloc, fin, nh, ch = front(cont, tokens, halo, ng, wc, cw, sp, shards)
    sin = shift(fin, 1)
    y = scan(cont, inner, vp, tot, tott)
    wg = [wgs, *over_cores(gate_plane[:1] + after(gate_plane[1:], y, sin))]
    output, gn, dgate, dmix, yd, sc, dlead, sums = gating(
        cont, tokens, cotangent, normed, inner, y, tot, sloc, sin, wg, wo_own, gg, sk, shards
    )
    din = shift(dlead, -1)
    wide = after(wide_grad(cont, gn, cotangent, normed, dgate, reps, shards), din)
    wide = lax.psum_scatter(wide, "rep", scatter_dimension=0, tiled=True)[0]
    gp, turned_gp, gph, turned_gph, csum, hsum = back(cont, inner, vp, cs, cin, stp, sig, tot, tott, sc, dmix, yd, din, cw, sp, sk, ch, width)

    ahead = shift(gph, -1)
    theirs = swap(after(conv_grad(cont, normed, turned_gp, nh, turned_gph, reps, shards, 1), ahead), shards)
    w = conv_grad(cont, normed, turned_gp, nh, turned_gph, reps, shards, 0)
    w = [total_of(w[j], theirs[j]) for j in range(reps // 2)]
    gp = after(gp, w, wide)
    wide = lax.psum_scatter(after(wide, w), "shard", scatter_dimension=0, tiled=True)[0]
    grad_tokens, grad_norm = input_grad(cont, tokens, cotangent, gp, dgate, ahead, ng, wc, wg, shards)
    packed = jnp.concatenate(
        [csum[0:CONVW].reshape(CONVW, shards, -1).transpose(1, 0, 2).reshape(shards, -1), csum[4].reshape(shards, -1),
         sums[0].reshape(shards, -1), grad_norm.sum(0).reshape(shards, -1), hsum[0, :H].reshape(shards, -1),
         hsum[1, :H].reshape(shards, -1), sums[1].reshape(H, P_SIZE).sum(1).reshape(shards, -1)], 1)
    packed = jnp.take(packed, mine ^ jnp.arange(shards), axis=0)
    others = [swap(w[j], 2 * shards * j) for j in range(1, reps // 2)]
    others, wide, packed = lax.optimization_barrier((others, wide, packed))
    w = total_of(w[0], *others)
    wide = lax.all_gather(wide, "rep", axis=0)
    w = [jnp.concatenate([w[k], two_halves(packed[k], m)], 0) for k in range(shards)]
    w = w[:1] + [swap(w[k], k) for k in range(1, shards)]
    rest = sum(one_value(v[part:]) for v in w)
    w = jnp.concatenate([total_of(*[v[:part] for v in w]), two_halves(rest.reshape(-1), m)], 0)
    pieces = over_cores(over_reps(w))
    gin, grad_out = finish_wide(cont, wide)
    grad_in, small = finish_conv(cont, nb, pieces, gin, part)
    grad_in = grad_in.T
    own = small.reshape(-1)
    got, at = [], 0
    for size in sizes:
        got.append(own[at : at + size])
        at += size
    return (
        output, grad_tokens, got[3], grad_in, got[0].reshape(CONVW, -1), got[1], got[4], got[5], got[6], got[2],
        grad_out,
    )


def solution(mesh):
    both = P(BOTH, None)
    in_specs = (
        both, both, P(), P(), P("shard"), P("shard", None), P(None, "shard"), P("shard"), P("shard"), P("shard"),
        P("shard"), P("shard"), P("shard", None),
    )
    out_specs = (
        both, both, P("shard"), P("shard", None), P(None, "shard"), P("shard"), P("shard"), P("shard"), P("shard"),
        P("shard"), P("shard", None),
    )
    return jax.shard_map(local, mesh=mesh, in_specs=in_specs, out_specs=out_specs, check_vma=False)
```

profile of v0, /device:TPU:0, one launch (start us, length us, event | category | flops | bytes accessed | tf_op | source)
XLA Modules:
  0.0 325.1 jit_solution(7130026470508909721)
XLA Ops:
  7.2 0.9 slice_reduce_fusion.10
  8.1 0.9 pad_add_fusion
  9.6 1.4 slice.253
  11.0 0.7 pad_maximum_fusion.7
  11.7 5.0 %collective-permute-start.3 = (bf16[320,256]{1,0:T(8,128)(2,1)}, bf16[320,256]{1,0:T(8,128)(2,1)}, u32[]{:S(2)}, u32[]{:S(2)}) collective-permute-start(bf16[320,256]{1,0:T(8,128)(2,1)} %pad_maximum_fusion.7), channel_id=1, source_target_pairs={{0,3},{1,2},{2,1},{3,0},{4,7},{5,6},{6,5},{7,4},{8,11},{9,10},{10,... | collective-permute-start | bytes 491528 | tf_op jit(solution)/shard_map/ppermute | solution.py:842
  17.3 1.4 slice.187
  18.7 1.5 collective-permute-start
  20.1 1.3 slice.265.rest_0_.rest_9_
  21.5 1.0 slice_bitcast_fusion.3
  22.5 1.2 pad_maximum_fusion.rest_9_
  23.8 0.8 pad_maximum_fusion.2
  24.8 0.8 select_reduce_fusion
  26.3 0.7 stack.50
  27.0 1.1 pad.61.rest_0_
  28.3 3.4 %collective-permute-done.2 = bf16[320,256]{1,0:T(8,128)(2,1)} collective-permute-done((bf16[320,256]{1,0:T(8,128)(2,1)}, bf16[320,256]{1,0:T(8,128)(2,1)}, u32[]{:S(2)}, u32[]{:S(2)}) %collective-permute-start.2) | collective-permute-done | bytes 163872 | tf_op jit(solution)/shard_map/ppermute | solution.py:842
  31.6 1.2 pad_maximum_fusion.1.rest_1_
  32.8 2.5 collective-permute-start.7
  36.4 0.7 slice_bitcast_fusion.9
  37.1 0.7 slice_bitcast_fusion.10
  37.8 0.7 slice_bitcast_fusion.11
  39.7 13.5 %all-gather.5.cloned.1.call-done = bf16[2048,256]{1,0:T(8,128)(2,1)} async-done(((bf16[512,256]{1,0:T(8,128)(2,1)}), bf16[2048,256]{1,0:T(8,128)(2,1)}) %all-gather.5.cloned.1.call-update) | async-done | bytes 1048592 | tf_op jit(solution)/shard_map/all_gather | solution.py:927
  53.3 1.8 gather_fusion.1
  55.3 1.3 collective-permute-done.6.rest_5_
  56.8 0.7 maximum_maximum_fusion.cw_ref
  58.7 1.7 collective-permute-start.15
  60.3 1.3 collective-permute-start.14
  63.1 25.9 %front.1 = (bf16[1024,1024]{1,0:T(8,128)(2,1)}, bf16[1024,2304]{1,0:T(8,128)(2,1)}, bf16[1024,2048]{1,0:T(8,128)(2,1)}, bf16[1024,2304]{1,0:T(8,128)(2,1)}, bf16...) custom-call(s32[7]{0:T(128)} %pad_add_fusion.1.cont, ...), custom_call_target="tpu_custom_call" | custom-call | flops 1000000 | bytes 1048576 | tf_op jit(solution)/shard_map/front/pallas_call | solution.py:693
  89.5 14.2 %scan.1.y_ref = f32[1024,2048]{1,0:T(8,128)} custom-call(s32[7]{0:T(128)} %pad_add_fusion.1.cont, bf16[1024,2304]{1,0:T(8,128)(2,1)} %get-tuple-element.64.kq_ref.inner_ref, bf16[1024,2048]{1,0:T(8,128)(2,1)} %get-tuple-element.65.vp_ref, f32[1024,128]{1,0:T(8,128)} %get-tuple-element.66.tot_ref, f32[4,128,256]{2,1,0:T(8,128)} %get-tuple-element.67.tott_ref), custom_call_target="tpu_custom_call" | custom-call | flops 1000000 | bytes 1048576 | tf_op jit(solution)/shard_map/scan/pallas_call | solution.py:710
  103.8 2.6 collective-permute-done.11.sin_ref
  108.0 0.7 broadcast_in_dim.71.sk_ref
  108.6 1.3 collective-permute-done.16.rest_4_.rest_13_
  110.1 1.1 collective-permute-done.18.rest_8_.rest_17_
  111.2 38.2 %gating.1 = (bf16[1024,1024]{1,0:T(8,128)(2,1)}, bf16[1024,2048]{1,0:T(8,128)(2,1)}, bf16[1024,2048]{1,0:T(8,128)(2,1)}, bf16[1024,2048]{1,0:T(8,128)(2,1)}, f32...) custom-call(s32[7]{0:T(128)} %pad_add_fusion.1.cont, ...), custom_call_target="tpu_custom_call" | custom-call | flops 35000000512 | bytes 41943040 | tf_op jit(solution)/shard_map/gating/pallas_call | solution.py:725
  149.5 2.8 collective-permute-start.19
  152.3 15.3 %wide_grad.1 = bf16[8,4,512,256]{3,2,1,0:T(8,128)(2,1)} custom-call(s32[7]{0:T(128)} %pad_add_fusion.1.cont, bf16[1024,2048]{1,0:T(8,128)(2,1)} %get-tuple-element.90.gn_ref, bf16[1024,1024]{1,0:T(8,128)(2,1)} %dy_ref.5, bf16[1024,1024]{1,0:T(8,128)(2,1)} %get-tuple-element.63.normed_ref, bf16[1024,2048]{1,0:T(8,128)(2,1)} %get-tuple-element.91.dgate_ref), custom_call_target="tpu_custom_call" | custom-call | flops 8600000512 | bytes 25165824 | tf_op jit(solution)/shard_map/wide_grad/pallas_call | solution.py:766
  167.6 0.8 copy-done.21
  168.4 46.1 %back.1 = (bf16[1024,2432]{1,0:T(8,128)(2,1)}, bf16[2432,1024]{1,0:T(8,128)(2,1)}, bf16[16,2432]{1,0:T(8,128)(2,1)}, bf16[2432,128]{1,0:T(8,128)(2,1)}, f32[8,2304]{1,0:T(8,128)}, /*index=5*/f32[8,128]{1,0:T(8,128)}) custom-call(s32[7]{0:T(128)} %pad_add_fusion.1.cont, bf16[1024,2304]{1,0:T(8,128)(2,1)} %get-tuple-element.64.kq_ref.inner_ref, ...), custom_call_target="tpu_custom_call" | custom-call | flops 60000002048 | bytes 31457280 | tf_op jit(solution)/shard_map/back/pallas_call | solution.py:745
  214.9 7.8 %conv_grad.3 = bf16[4,4,304,256]{3,2,1,0:T(8,128)(2,1)} custom-call(s32[7]{0:T(128)} %pad_add_fusion.1.cont, bf16[1024,1024]{1,0:T(8,128)(2,1)} %get-tuple-element.63.normed_ref, bf16[2432,1024]{1,0:T(8,128)(2,1)} %get-tuple-element.85.turned_ref, bf16[128,1024]{1,0:T(8,128)(2,1)} %get-tuple-element.86.nh_ref, ...), custom_call_target="tpu_custom_call" | custom-call | flops 5000000000 | bytes 8388608 | tf_op jit(solution)/shard_map/conv_grad/pallas_call | solution.py:781
  222.7 7.7 %conv_grad.2 = bf16[4,4,304,256]{3,2,1,0:T(8,128)(2,1)} custom-call(s32[7]{0:T(128)} %pad_add_fusion.1.cont, bf16[1024,1024]{1,0:T(8,128)(2,1)} %get-tuple-element.63.normed_ref, bf16[2432,1024]{1,0:T(8,128)(2,1)} %get-tuple-element.85.turned_ref, bf16[128,1024]{1,0:T(8,128)(2,1)} %get-tuple-element.86.nh_ref, ...), custom_call_target="tpu_custom_call" | custom-call | flops 5000000000 | bytes 8388608 | tf_op jit(solution)/shard_map/conv_grad/pallas_call | solution.py:781
  230.5 2.3 fusion.3
  232.8 3.7 %reduce-scatter.3.cloned.1.call-done = bf16[1,4,512,256]{3,2,1,0:T(8,128)(2,1)} async-done(((bf16[8,4,512,256]{3,2,1,0:T(8,128)(2,1)}), bf16[1,4,512,256]{3,2,1,0:T(8,128)(2,1)}) %reduce-scatter.3.cloned.1.call-update) | async-done | bytes 1048592 | tf_op jit(solution)/shard_map/reduce_scatter | solution.py:957
  236.8 1.0 slice_reduce_fusion.5
  238.0 0.8 slice_reduce_fusion.11
  239.3 1.5 collective-permute-start.24
  240.8 1.4 collective-permute-start.23
  242.2 0.7 collective-permute-start.22
  242.9 21.2 %input_grad.1 = (bf16[1024,1024]{1,0:T(8,128)(2,1)}, f32[8,1024]{1,0:T(8,128)}) custom-call(s32[7]{0:T(128)} %pad_add_fusion.1.cont, bf16[1024,1024]{1,0:T(8,128)(2,1)} %x_ref.5, bf16[1024,1024]{1,0:T(8,128)(2,1)} %dy_ref.5, bf16[1024,2432]{1,0:T(8,128)(2,1)} %get-tuple-element.93.gp_ref, bf16[1024,2048]{1,0:T(8,128)(2,1)} %get-tuple-element.91.dgate_ref, ...), custom_call_target="tpu_custom_call" | custom-call | flops 10000000000 | bytes 25165824 | tf_op jit(solution)/shard_map/input_grad/pallas_call | solution.py:797
  264.1 0.8 reduce_sum.28
  265.7 3.8 %collective-permute-done.23 = bf16[4,304,256]{2,1,0:T(8,128)(2,1)} collective-permute-done((bf16[4,304,256]{2,1,0:T(8,128)(2,1)S(1)}, bf16[4,304,256]{2,1,0:T(8,128)(2,1)}, u32[]{:S(2)}, u32[]{:S(2)}) %collective-permute-start.23) | collective-permute-done | bytes 622624 | tf_op jit(solution)/shard_map/ppermute | solution.py:842
  269.8 1.6 add_convert_fusion
  271.5 2.5 collective-permute-start.26
  274.0 1.5 collective-permute-start.27
  275.7 11.4 %collective-permute-done.26 = bf16[336,256]{1,0:T(8,128)(2,1)S(1)} collective-permute-done((bf16[336,256]{1,0:T(8,128)(2,1)S(1)}, bf16[336,256]{1,0:T(8,128)(2,1)S(1)}, u32[]{:S(2)}, u32[]{:S(2)}) %collective-permute-start.26) | collective-permute-done | bytes 172064 | tf_op jit(solution)/shard_map/ppermute | solution.py:842
  287.8 1.5 collective-permute-start.33
  289.3 1.4 collective-permute-start.31
  290.7 0.7 collective-permute-start.29
  291.3 7.4 %collective-permute-done.33.rest_6_ = bf16[336,256]{1,0:T(8,128)(2,1)S(1)} collective-permute-done((bf16[336,256]{1,0:T(8,128)(2,1)S(1)}, bf16[336,256]{1,0:T(8,128)(2,1)S(1)}, u32[]{:S(2)}, u32[]{:S(2)}) %collective-permute-start.33) | collective-permute-done | bytes 172064 | tf_op jit(solution)/shard_map/ppermute | solution.py:842
  298.7 2.5 collective-permute-done.31.rest_4_
  301.2 0.7 collective-permute-done.29.rest_2_
  301.9 1.8 all-gather.7.cloned.1.call-done
  303.8 5.0 %finish_wide.1 = (f32[4384,256]{1,0:T(8,128)}, f32[512,1024]{1,0:T(8,128)}) custom-call(s32[7]{0:T(128)} %pad_add_fusion.1.cont, bf16[8,512,256]{2,1,0:T(8,128)(2,1)} %bitcast.74), custom_call_target="tpu_custom_call" | custom-call | flops 1000000 | bytes 8388608 | tf_op jit(solution)/shard_map/finish_wide/pallas_call | solution.py:812
  309.7 4.3 %finish_conv.1 = (f32[4384,256]{1,0:T(8,128)}, f32[16,256]{1,0:T(8,128)}) custom-call(s32[7]{0:T(128)} %pad_add_fusion.1.cont, bf16[336,256]{1,0:T(8,128)(2,1)} %copy-done.5, bf16[336,256]{1,0:T(8,128)(2,1)} %copy-done.12, bf16[336,256]{1,0:T(8,128)(2,1)} %copy-done.11, bf16[336,256]{1,0:T(8,128)(2,1)} %copy-done.15, ...), custom_call_target="tpu_custom_call", output_to_operand_aliasing={{0}: (9, {})} | custom-call | flops 1000000 | bytes 5242880 | tf_op jit(solution)/shard_map/finish_conv/pallas_call | solution.py:825
  314.0 0.7 copy.33
  317.2 1.4 reshape.203
  (181 shorter events, 16.5 us)
Async XLA Ops:
  7.2 46.1 %all-gather.5.cloned.1.call-start = ((), (), s32[]{:S(2)}) async-start(), calls=%async_computation.4 | async-start | bytes 1310720 | tf_op jit(solution)/shard_map/all_gather | solution.py:927
  9.0 0.6 copy-start.16
  10.9 10.5 %copy-start.3 = (bf16[512,1024]{1,0:T(8,128)(2,1)S(1)}, bf16[512,1024]{1,0:T(8,128)(2,1)}, u32[]{:S(2)}) copy-start(bf16[512,1024]{1,0:T(8,128)(2,1)} %param.24) | copy-start | bytes 3145732
  11.7 16.6 %collective-permute-start.3 = (bf16[320,256]{1,0:T(8,128)(2,1)}, bf16[320,256]{1,0:T(8,128)(2,1)}, u32[]{:S(2)}, u32[]{:S(2)}) collective-permute-start(bf16[320,256]{1,0:T(8,128)(2,1)} %pad_maximum_fusion.7), channel_id=1, source_target_pairs={{0,3},{1,2},{2,1},{3,0},{4,7},{5,6},{6,5},{7,4},{8,11},{9,10},{10,... | collective-permute-start | bytes 491528 | tf_op jit(solution)/shard_map/ppermute | solution.py:842
  16.7 14.9 %collective-permute-start.2 = (bf16[320,256]{1,0:T(8,128)(2,1)}, bf16[320,256]{1,0:T(8,128)(2,1)}, u32[]{:S(2)}, u32[]{:S(2)}) collective-permute-start(bf16[320,256]{1,0:T(8,128)(2,1)} %pad_maximum_fusion.7), channel_id=1, source_target_pairs={{0,2},{1,3},{2,0},{3,1},{4,6},{5,7},{6,4},{7,5},{8,10},{9,11},{10,... | collective-permute-start | bytes 491528 | tf_op jit(solution)/shard_map/ppermute | solution.py:842
  16.7 14.9 %collective-permute-start.1 = (bf16[320,256]{1,0:T(8,128)(2,1)}, bf16[320,256]{1,0:T(8,128)(2,1)}, u32[]{:S(2)}, u32[]{:S(2)}) collective-permute-start(bf16[320,256]{1,0:T(8,128)(2,1)} %pad_maximum_fusion.7), channel_id=1, source_target_pairs={{0,1},{1,0},{2,3},{3,2},{4,5},{5,4},{6,7},{7,6},{8,9},{9,8},{10,11... | collective-permute-start | bytes 491528 | tf_op jit(solution)/shard_map/ppermute | solution.py:842
  18.7 40.0 %collective-permute-start = (bf16[16,1024]{1,0:T(8,128)(2,1)}, bf16[16,1024]{1,0:T(8,128)(2,1)}, u32[]{:S(2)}, u32[]{:S(2)}) collective-permute-start(bf16[16,1024]{1,0:T(8,128)(2,1)} %slice.187), channel_id=1, source_target_pairs={{0,1},{1,2},{2,3},{3,4},{4,5},{5,6},{6,7},{7,8},{8,9},{9,10},{10,1... | collective-permute-start | bytes 98312 | tf_op jit(solution)/shard_map/ppermute | solution.py:837
  21.4 2.3 copy-start.1
  23.7 9.1 %copy-start.2 = (bf16[4,512,256]{2,1,0:T(8,128)(2,1)}, bf16[4,512,256]{2,1,0:T(8,128)(2,1)S(1)}, u32[]{:S(2)}) copy-start(bf16[4,512,256]{2,1,0:T(8,128)(2,1)S(1)} %pad_maximum_fusion.rest_9_) | copy-start | bytes 3145732
  24.6 211.8 %reduce-scatter.3.cloned.1.call-start = ((), (), s32[]{:S(2)}) async-start(), calls=%async_computation.2 | async-start | bytes 9437184 | tf_op jit(solution)/shard_map/reduce_scatter | solution.py:957
  32.8 24.7 %copy-start = (bf16[3,320,256]{2,1,0:T(8,128)(2,1)}, bf16[3,320,256]{2,1,0:T(8,128)(2,1)S(1)}, u32[]{:S(2)}) copy-start(bf16[3,320,256]{2,1,0:T(8,128)(2,1)S(1)} %pad_maximum_fusion.1.rest_1_) | copy-start | bytes 1474564
  32.8 22.5 %collective-permute-start.7 = (bf16[3,320,256]{2,1,0:T(8,128)(2,1)S(1)}, bf16[3,320,256]{2,1,0:T(8,128)(2,1)S(1)}, u32[]{:S(2)}, u32[]{:S(2)}) collective-permute-start(bf16[3,320,256]{2,1,0:T(8,128)(2,1)S(1)} %pad_maximum_fusion.1.rest_1_), channel_id=1, source_target_pairs={{0,24},{1,25},{2,26},{3,27},{4,28},{5,29},{6,30},{7,31},{8,16},{9,... | collective-permute-start | bytes 1474568 | tf_op jit(solution)/shard_map/ppermute | solution.py:842
  35.3 21.2 %collective-permute-start.6 = (bf16[3,320,256]{2,1,0:T(8,128)(2,1)S(1)}, bf16[3,320,256]{2,1,0:T(8,128)(2,1)S(1)}, u32[]{:S(2)}, u32[]{:S(2)}) collective-permute-start(bf16[3,320,256]{2,1,0:T(8,128)(2,1)S(1)} %pad_maximum_fusion.1.rest_1_), channel_id=1, source_target_pairs={{0,16},{1,17},{2,18},{3,19},{4,20},{5,21},{6,22},{7,23},{8,24},{9,... | collective-permute-start | bytes 1474568 | tf_op jit(solution)/shard_map/ppermute | solution.py:842
  35.8 20.9 %collective-permute-start.5 = (bf16[3,320,256]{2,1,0:T(8,128)(2,1)S(1)}, bf16[3,320,256]{2,1,0:T(8,128)(2,1)}, u32[]{:S(2)}, u32[]{:S(2)}) collective-permute-start(bf16[3,320,256]{2,1,0:T(8,128)(2,1)S(1)} %pad_maximum_fusion.1.rest_1_), channel_id=1, source_target_pairs={{0,8},{1,9},{2,10},{3,11},{4,12},{5,13},{6,14},{7,15},{8,0},{9,1},... | collective-permute-start | bytes 1474568 | tf_op jit(solution)/shard_map/ppermute | solution.py:842
  39.4 21.0 %collective-permute-start.4 = (bf16[3,320,256]{2,1,0:T(8,128)(2,1)S(1)}, bf16[3,320,256]{2,1,0:T(8,128)(2,1)}, u32[]{:S(2)}, u32[]{:S(2)}) collective-permute-start(bf16[3,320,256]{2,1,0:T(8,128)(2,1)S(1)} %pad_maximum_fusion.1.rest_1_), channel_id=1, source_target_pairs={{0,4},{1,5},{2,6},{3,7},{4,0},{5,1},{6,2},{7,3},{8,12},{9,13},{10,... | collective-permute-start | bytes 1474568 | tf_op jit(solution)/shard_map/ppermute | solution.py:842
  55.3 34.2 %copy-start.4 = (bf16[3,512,256]{2,1,0:T(8,128)(2,1)}, bf16[3,512,256]{2,1,0:T(8,128)(2,1)S(1)}, u32[]{:S(2)}) copy-start(bf16[3,512,256]{2,1,0:T(8,128)(2,1)S(1)} %broadcast_select_fusion.rest_1_.rest_10_) | copy-start | bytes 2359300
  55.3 7.8 %copy-start.6 = (bf16[3,320,256]{2,1,0:T(8,128)(2,1)}, bf16[3,320,256]{2,1,0:T(8,128)(2,1)S(1)}, u32[]{:S(2)}) copy-start(bf16[3,320,256]{2,1,0:T(8,128)(2,1)S(1)} %collective-permute-done.7.rest_7_) | copy-start | bytes 1474564
  56.6 6.5 %copy-start.7 = (bf16[3,320,256]{2,1,0:T(8,128)(2,1)}, bf16[3,320,256]{2,1,0:T(8,128)(2,1)S(1)}, u32[]{:S(2)}) copy-start(bf16[3,320,256]{2,1,0:T(8,128)(2,1)S(1)} %collective-permute-done.6.rest_5_) | copy-start | bytes 1474564
  56.8 4.9 %collective-permute-start.8 = (bf16[3,320,256]{2,1,0:T(8,128)(2,1)}, bf16[3,320,256]{2,1,0:T(8,128)(2,1)S(1)}, u32[]{:S(2)}, u32[]{:S(2)}) collective-permute-start(bf16[3,320,256]{2,1,0:T(8,128)(2,1)} %collective-permute-done.5.rest_3_), channel_id=1, source_target_pairs={{0,4},{1,5},{2,6},{3,7},{4,0},{5,1},{6,2},{7,3},{8,12},{9,13},{10,... | collective-permute-start | bytes 1474568 | tf_op jit(solution)/shard_map/ppermute | solution.py:842
  57.5 5.5 %collective-permute-start.9 = (bf16[3,320,256]{2,1,0:T(8,128)(2,1)S(1)}, bf16[3,320,256]{2,1,0:T(8,128)(2,1)}, u32[]{:S(2)}, u32[]{:S(2)}) collective-permute-start(bf16[3,320,256]{2,1,0:T(8,128)(2,1)S(1)} %collective-permute-done.6.rest_5_), channel_id=1, source_target_pairs={{0,4},{1,5},{2,6},{3,7},{4,0},{5,1},{6,2},{7,3},{8,12},{9,13},{10,... | collective-permute-start | bytes 1474568 | tf_op jit(solution)/shard_map/ppermute | solution.py:842
  58.0 5.0 %collective-permute-start.10 = (bf16[3,320,256]{2,1,0:T(8,128)(2,1)S(1)}, bf16[3,320,256]{2,1,0:T(8,128)(2,1)}, u32[]{:S(2)}, u32[]{:S(2)}) collective-permute-start(bf16[3,320,256]{2,1,0:T(8,128)(2,1)S(1)} %collective-permute-done.7.rest_7_), channel_id=1, source_target_pairs={{0,4},{1,5},{2,6},{3,7},{4,0},{5,1},{6,2},{7,3},{8,12},{9,13},{10,... | collective-permute-start | bytes 1474568 | tf_op jit(solution)/shard_map/ppermute | solution.py:842
  58.7 45.1 %collective-permute-start.15 = (bf16[3,512,256]{2,1,0:T(8,128)(2,1)S(1)}, bf16[3,512,256]{2,1,0:T(8,128)(2,1)}, u32[]{:S(2)}, u32[]{:S(2)}) collective-permute-start(bf16[3,512,256]{2,1,0:T(8,128)(2,1)S(1)} %broadcast_select_fusion.rest_1_.rest_10_), channel_id=1, source_target_pairs={{0,24},{1,25},{2,26},{3,27},{4,28},{5,29},{6,30},{7,31},{8,16},{9,... | collective-permute-start | bytes 2359304 | tf_op jit(solution)/shard_map/ppermute | solution.py:842
  60.3 43.4 %collective-permute-start.14 = (bf16[3,512,256]{2,1,0:T(8,128)(2,1)S(1)}, bf16[3,512,256]{2,1,0:T(8,128)(2,1)}, u32[]{:S(2)}, u32[]{:S(2)}) collective-permute-start(bf16[3,512,256]{2,1,0:T(8,128)(2,1)S(1)} %broadcast_select_fusion.rest_1_.rest_10_), channel_id=1, source_target_pairs={{0,16},{1,17},{2,18},{3,19},{4,20},{5,21},{6,22},{7,23},{8,24},{9,... | collective-permute-start | bytes 2359304 | tf_op jit(solution)/shard_map/ppermute | solution.py:842
  61.6 1.4 copy-start.8
  61.6 42.1 %collective-permute-start.13 = (bf16[3,512,256]{2,1,0:T(8,128)(2,1)S(1)}, bf16[3,512,256]{2,1,0:T(8,128)(2,1)}, u32[]{:S(2)}, u32[]{:S(2)}) collective-permute-start(bf16[3,512,256]{2,1,0:T(8,128)(2,1)S(1)} %broadcast_select_fusion.rest_1_.rest_10_), channel_id=1, source_target_pairs={{0,8},{1,9},{2,10},{3,11},{4,12},{5,13},{6,14},{7,15},{8,0},{9,1},... | collective-permute-start | bytes 2359304 | tf_op jit(solution)/shard_map/ppermute | solution.py:842
  89.0 17.3 %collective-permute-start.11 = (bf16[128,2048]{1,0:T(8,128)(2,1)}, bf16[128,2048]{1,0:T(8,128)(2,1)S(1)}, u32[]{:S(2)}, u32[]{:S(2)}) collective-permute-start(bf16[128,2048]{1,0:T(8,128)(2,1)} %get-tuple-element.69), channel_id=1, source_target_pairs={{0,1},{1,2},{2,3},{3,4},{4,5},{5,6},{6,7},{7,8},{8,9},{9,10},{10,1... | collective-permute-start | bytes 1572872 | tf_op jit(solution)/shard_map/ppermute | solution.py:837
  89.5 19.1 %collective-permute-start.12 = (bf16[3,512,256]{2,1,0:T(8,128)(2,1)S(1)}, bf16[3,512,256]{2,1,0:T(8,128)(2,1)S(1)}, u32[]{:S(2)}, u32[]{:S(2)}) collective-permute-start(bf16[3,512,256]{2,1,0:T(8,128)(2,1)S(1)} %broadcast_select_fusion.rest_1_.rest_10_), channel_id=1, source_target_pairs={{0,4},{1,5},{2,6},{3,7},{4,0},{5,1},{6,2},{7,3},{8,12},{9,13},{10,... | collective-permute-start | bytes 2359304 | tf_op jit(solution)/shard_map/ppermute | solution.py:842
  106.3 0.8 copy-start.20
  106.3 3.6 %collective-permute-start.16 = (bf16[3,512,256]{2,1,0:T(8,128)(2,1)}, bf16[3,512,256]{2,1,0:T(8,128)(2,1)S(1)}, u32[]{:S(2)}, u32[]{:S(2)}) collective-permute-start(bf16[3,512,256]{2,1,0:T(8,128)(2,1)} %collective-permute-done.13.rest_3_.rest_12_), channel_id=1, source_target_pairs={{0,4},{1,5},{2,6},{3,7},{4,0},{5,1},{6,2},{7,3},{8,12},{9,13},{10,... | collective-permute-start | bytes 2359304 | tf_op jit(solution)/shard_map/ppermute | solution.py:842
  106.3 3.7 %collective-permute-start.17 = (bf16[3,512,256]{2,1,0:T(8,128)(2,1)}, bf16[3,512,256]{2,1,0:T(8,128)(2,1)}, u32[]{:S(2)}, u32[]{:S(2)}) collective-permute-start(bf16[3,512,256]{2,1,0:T(8,128)(2,1)} %collective-permute-done.14.rest_5_.rest_14_), channel_id=1, source_target_pairs={{0,4},{1,5},{2,6},{3,7},{4,0},{5,1},{6,2},{7,3},{8,12},{9,13},{10,... | collective-permute-start | bytes 2359304 | tf_op jit(solution)/shard_map/ppermute | solution.py:842
  106.9 4.4 %collective-permute-start.18 = (bf16[3,512,256]{2,1,0:T(8,128)(2,1)}, bf16[3,512,256]{2,1,0:T(8,128)(2,1)}, u32[]{:S(2)}, u32[]{:S(2)}) collective-permute-start(bf16[3,512,256]{2,1,0:T(8,128)(2,1)} %collective-permute-done.15.rest_7_.rest_16_), channel_id=1, source_target_pairs={{0,4},{1,5},{2,6},{3,7},{4,0},{5,1},{6,2},{7,3},{8,12},{9,13},{10,... | collective-permute-start | bytes 2359304 | tf_op jit(solution)/shard_map/ppermute | solution.py:842
  108.6 2.6 copy-start.18
  109.9 1.3 copy-start.19
  149.5 18.1 %collective-permute-start.19 = (bf16[128,2048]{1,0:T(8,128)(2,1)}, bf16[128,2048]{1,0:T(8,128)(2,1)S(1)}, u32[]{:S(2)}, u32[]{:S(2)}) collective-permute-start(bf16[128,2048]{1,0:T(8,128)(2,1)} %get-tuple-element.82), channel_id=1, source_target_pairs={{0,31},{1,0},{2,1},{3,2},{4,3},{5,4},{6,5},{7,6},{8,7},{9,8},{10,9... | collective-permute-start | bytes 1572872 | tf_op jit(solution)/shard_map/ppermute | solution.py:837
  167.6 0.8 copy-start.21
  168.3 101.2 %reduce-scatter.5.cloned.1.call-start = ((), (), s32[]{:S(2)}) async-start(), calls=%async_computation.3 | async-start | bytes 1310720 | tf_op jit(solution)/shard_map/reduce_scatter | solution.py:965
  214.5 8.1 %collective-permute-start.20 = (bf16[16,2432]{1,0:T(8,128)(2,1)}, bf16[16,2432]{1,0:T(8,128)(2,1)S(1)}, u32[]{:S(2)}, u32[]{:S(2)}) collective-permute-start(bf16[16,2432]{1,0:T(8,128)(2,1)} %get-tuple-element.88), channel_id=1, source_target_pairs={{0,31},{1,0},{2,1},{3,2},{4,3},{5,4},{6,5},{7,6},{8,7},{9,8},{10,9... | collective-permute-start | bytes 233480 | tf_op jit(solution)/shard_map/ppermute | solution.py:837
  222.6 7.8 %copy-start.22 = (bf16[16,2432]{1,0:T(8,128)(2,1)}, bf16[16,2432]{1,0:T(8,128)(2,1)S(1)}, u32[]{:S(2)}) copy-start(bf16[16,2432]{1,0:T(8,128)(2,1)S(1)} %collective-permute-done.20.ahead_ref) | copy-start | bytes 233476
  222.6 7.8 %collective-permute-start.21 = (bf16[4,4,304,256]{3,2,1,0:T(8,128)(2,1)}, bf16[4,4,304,256]{3,2,1,0:T(8,128)(2,1)S(1)}, u32[]{:S(2)}, u32[]{:S(2)}) collective-permute-start(bf16[4,4,304,256]{3,2,1,0:T(8,128)(2,1)} %conv_grad.3), channel_id=1, source_target_pairs={{0,4},{1,5},{2,6},{3,7},{4,0},{5,1},{6,2},{7,3},{8,12},{9,13},{10,... | collective-permute-start | bytes 7471112 | tf_op jit(solution)/shard_map/ppermute | solution.py:842
  230.4 8.5 %copy-start.17 = (f32[8,2304]{1,0:T(8,128)S(1)}, f32[8,2304]{1,0:T(8,128)}, u32[]{:S(2)}) copy-start(f32[8,2304]{1,0:T(8,128)} %get-tuple-element.96) | copy-start | bytes 221188
  236.5 67.3 %all-gather.7.cloned.1.call-start = ((), (), s32[]{:S(2)}) async-start(), calls=%async_computation.5 | async-start | bytes 2359296 | tf_op jit(solution)/shard_map/all_gather | solution.py:975
  239.3 26.3 %collective-permute-start.24 = (bf16[4,304,256]{2,1,0:T(8,128)(2,1)S(1)}, bf16[4,304,256]{2,1,0:T(8,128)(2,1)S(1)}, u32[]{:S(2)}, u32[]{:S(2)}) collective-permute-start(bf16[4,304,256]{2,1,0:T(8,128)(2,1)S(1)} %get-tuple-element.129), channel_id=1, source_target_pairs={{0,24},{1,25},{2,26},{3,27},{4,28},{5,29},{6,30},{7,31},{8,16},{9,... | collective-permute-start | bytes 1867784 | tf_op jit(solution)/shard_map/ppermute | solution.py:842
  240.8 28.7 %collective-permute-start.23 = (bf16[4,304,256]{2,1,0:T(8,128)(2,1)S(1)}, bf16[4,304,256]{2,1,0:T(8,128)(2,1)}, u32[]{:S(2)}, u32[]{:S(2)}) collective-permute-start(bf16[4,304,256]{2,1,0:T(8,128)(2,1)S(1)} %get-tuple-element.130), channel_id=1, source_target_pairs={{0,16},{1,17},{2,18},{3,19},{4,20},{5,21},{6,22},{7,23},{8,24},{9,... | collective-permute-start | bytes 1867784 | tf_op jit(solution)/shard_map/ppermute | solution.py:842
  242.2 27.3 %collective-permute-start.22 = (bf16[4,304,256]{2,1,0:T(8,128)(2,1)S(1)}, bf16[4,304,256]{2,1,0:T(8,128)(2,1)}, u32[]{:S(2)}, u32[]{:S(2)}) collective-permute-start(bf16[4,304,256]{2,1,0:T(8,128)(2,1)S(1)} %get-tuple-element.131), channel_id=1, source_target_pairs={{0,8},{1,9},{2,10},{3,11},{4,12},{5,13},{6,14},{7,15},{8,0},{9,1},... | collective-permute-start | bytes 1867784 | tf_op jit(solution)/shard_map/ppermute | solution.py:842
  271.5 15.6 %collective-permute-start.26 = (bf16[336,256]{1,0:T(8,128)(2,1)S(1)}, bf16[336,256]{1,0:T(8,128)(2,1)S(1)}, u32[]{:S(2)}, u32[]{:S(2)}) collective-permute-start(bf16[336,256]{1,0:T(8,128)(2,1)S(1)} %pad_maximum_fusion.4), channel_id=1, source_target_pairs={{0,2},{1,3},{2,0},{3,1},{4,6},{5,7},{6,4},{7,5},{8,10},{9,11},{10,... | collective-permute-start | bytes 516104 | tf_op jit(solution)/shard_map/ppermute | solution.py:842
  274.0 13.1 %collective-permute-start.27 = (bf16[336,256]{1,0:T(8,128)(2,1)S(1)}, bf16[336,256]{1,0:T(8,128)(2,1)S(1)}, u32[]{:S(2)}, u32[]{:S(2)}) collective-permute-start(bf16[336,256]{1,0:T(8,128)(2,1)S(1)} %pad_maximum_fusion.5), channel_id=1, source_target_pairs={{0,3},{1,2},{2,1},{3,0},{4,7},{5,6},{6,5},{7,4},{8,11},{9,10},{10,... | collective-permute-start | bytes 516104 | tf_op jit(solution)/shard_map/ppermute | solution.py:842
  275.5 12.2 %collective-permute-start.25 = (bf16[336,256]{1,0:T(8,128)(2,1)S(1)}, bf16[336,256]{1,0:T(8,128)(2,1)S(1)}, u32[]{:S(2)}, u32[]{:S(2)}) collective-permute-start(bf16[336,256]{1,0:T(8,128)(2,1)S(1)} %pad_maximum_fusion.3), channel_id=1, source_target_pairs={{0,1},{1,0},{2,3},{3,2},{4,5},{5,4},{6,7},{7,6},{8,9},{9,8},{10,11... | collective-permute-start | bytes 516104 | tf_op jit(solution)/shard_map/ppermute | solution.py:842
  287.8 21.1 %copy-start.5 = (bf16[336,256]{1,0:T(8,128)(2,1)}, bf16[336,256]{1,0:T(8,128)(2,1)S(1)}, u32[]{:S(2)}) copy-start(bf16[336,256]{1,0:T(8,128)(2,1)S(1)} %pad_maximum_fusion.6.rest_0_) | copy-start | bytes 516100
  287.8 10.9 %collective-permute-start.33 = (bf16[336,256]{1,0:T(8,128)(2,1)S(1)}, bf16[336,256]{1,0:T(8,128)(2,1)S(1)}, u32[]{:S(2)}, u32[]{:S(2)}) collective-permute-start(bf16[336,256]{1,0:T(8,128)(2,1)S(1)} %pad_maximum_fusion.6.rest_0_), channel_id=1, source_target_pairs={{0,24},{1,25},{2,26},{3,27},{4,28},{5,29},{6,30},{7,31},{8,16},{9,... | collective-permute-start | bytes 516104 | tf_op jit(solution)/shard_map/ppermute | solution.py:842
  289.3 11.9 %collective-permute-start.31 = (bf16[336,256]{1,0:T(8,128)(2,1)S(1)}, bf16[336,256]{1,0:T(8,128)(2,1)S(1)}, u32[]{:S(2)}, u32[]{:S(2)}) collective-permute-start(bf16[336,256]{1,0:T(8,128)(2,1)S(1)} %pad_maximum_fusion.6.rest_0_), channel_id=1, source_target_pairs={{0,16},{1,17},{2,18},{3,19},{4,20},{5,21},{6,22},{7,23},{8,24},{9,... | collective-permute-start | bytes 516104 | tf_op jit(solution)/shard_map/ppermute | solution.py:842
  290.7 11.2 %collective-permute-start.29 = (bf16[336,256]{1,0:T(8,128)(2,1)S(1)}, bf16[336,256]{1,0:T(8,128)(2,1)S(1)}, u32[]{:S(2)}, u32[]{:S(2)}) collective-permute-start(bf16[336,256]{1,0:T(8,128)(2,1)S(1)} %pad_maximum_fusion.6.rest_0_), channel_id=1, source_target_pairs={{0,8},{1,9},{2,10},{3,11},{4,12},{5,13},{6,14},{7,15},{8,0},{9,1},... | collective-permute-start | bytes 516104 | tf_op jit(solution)/shard_map/ppermute | solution.py:842
  291.3 17.5 %collective-permute-start.28 = (bf16[336,256]{1,0:T(8,128)(2,1)S(1)}, bf16[336,256]{1,0:T(8,128)(2,1)S(1)}, u32[]{:S(2)}, u32[]{:S(2)}) collective-permute-start(bf16[336,256]{1,0:T(8,128)(2,1)S(1)} %pad_maximum_fusion.6.rest_0_), channel_id=1, source_target_pairs={{0,4},{1,5},{2,6},{3,7},{4,0},{5,1},{6,2},{7,3},{8,12},{9,13},{10,... | collective-permute-start | bytes 516104 | tf_op jit(solution)/shard_map/ppermute | solution.py:842
  298.7 10.2 %copy-start.9 = (bf16[336,256]{1,0:T(8,128)(2,1)}, bf16[336,256]{1,0:T(8,128)(2,1)S(1)}, u32[]{:S(2)}) copy-start(bf16[336,256]{1,0:T(8,128)(2,1)S(1)} %collective-permute-done.33.rest_6_) | copy-start | bytes 516100
  298.7 10.1 %collective-permute-start.34 = (bf16[336,256]{1,0:T(8,128)(2,1)S(1)}, bf16[336,256]{1,0:T(8,128)(2,1)S(1)}, u32[]{:S(2)}, u32[]{:S(2)}) collective-permute-start(bf16[336,256]{1,0:T(8,128)(2,1)S(1)} %collective-permute-done.33.rest_6_), channel_id=1, source_target_pairs={{0,4},{1,5},{2,6},{3,7},{4,0},{5,1},{6,2},{7,3},{8,12},{9,13},{10,... | collective-permute-start | bytes 516104 | tf_op jit(solution)/shard_map/ppermute | solution.py:842
  301.2 7.7 %copy-start.10 = (bf16[336,256]{1,0:T(8,128)(2,1)}, bf16[336,256]{1,0:T(8,128)(2,1)S(1)}, u32[]{:S(2)}) copy-start(bf16[336,256]{1,0:T(8,128)(2,1)S(1)} %collective-permute-done.31.rest_4_) | copy-start | bytes 516100
  301.2 7.6 %collective-permute-start.32 = (bf16[336,256]{1,0:T(8,128)(2,1)S(1)}, bf16[336,256]{1,0:T(8,128)(2,1)S(1)}, u32[]{:S(2)}, u32[]{:S(2)}) collective-permute-start(bf16[336,256]{1,0:T(8,128)(2,1)S(1)} %collective-permute-done.31.rest_4_), channel_id=1, source_target_pairs={{0,4},{1,5},{2,6},{3,7},{4,0},{5,1},{6,2},{7,3},{8,12},{9,13},{10,... | collective-permute-start | bytes 516104 | tf_op jit(solution)/shard_map/ppermute | solution.py:842
  301.9 7.0 %copy-start.11 = (bf16[336,256]{1,0:T(8,128)(2,1)}, bf16[336,256]{1,0:T(8,128)(2,1)S(1)}, u32[]{:S(2)}) copy-start(bf16[336,256]{1,0:T(8,128)(2,1)S(1)} %collective-permute-done.29.rest_2_) | copy-start | bytes 516100
  301.9 6.9 %collective-permute-start.30 = (bf16[336,256]{1,0:T(8,128)(2,1)S(1)}, bf16[336,256]{1,0:T(8,128)(2,1)S(1)}, u32[]{:S(2)}, u32[]{:S(2)}) collective-permute-start(bf16[336,256]{1,0:T(8,128)(2,1)S(1)} %collective-permute-done.29.rest_2_), channel_id=1, source_target_pairs={{0,4},{1,5},{2,6},{3,7},{4,0},{5,1},{6,2},{7,3},{8,12},{9,13},{10,... | collective-permute-start | bytes 516104 | tf_op jit(solution)/shard_map/ppermute | solution.py:842
  308.8 0.7 copy-start.12
  308.8 0.7 copy-start.13
  308.8 0.8 copy-start.14
  308.9 0.8 copy-start.15
Sparse Core Ops, SparseCore 0:
  24.8 28.4 all-gather.4
  167.7 68.6 reduce-scatter.2
  238.8 27.0 reduce-scatter.4
  269.7 34.0 all-gather.6
where the time goes:
time: 326 us; the launch traced here: 325 us
  Pallas kernels  186 us (57%)
  waiting for transfers between devices  55.6 us (17%)
  starting transfers between devices  30.6 us (9%)
  local copies, waits for them, and re-layouts  25.6 us (8%)
  between operations  14.5 us (4%)
  other arithmetic  13.1 us (4%)
    pallas_call x1, Pallas kernels, back(): call(back_kernel, nb, [rows_of(2 * NS, nb, DI // (2 * NS)), rows_of(DI, n...  46.1 us
    pallas_call x1, Pallas kernels, gating(): call(partial(gate_kernel, count), nb, [rows_of(D), rows_of(D), rows_of(D)...  38.2 us
    ppermute x31, waiting for transfers between devices, swap(): return lax.ppermute(v, BOTH, [(i, i ^ mask) for i in range(n)])  33.9 us
    pallas_call x1, Pallas kernels, front(): call(partial(front_kernel, count), nb, [rows_of(D), whole(16, D), whole(1...  25.9 us
    ppermute x31, starting transfers between devices, swap(): return lax.ppermute(v, BOTH, [(i, i ^ mask) for i in range(n)])  25.1 us
    pallas_call x1, Pallas kernels, input_grad(): call(partial(input_grad_kernel, convs, gates), nb, [rows_of(D), rows_of(D...  21.2 us
    pallas_call x2, Pallas kernels, conv_grad(): call(partial(conv_grad_kernel, nb), shards, [pl.BlockSpec((rows, m), lamb...  15.5 us
    pallas_call x1, Pallas kernels, wide_grad(): call(wide_grad_kernel, shards, [pl.BlockSpec((rows, block), lambda k, c:...  15.3 us
  transfers between devices with their start and end apart: 39, of which 16 were waited for; matrix products, arithmetic and copies ran while one was open for 9% of the time, Pallas kernels for 44%

commit v1 on v0

--- a/solution.py
+++ b/solution.py
@@ -613,35 +613,61 @@
         gt_ref[rows] = (inv * v - x * (inv * inv * inv * mean) + dy_ref[rows].astype(F32)).astype(BF)
 
 
-def finish_wide_kernel(cont, wide_ref, gin_ref, gout_ref, buf, sem):
+def finish_wide_kernel(cont, wide_ref, gin_ref, gout_ref, buf, sems):
+    i = pl.program_id(0)
     reps, rows, m = wide_ref.shape
-    part = DI // reps
+    part = buf.shape[1] // reps
     for r in range(reps):
-        buf[r * part : (r + 1) * part, :] = wide_ref[r, rows - part :, :].astype(F32)
-    copy = pltpu.make_async_copy(buf, gin_ref.at[pl.ds(0, DI)], sem)
-    copy.start()
-    part = (rows - part) * m // D
+        buf[i, r * part : (r + 1) * part, :] = wide_ref[r, rows - part :, :].astype(F32)
+
+    def copy(step):
+        to = pl.ds(pl.multiple_of(step * reps * part, 16), reps * part)
+        return pltpu.make_async_copy(buf.at[step], gin_ref.at[to], sems.at[step])
+
+    copy(i).start()
+    lines = (rows - part) * m // D
     for r in range(reps):
         for u in range(D // m):
-            block = wide_ref[r, u * part : (u + 1) * part, :]
-            gout_ref[r * part : (r + 1) * part, u * m : (u + 1) * m] = block.astype(F32)
-    copy.wait()
+            block = wide_ref[r, u * lines : (u + 1) * lines, :]
+            gout_ref[r * lines : (r + 1) * lines, u * m : (u + 1) * m] = block.astype(F32)
+
+    @pl.when(i == pl.num_programs(0) - 1)
+    def _():
+        for step in range(buf.shape[0]):
+            copy(step).wait()
 
 
 def finish_conv_kernel(nb, count, part, cont, *rest):
     pieces = rest[:count]
-    gin_ref, small_ref, buf, sem = rest[count + 1 :]
+    gin_ref, small_ref, buf, sems = rest[count + 1 :]
+    full, left = divmod(CH + H, part)
+
+    def each(i, act):
+        place = slot_of(cont[nb + 2] ^ i, count)
+        first = pl.multiple_of(DI + place * part, 16)
+
+        @pl.when(place < full)
+        def _():
+            act(pltpu.make_async_copy(buf.at[i], gin_ref.at[pl.ds(first, part)], sems.at[i]))
+
+        if left:
+
+            @pl.when(place == full)
+            def _():
+                act(pltpu.make_async_copy(buf.at[i, pl.ds(0, left)], gin_ref.at[pl.ds(first, left)], sems.at[i]))
+
     for i, piece in enumerate(pieces):
-        place = slot_of(cont[nb + 2] ^ i, count)
-        buf[pl.ds(pl.multiple_of(place * part, 16), part), :] = piece[0:part].astype(F32)
-    copy = pltpu.make_async_copy(buf.at[pl.ds(0, CH + H)], gin_ref.at[pl.ds(DI, CH + H)], sem)
-    copy.start()
-    half = small_ref.shape[0]
-    small = jnp.zeros(small_ref.shape, F32)
+        buf[i] = piece[0:part].astype(F32)
+        each(i, lambda c: c.start())
+    m = buf.shape[2]
+    half = small_ref.shape[1] // m
+    small = jnp.zeros((half, m), F32)
     for piece in pieces:
         small = small + (piece[part : part + half].astype(F32) + piece[part + half :].astype(F32))
-    small_ref[...] = small
-    copy.wait()
+    for r in range(half):
+        small_ref[:, r * m : (r + 1) * m] = small[r : r + 1]
+    for i in range(count):
+        each(i, lambda c: c.wait())
 
 
 def rows_of(width, reverse=0, column=0):
@@ -809,12 +835,13 @@
 def finish_wide(cont, wide):
     reps, rows, m = wide.shape
     shards = D // m
+    steps = 4
     return call(
-        finish_wide_kernel, 1,
-        [whole(*wide.shape)],
-        [pl.BlockSpec(memory_space=pl.ANY), fixed(DI // shards, D)],
+        finish_wide_kernel, steps,
+        [pl.BlockSpec((reps // steps, rows, m), lambda i, c: (i, 0, 0))],
+        [pl.BlockSpec(memory_space=pl.ANY), pl.BlockSpec((DI // shards // steps, D), lambda i, c: (i, 0))],
         [((DI + CH + H, m), F32), ((DI // shards, D), F32)],
-        [pltpu.VMEM((DI, m), F32), pltpu.SemaphoreType.DMA],
+        [pltpu.VMEM((steps, DI // steps, m), F32), pltpu.SemaphoreType.DMA((steps,))],
         1_000_000, 8 << 20, "finish_wide",
     )(cont, wide)
 
@@ -822,12 +849,13 @@
 def finish_conv(cont, nb, pieces, gin, part):
     rows, m = pieces[0].shape
     count = len(pieces)
+    flat = (rows - part) // 2 * m
     return call(
         partial(finish_conv_kernel, nb, count, part), 1,
         [*[whole(rows, m)] * count, pl.BlockSpec(memory_space=pl.ANY)],
-        [pl.BlockSpec(memory_space=pl.ANY), fixed((rows - part) // 2, m)],
-        [(gin.shape, F32), (((rows - part) // 2, m), F32)],
-        [pltpu.VMEM((count * part, m), F32), pltpu.SemaphoreType.DMA],
+        [pl.BlockSpec(memory_space=pl.ANY), fixed(1, flat)],
+        [(gin.shape, F32), ((1, flat), F32)],
+        [pltpu.VMEM((count, part, m), F32), pltpu.SemaphoreType.DMA((count,))],
         1_000_000, 5 << 20, "finish_conv", {1 + count: 0},
     )(cont, *pieces, gin)
 
@@ -964,16 +992,18 @@
     gp = after(gp, w, wide)
     wide = lax.psum_scatter(after(wide, w), "shard", scatter_dimension=0, tiled=True)[0]
     grad_tokens, grad_norm = input_grad(cont, tokens, cotangent, gp, dgate, ahead, ng, wc, wg, shards)
+    csum, hsum, sums, grad_norm, wide = lax.optimization_barrier((csum, hsum, sums, grad_norm, wide))
+    wide = lax.all_gather(wide, "rep", axis=0)
     packed = jnp.concatenate(
         [csum[0:CONVW].reshape(CONVW, shards, -1).transpose(1, 0, 2).reshape(shards, -1), csum[4].reshape(shards, -1),
          sums[0].reshape(shards, -1), grad_norm.sum(0).reshape(shards, -1), hsum[0, :H].reshape(shards, -1),
          hsum[1, :H].reshape(shards, -1), sums[1].reshape(H, P_SIZE).sum(1).reshape(shards, -1)], 1)
     packed = jnp.take(packed, mine ^ jnp.arange(shards), axis=0)
     others = [swap(w[j], 2 * shards * j) for j in range(1, reps // 2)]
-    others, wide, packed = lax.optimization_barrier((others, wide, packed))
+    halves = [two_halves(packed[k], m) for k in range(shards)]
+    others, halves = lax.optimization_barrier((others, halves))
     w = total_of(w[0], *others)
-    wide = lax.all_gather(wide, "rep", axis=0)
-    w = [jnp.concatenate([w[k], two_halves(packed[k], m)], 0) for k in range(shards)]
+    w = [jnp.concatenate([w[k], halves[k]], 0) for k in range(shards)]
     w = w[:1] + [swap(w[k], k) for k in range(1, shards)]
     rest = sum(one_value(v[part:]) for v in w)
     w = jnp.concatenate([total_of(*[v[:part] for v in w]), two_halves(rest.reshape(-1), m)], 0)

time: 326 us -> 325 us (level)
  waiting for transfers between devices: 55.6 us -> 52.1 us
    ppermute x31, waiting for transfers between devices: 33.9 us -> 28 us  [swap(): return lax.ppermute(v, BOTH, [(i, i ^ mask) for i in range(n)])]
    reduce_scatter x1, waiting for transfers between devices: 0.01 us -> 4.3 us  [local(): lax.psum_scatter(after(wide, w), 'shard', scatter_dimension=0, tiled=True)]
    slice x4 -> x5, local copies, waits for them, and re-layouts: 2.47 us -> 5.91 us  [local(): got.append(own[at:at + size])]
    unnamed x57 -> x56, local copies, waits for them, and re-layouts: 6.65 us -> 5.89 us
  transfers between devices with their start and end apart: 39 -> 39, of which waited for: 16 -> 14; matrix products, arithmetic and copies ran while one was open for 9% -> 9% of each run, Pallas kernels for 44% -> 44%
where the time goes in v1:
time: 325 us; the launch traced here: 324 us
  Pallas kernels  186 us (57%)
  waiting for transfers between devices  52.1 us (16%)
  starting transfers between devices  30.6 us (9%)
  local copies, waits for them, and re-layouts  27.5 us (8%)
  between operations  14.6 us (4%)
  other arithmetic  13 us (4%)
    pallas_call x1, Pallas kernels, back(): call(back_kernel, nb, [rows_of(2 * NS, nb, DI // (2 * NS)), rows_of(DI, n...  46.1 us
    pallas_call x1, Pallas kernels, gating(): call(partial(gate_kernel, count), nb, [rows_of(D), rows_of(D), rows_of(D)...  38.2 us
    ppermute x31, waiting for transfers between devices, swap(): return lax.ppermute(v, BOTH, [(i, i ^ mask) for i in range(n)])  28 us
    pallas_call x1, Pallas kernels, front(): call(partial(front_kernel, count), nb, [rows_of(D), whole(16, D), whole(1...  25.9 us
    ppermute x31, starting transfers between devices, swap(): return lax.ppermute(v, BOTH, [(i, i ^ mask) for i in range(n)])  25.1 us
    pallas_call x1, Pallas kernels, input_grad(): call(partial(input_grad_kernel, convs, gates), nb, [rows_of(D), rows_of(D...  21.4 us
    pallas_call x2, Pallas kernels, conv_grad(): call(partial(conv_grad_kernel, nb), shards, [pl.BlockSpec((rows, m), lamb...  15.5 us
    pallas_call x1, Pallas kernels, wide_grad(): call(wide_grad_kernel, shards, [pl.BlockSpec((rows, block), lambda k, c:...  15.3 us
  transfers between devices with their start and end apart: 39, of which 14 were waited for; matrix products, arithmetic and copies ran while one was open for 9% of the time, Pallas kernels for 44%

profile of v1, /device:TPU:0, one launch (start us, length us, event | category | flops | bytes accessed | tf_op | source)
XLA Modules:
  0.0 324.1 jit_solution(17618166248504396191)
XLA Ops:
  7.2 0.9 slice_reduce_fusion.12
  8.1 0.9 pad_add_fusion
  9.6 1.4 slice.285
  11.0 0.7 pad_maximum_fusion.7
  11.7 5.0 %collective-permute-start.3 = (bf16[320,256]{1,0:T(8,128)(2,1)}, bf16[320,256]{1,0:T(8,128)(2,1)}, u32[]{:S(2)}, u32[]{:S(2)}) collective-permute-start(bf16[320,256]{1,0:T(8,128)(2,1)} %pad_maximum_fusion.7), channel_id=1, source_target_pairs={{0,3},{1,2},{2,1},{3,0},{4,7},{5,6},{6,5},{7,4},{8,11},{9,10},{10,... | collective-permute-start | bytes 491528 | tf_op jit(solution)/shard_map/ppermute | solution.py:870
  17.3 1.4 slice.211
  18.7 1.5 collective-permute-start
  20.1 1.3 slice.297.rest_0_.rest_9_
  21.5 1.0 slice_bitcast_fusion.3
  22.5 1.2 pad_maximum_fusion.rest_9_
  23.7 0.8 pad_maximum_fusion.2
  24.7 0.8 select_reduce_fusion
  26.3 0.7 stack.50
  27.0 1.1 pad.61.rest_0_
  28.3 3.4 %collective-permute-done.2 = bf16[320,256]{1,0:T(8,128)(2,1)} collective-permute-done((bf16[320,256]{1,0:T(8,128)(2,1)}, bf16[320,256]{1,0:T(8,128)(2,1)}, u32[]{:S(2)}, u32[]{:S(2)}) %collective-permute-start.2) | collective-permute-done | bytes 163872 | tf_op jit(solution)/shard_map/ppermute | solution.py:870
  31.6 1.2 pad_maximum_fusion.1.rest_1_
  32.8 2.5 collective-permute-start.7
  36.4 0.7 slice_bitcast_fusion.9
  37.1 0.7 slice_bitcast_fusion.10
  37.8 0.7 slice_bitcast_fusion.11
  39.7 13.5 %all-gather.5.cloned.1.call-done = bf16[2048,256]{1,0:T(8,128)(2,1)} async-done(((bf16[512,256]{1,0:T(8,128)(2,1)}), bf16[2048,256]{1,0:T(8,128)(2,1)}) %all-gather.5.cloned.1.call-update) | async-done | bytes 1048592 | tf_op jit(solution)/shard_map/all_gather | solution.py:955
  53.3 1.8 gather_fusion.1
  55.3 1.3 collective-permute-done.6.rest_5_
  56.8 0.7 maximum_maximum_fusion.cw_ref
  58.7 1.6 collective-permute-start.15
  60.3 1.3 collective-permute-start.14
  63.0 25.9 %front.1 = (bf16[1024,1024]{1,0:T(8,128)(2,1)}, bf16[1024,2304]{1,0:T(8,128)(2,1)}, bf16[1024,2048]{1,0:T(8,128)(2,1)}, bf16[1024,2304]{1,0:T(8,128)(2,1)}, bf16...) custom-call(s32[7]{0:T(128)} %pad_add_fusion.1.cont, ...), custom_call_target="tpu_custom_call" | custom-call | flops 1000000 | bytes 1048576 | tf_op jit(solution)/shard_map/front/pallas_call | solution.py:719
  89.5 14.3 %scan.1.y_ref = f32[1024,2048]{1,0:T(8,128)} custom-call(s32[7]{0:T(128)} %pad_add_fusion.1.cont, bf16[1024,2304]{1,0:T(8,128)(2,1)} %get-tuple-element.71.kq_ref.inner_ref, bf16[1024,2048]{1,0:T(8,128)(2,1)} %get-tuple-element.72.vp_ref, f32[1024,128]{1,0:T(8,128)} %get-tuple-element.73.tot_ref, f32[4,128,256]{2,1,0:T(8,128)} %get-tuple-element.74.tott_ref), custom_call_target="tpu_custom_call" | custom-call | flops 1000000 | bytes 1048576 | tf_op jit(solution)/shard_map/scan/pallas_call | solution.py:736
  103.8 2.6 collective-permute-done.11.sin_ref
  107.9 0.7 broadcast_in_dim.71.sk_ref
  108.6 1.3 collective-permute-done.16.rest_4_.rest_13_
  110.1 1.1 collective-permute-done.18.rest_8_.rest_17_
  111.2 38.2 %gating.1 = (bf16[1024,1024]{1,0:T(8,128)(2,1)}, bf16[1024,2048]{1,0:T(8,128)(2,1)}, bf16[1024,2048]{1,0:T(8,128)(2,1)}, bf16[1024,2048]{1,0:T(8,128)(2,1)}, f32...) custom-call(s32[7]{0:T(128)} %pad_add_fusion.1.cont, ...), custom_call_target="tpu_custom_call" | custom-call | flops 35000000512 | bytes 41943040 | tf_op jit(solution)/shard_map/gating/pallas_call | solution.py:751
  149.5 2.8 collective-permute-start.19
  152.3 15.3 %wide_grad.1 = bf16[8,4,512,256]{3,2,1,0:T(8,128)(2,1)} custom-call(s32[7]{0:T(128)} %pad_add_fusion.1.cont, bf16[1024,2048]{1,0:T(8,128)(2,1)} %get-tuple-element.97.gn_ref, bf16[1024,1024]{1,0:T(8,128)(2,1)} %dy_ref.5, bf16[1024,1024]{1,0:T(8,128)(2,1)} %get-tuple-element.70.normed_ref, bf16[1024,2048]{1,0:T(8,128)(2,1)} %get-tuple-element.98.dgate_ref), custom_call_target="tpu_custom_call" | custom-call | flops 8600000512 | bytes 25165824 | tf_op jit(solution)/shard_map/wide_grad/pallas_call | solution.py:792
  167.6 0.8 copy-done.21
  168.3 46.1 %back.1 = (bf16[1024,2432]{1,0:T(8,128)(2,1)}, bf16[2432,1024]{1,0:T(8,128)(2,1)}, bf16[16,2432]{1,0:T(8,128)(2,1)}, bf16[2432,128]{1,0:T(8,128)(2,1)}, f32[8,2304]{1,0:T(8,128)}, /*index=5*/f32[8,128]{1,0:T(8,128)}) custom-call(s32[7]{0:T(128)} %pad_add_fusion.1.cont, bf16[1024,2304]{1,0:T(8,128)(2,1)} %get-tuple-element.71.kq_ref.inner_ref, ...), custom_call_target="tpu_custom_call" | custom-call | flops 60000002048 | bytes 31457280 | tf_op jit(solution)/shard_map/back/pallas_call | solution.py:771
  214.8 7.8 %conv_grad.3 = bf16[4,4,304,256]{3,2,1,0:T(8,128)(2,1)} custom-call(s32[7]{0:T(128)} %pad_add_fusion.1.cont, bf16[1024,1024]{1,0:T(8,128)(2,1)} %get-tuple-element.70.normed_ref, bf16[2432,1024]{1,0:T(8,128)(2,1)} %get-tuple-element.92.turned_ref, bf16[128,1024]{1,0:T(8,128)(2,1)} %get-tuple-element.93.nh_ref, ...), custom_call_target="tpu_custom_call" | custom-call | flops 5000000000 | bytes 8388608 | tf_op jit(solution)/shard_map/conv_grad/pallas_call | solution.py:807
  222.7 7.7 %conv_grad.2 = bf16[4,4,304,256]{3,2,1,0:T(8,128)(2,1)} custom-call(s32[7]{0:T(128)} %pad_add_fusion.1.cont, bf16[1024,1024]{1,0:T(8,128)(2,1)} %get-tuple-element.70.normed_ref, bf16[2432,1024]{1,0:T(8,128)(2,1)} %get-tuple-element.92.turned_ref, bf16[128,1024]{1,0:T(8,128)(2,1)} %get-tuple-element.93.nh_ref, ...), custom_call_target="tpu_custom_call" | custom-call | flops 5000000000 | bytes 8388608 | tf_op jit(solution)/shard_map/conv_grad/pallas_call | solution.py:807
  230.4 2.3 fusion.3
  232.7 3.7 %reduce-scatter.3.cloned.1.call-done = bf16[1,4,512,256]{3,2,1,0:T(8,128)(2,1)} async-done(((bf16[8,4,512,256]{3,2,1,0:T(8,128)(2,1)}), bf16[1,4,512,256]{3,2,1,0:T(8,128)(2,1)}) %reduce-scatter.3.cloned.1.call-update) | async-done | bytes 1048592 | tf_op jit(solution)/shard_map/reduce_scatter | solution.py:985
  236.7 1.5 collective-permute-start.24
  238.2 1.4 collective-permute-start.23
  240.3 21.4 %input_grad.1 = (bf16[1024,1024]{1,0:T(8,128)(2,1)}, f32[8,1024]{1,0:T(8,128)}) custom-call(s32[7]{0:T(128)} %pad_add_fusion.1.cont, bf16[1024,1024]{1,0:T(8,128)(2,1)} %x_ref.5, bf16[1024,1024]{1,0:T(8,128)(2,1)} %dy_ref.5, bf16[1024,2432]{1,0:T(8,128)(2,1)} %get-tuple-element.100.gp_ref, bf16[1024,2048]{1,0:T(8,128)(2,1)} %get-tuple-element.98.dgate_ref, ...), custom_call_target="tpu_custom_call" | custom-call | flops 10000000000 | bytes 25165824 | tf_op jit(solution)/shard_map/input_grad/pallas_call | solution.py:823
  261.6 4.3 %reduce-scatter.5.cloned.1.call-done = bf16[1,512,256]{2,1,0:T(8,128)(2,1)} async-done(((bf16[4,512,256]{2,1,0:T(8,128)(2,1)}), bf16[1,512,256]{2,1,0:T(8,128)(2,1)}) %reduce-scatter.5.cloned.1.call-update) | async-done | bytes 262160 | tf_op jit(solution)/shard_map/reduce_scatter | solution.py:993
  266.0 1.0 slice_reduce_fusion.6
  267.0 0.8 slice_reduce_fusion.13
  267.9 0.8 reduce_sum.28
  270.5 1.6 add_convert_fusion
  272.1 1.1 collective-permute-start.26
  273.2 0.8 collective-permute-start.27
  274.1 1.8 collective-permute-start.25
  275.8 9.8 %collective-permute-done.26 = bf16[336,256]{1,0:T(8,128)(2,1)S(1)} collective-permute-done((bf16[336,256]{1,0:T(8,128)(2,1)S(1)}, bf16[336,256]{1,0:T(8,128)(2,1)S(1)}, u32[]{:S(2)}, u32[]{:S(2)}) %collective-permute-start.26) | collective-permute-done | bytes 172064 | tf_op jit(solution)/shard_map/ppermute | solution.py:870
  285.6 1.4 collective-permute-done.25
  287.2 2.4 collective-permute-start.33
  290.7 7.4 %collective-permute-done.33.rest_6_ = bf16[336,256]{1,0:T(8,128)(2,1)S(1)} collective-permute-done((bf16[336,256]{1,0:T(8,128)(2,1)S(1)}, bf16[336,256]{1,0:T(8,128)(2,1)S(1)}, u32[]{:S(2)}, u32[]{:S(2)}) %collective-permute-start.33) | collective-permute-done | bytes 172064 | tf_op jit(solution)/shard_map/ppermute | solution.py:870
  298.1 1.9 collective-permute-done.31.rest_4_
  300.5 5.4 %finish_wide.1 = (f32[4384,256]{1,0:T(8,128)}, f32[512,1024]{1,0:T(8,128)}) custom-call(s32[7]{0:T(128)} %pad_add_fusion.1.cont, bf16[8,512,256]{2,1,0:T(8,128)(2,1)} %bitcast.79), custom_call_target="tpu_custom_call" | custom-call | flops 1000000 | bytes 8388608 | tf_op jit(solution)/shard_map/finish_wide/pallas_call | solution.py:839
  306.9 4.2 %finish_conv.1 = (f32[4384,256]{1,0:T(8,128)}, f32[1,4096]{1,0:T(1,128)}) custom-call(s32[7]{0:T(128)} %pad_add_fusion.1.cont, bf16[336,256]{1,0:T(8,128)(2,1)} %copy-done.5, bf16[336,256]{1,0:T(8,128)(2,1)} %copy-done.12, bf16[336,256]{1,0:T(8,128)(2,1)} %copy-done.11, bf16[336,256]{1,0:T(8,128)(2,1)} %copy-done.15, ...), custom_call_target="tpu_custom_call", output_to_operand_aliasing={{0}: (9, {})} | custom-call | flops 1000000 | bytes 5242880 | tf_op jit(solution)/shard_map/finish_conv/pallas_call | solution.py:853
  311.0 1.3 slice.265
  312.3 1.3 slice_bitcast_fusion.13
  313.6 1.3 slice.276
  314.9 1.3 slice_reduce_fusion.8
  316.2 0.7 slice_reduce_fusion.4
  (184 shorter events, 16.3 us)
Async XLA Ops:
  7.2 46.1 %all-gather.5.cloned.1.call-start = ((), (), s32[]{:S(2)}) async-start(), calls=%async_computation.4 | async-start | bytes 1310720 | tf_op jit(solution)/shard_map/all_gather | solution.py:955
  9.0 0.6 copy-start.16
  10.9 10.5 %copy-start.3 = (bf16[512,1024]{1,0:T(8,128)(2,1)S(1)}, bf16[512,1024]{1,0:T(8,128)(2,1)}, u32[]{:S(2)}) copy-start(bf16[512,1024]{1,0:T(8,128)(2,1)} %param.24) | copy-start | bytes 3145732
  11.7 16.6 %collective-permute-start.3 = (bf16[320,256]{1,0:T(8,128)(2,1)}, bf16[320,256]{1,0:T(8,128)(2,1)}, u32[]{:S(2)}, u32[]{:S(2)}) collective-permute-start(bf16[320,256]{1,0:T(8,128)(2,1)} %pad_maximum_fusion.7), channel_id=1, source_target_pairs={{0,3},{1,2},{2,1},{3,0},{4,7},{5,6},{6,5},{7,4},{8,11},{9,10},{10,... | collective-permute-start | bytes 491528 | tf_op jit(solution)/shard_map/ppermute | solution.py:870
  16.7 14.9 %collective-permute-start.2 = (bf16[320,256]{1,0:T(8,128)(2,1)}, bf16[320,256]{1,0:T(8,128)(2,1)}, u32[]{:S(2)}, u32[]{:S(2)}) collective-permute-start(bf16[320,256]{1,0:T(8,128)(2,1)} %pad_maximum_fusion.7), channel_id=1, source_target_pairs={{0,2},{1,3},{2,0},{3,1},{4,6},{5,7},{6,4},{7,5},{8,10},{9,11},{10,... | collective-permute-start | bytes 491528 | tf_op jit(solution)/shard_map/ppermute | solution.py:870
  16.7 14.9 %collective-permute-start.1 = (bf16[320,256]{1,0:T(8,128)(2,1)}, bf16[320,256]{1,0:T(8,128)(2,1)}, u32[]{:S(2)}, u32[]{:S(2)}) collective-permute-start(bf16[320,256]{1,0:T(8,128)(2,1)} %pad_maximum_fusion.7), channel_id=1, source_target_pairs={{0,1},{1,0},{2,3},{3,2},{4,5},{5,4},{6,7},{7,6},{8,9},{9,8},{10,11... | collective-permute-start | bytes 491528 | tf_op jit(solution)/shard_map/ppermute | solution.py:870
  18.7 40.0 %collective-permute-start = (bf16[16,1024]{1,0:T(8,128)(2,1)}, bf16[16,1024]{1,0:T(8,128)(2,1)}, u32[]{:S(2)}, u32[]{:S(2)}) collective-permute-start(bf16[16,1024]{1,0:T(8,128)(2,1)} %slice.211), channel_id=1, source_target_pairs={{0,1},{1,2},{2,3},{3,4},{4,5},{5,6},{6,7},{7,8},{8,9},{9,10},{10,1... | collective-permute-start | bytes 98312 | tf_op jit(solution)/shard_map/ppermute | solution.py:865
  21.4 2.3 copy-start.1
  23.7 9.1 %copy-start.2 = (bf16[4,512,256]{2,1,0:T(8,128)(2,1)}, bf16[4,512,256]{2,1,0:T(8,128)(2,1)S(1)}, u32[]{:S(2)}) copy-start(bf16[4,512,256]{2,1,0:T(8,128)(2,1)S(1)} %pad_maximum_fusion.rest_9_) | copy-start | bytes 3145732
  24.6 211.7 %reduce-scatter.3.cloned.1.call-start = ((), (), s32[]{:S(2)}) async-start(), calls=%async_computation.2 | async-start | bytes 9437184 | tf_op jit(solution)/shard_map/reduce_scatter | solution.py:985
  32.8 24.7 %copy-start = (bf16[3,320,256]{2,1,0:T(8,128)(2,1)}, bf16[3,320,256]{2,1,0:T(8,128)(2,1)S(1)}, u32[]{:S(2)}) copy-start(bf16[3,320,256]{2,1,0:T(8,128)(2,1)S(1)} %pad_maximum_fusion.1.rest_1_) | copy-start | bytes 1474564
  32.8 22.4 %collective-permute-start.7 = (bf16[3,320,256]{2,1,0:T(8,128)(2,1)S(1)}, bf16[3,320,256]{2,1,0:T(8,128)(2,1)S(1)}, u32[]{:S(2)}, u32[]{:S(2)}) collective-permute-start(bf16[3,320,256]{2,1,0:T(8,128)(2,1)S(1)} %pad_maximum_fusion.1.rest_1_), channel_id=1, source_target_pairs={{0,24},{1,25},{2,26},{3,27},{4,28},{5,29},{6,30},{7,31},{8,16},{9,... | collective-permute-start | bytes 1474568 | tf_op jit(solution)/shard_map/ppermute | solution.py:870
  35.3 21.2 %collective-permute-start.6 = (bf16[3,320,256]{2,1,0:T(8,128)(2,1)S(1)}, bf16[3,320,256]{2,1,0:T(8,128)(2,1)S(1)}, u32[]{:S(2)}, u32[]{:S(2)}) collective-permute-start(bf16[3,320,256]{2,1,0:T(8,128)(2,1)S(1)} %pad_maximum_fusion.1.rest_1_), channel_id=1, source_target_pairs={{0,16},{1,17},{2,18},{3,19},{4,20},{5,21},{6,22},{7,23},{8,24},{9,... | collective-permute-start | bytes 1474568 | tf_op jit(solution)/shard_map/ppermute | solution.py:870
  35.8 20.9 %collective-permute-start.5 = (bf16[3,320,256]{2,1,0:T(8,128)(2,1)S(1)}, bf16[3,320,256]{2,1,0:T(8,128)(2,1)}, u32[]{:S(2)}, u32[]{:S(2)}) collective-permute-start(bf16[3,320,256]{2,1,0:T(8,128)(2,1)S(1)} %pad_maximum_fusion.1.rest_1_), channel_id=1, source_target_pairs={{0,8},{1,9},{2,10},{3,11},{4,12},{5,13},{6,14},{7,15},{8,0},{9,1},... | collective-permute-start | bytes 1474568 | tf_op jit(solution)/shard_map/ppermute | solution.py:870
  39.4 21.0 %collective-permute-start.4 = (bf16[3,320,256]{2,1,0:T(8,128)(2,1)S(1)}, bf16[3,320,256]{2,1,0:T(8,128)(2,1)}, u32[]{:S(2)}, u32[]{:S(2)}) collective-permute-start(bf16[3,320,256]{2,1,0:T(8,128)(2,1)S(1)} %pad_maximum_fusion.1.rest_1_), channel_id=1, source_target_pairs={{0,4},{1,5},{2,6},{3,7},{4,0},{5,1},{6,2},{7,3},{8,12},{9,13},{10,... | collective-permute-start | bytes 1474568 | tf_op jit(solution)/shard_map/ppermute | solution.py:870
  55.3 34.2 %copy-start.4 = (bf16[3,512,256]{2,1,0:T(8,128)(2,1)}, bf16[3,512,256]{2,1,0:T(8,128)(2,1)S(1)}, u32[]{:S(2)}) copy-start(bf16[3,512,256]{2,1,0:T(8,128)(2,1)S(1)} %broadcast_select_fusion.rest_1_.rest_10_) | copy-start | bytes 2359300
  55.3 7.8 %copy-start.6 = (bf16[3,320,256]{2,1,0:T(8,128)(2,1)}, bf16[3,320,256]{2,1,0:T(8,128)(2,1)S(1)}, u32[]{:S(2)}) copy-start(bf16[3,320,256]{2,1,0:T(8,128)(2,1)S(1)} %collective-permute-done.7.rest_7_) | copy-start | bytes 1474564
  56.6 6.5 %copy-start.7 = (bf16[3,320,256]{2,1,0:T(8,128)(2,1)}, bf16[3,320,256]{2,1,0:T(8,128)(2,1)S(1)}, u32[]{:S(2)}) copy-start(bf16[3,320,256]{2,1,0:T(8,128)(2,1)S(1)} %collective-permute-done.6.rest_5_) | copy-start | bytes 1474564
  56.8 4.8 %collective-permute-start.8 = (bf16[3,320,256]{2,1,0:T(8,128)(2,1)}, bf16[3,320,256]{2,1,0:T(8,128)(2,1)S(1)}, u32[]{:S(2)}, u32[]{:S(2)}) collective-permute-start(bf16[3,320,256]{2,1,0:T(8,128)(2,1)} %collective-permute-done.5.rest_3_), channel_id=1, source_target_pairs={{0,4},{1,5},{2,6},{3,7},{4,0},{5,1},{6,2},{7,3},{8,12},{9,13},{10,... | collective-permute-start | bytes 1474568 | tf_op jit(solution)/shard_map/ppermute | solution.py:870
  57.5 5.5 %collective-permute-start.9 = (bf16[3,320,256]{2,1,0:T(8,128)(2,1)S(1)}, bf16[3,320,256]{2,1,0:T(8,128)(2,1)}, u32[]{:S(2)}, u32[]{:S(2)}) collective-permute-start(bf16[3,320,256]{2,1,0:T(8,128)(2,1)S(1)} %collective-permute-done.6.rest_5_), channel_id=1, source_target_pairs={{0,4},{1,5},{2,6},{3,7},{4,0},{5,1},{6,2},{7,3},{8,12},{9,13},{10,... | collective-permute-start | bytes 1474568 | tf_op jit(solution)/shard_map/ppermute | solution.py:870
  58.0 5.0 %collective-permute-start.10 = (bf16[3,320,256]{2,1,0:T(8,128)(2,1)S(1)}, bf16[3,320,256]{2,1,0:T(8,128)(2,1)}, u32[]{:S(2)}, u32[]{:S(2)}) collective-permute-start(bf16[3,320,256]{2,1,0:T(8,128)(2,1)S(1)} %collective-permute-done.7.rest_7_), channel_id=1, source_target_pairs={{0,4},{1,5},{2,6},{3,7},{4,0},{5,1},{6,2},{7,3},{8,12},{9,13},{10,... | collective-permute-start | bytes 1474568 | tf_op jit(solution)/shard_map/ppermute | solution.py:870
  58.7 45.1 %collective-permute-start.15 = (bf16[3,512,256]{2,1,0:T(8,128)(2,1)S(1)}, bf16[3,512,256]{2,1,0:T(8,128)(2,1)}, u32[]{:S(2)}, u32[]{:S(2)}) collective-permute-start(bf16[3,512,256]{2,1,0:T(8,128)(2,1)S(1)} %broadcast_select_fusion.rest_1_.rest_10_), channel_id=1, source_target_pairs={{0,24},{1,25},{2,26},{3,27},{4,28},{5,29},{6,30},{7,31},{8,16},{9,... | collective-permute-start | bytes 2359304 | tf_op jit(solution)/shard_map/ppermute | solution.py:870
  60.3 43.4 %collective-permute-start.14 = (bf16[3,512,256]{2,1,0:T(8,128)(2,1)S(1)}, bf16[3,512,256]{2,1,0:T(8,128)(2,1)}, u32[]{:S(2)}, u32[]{:S(2)}) collective-permute-start(bf16[3,512,256]{2,1,0:T(8,128)(2,1)S(1)} %broadcast_select_fusion.rest_1_.rest_10_), channel_id=1, source_target_pairs={{0,16},{1,17},{2,18},{3,19},{4,20},{5,21},{6,22},{7,23},{8,24},{9,... | collective-permute-start | bytes 2359304 | tf_op jit(solution)/shard_map/ppermute | solution.py:870
  61.6 1.4 copy-start.8
  61.6 42.1 %collective-permute-start.13 = (bf16[3,512,256]{2,1,0:T(8,128)(2,1)S(1)}, bf16[3,512,256]{2,1,0:T(8,128)(2,1)}, u32[]{:S(2)}, u32[]{:S(2)}) collective-permute-start(bf16[3,512,256]{2,1,0:T(8,128)(2,1)S(1)} %broadcast_select_fusion.rest_1_.rest_10_), channel_id=1, source_target_pairs={{0,8},{1,9},{2,10},{3,11},{4,12},{5,13},{6,14},{7,15},{8,0},{9,1},... | collective-permute-start | bytes 2359304 | tf_op jit(solution)/shard_map/ppermute | solution.py:870
  89.0 17.3 %collective-permute-start.11 = (bf16[128,2048]{1,0:T(8,128)(2,1)}, bf16[128,2048]{1,0:T(8,128)(2,1)S(1)}, u32[]{:S(2)}, u32[]{:S(2)}) collective-permute-start(bf16[128,2048]{1,0:T(8,128)(2,1)} %get-tuple-element.76), channel_id=1, source_target_pairs={{0,1},{1,2},{2,3},{3,4},{4,5},{5,6},{6,7},{7,8},{8,9},{9,10},{10,1... | collective-permute-start | bytes 1572872 | tf_op jit(solution)/shard_map/ppermute | solution.py:865
  89.5 19.1 %collective-permute-start.12 = (bf16[3,512,256]{2,1,0:T(8,128)(2,1)S(1)}, bf16[3,512,256]{2,1,0:T(8,128)(2,1)S(1)}, u32[]{:S(2)}, u32[]{:S(2)}) collective-permute-start(bf16[3,512,256]{2,1,0:T(8,128)(2,1)S(1)} %broadcast_select_fusion.rest_1_.rest_10_), channel_id=1, source_target_pairs={{0,4},{1,5},{2,6},{3,7},{4,0},{5,1},{6,2},{7,3},{8,12},{9,13},{10,... | collective-permute-start | bytes 2359304 | tf_op jit(solution)/shard_map/ppermute | solution.py:870
  106.3 0.8 copy-start.20
  106.3 3.6 %collective-permute-start.16 = (bf16[3,512,256]{2,1,0:T(8,128)(2,1)}, bf16[3,512,256]{2,1,0:T(8,128)(2,1)S(1)}, u32[]{:S(2)}, u32[]{:S(2)}) collective-permute-start(bf16[3,512,256]{2,1,0:T(8,128)(2,1)} %collective-permute-done.13.rest_3_.rest_12_), channel_id=1, source_target_pairs={{0,4},{1,5},{2,6},{3,7},{4,0},{5,1},{6,2},{7,3},{8,12},{9,13},{10,... | collective-permute-start | bytes 2359304 | tf_op jit(solution)/shard_map/ppermute | solution.py:870
  106.3 3.7 %collective-permute-start.17 = (bf16[3,512,256]{2,1,0:T(8,128)(2,1)}, bf16[3,512,256]{2,1,0:T(8,128)(2,1)}, u32[]{:S(2)}, u32[]{:S(2)}) collective-permute-start(bf16[3,512,256]{2,1,0:T(8,128)(2,1)} %collective-permute-done.14.rest_5_.rest_14_), channel_id=1, source_target_pairs={{0,4},{1,5},{2,6},{3,7},{4,0},{5,1},{6,2},{7,3},{8,12},{9,13},{10,... | collective-permute-start | bytes 2359304 | tf_op jit(solution)/shard_map/ppermute | solution.py:870
  106.8 4.4 %collective-permute-start.18 = (bf16[3,512,256]{2,1,0:T(8,128)(2,1)}, bf16[3,512,256]{2,1,0:T(8,128)(2,1)}, u32[]{:S(2)}, u32[]{:S(2)}) collective-permute-start(bf16[3,512,256]{2,1,0:T(8,128)(2,1)} %collective-permute-done.15.rest_7_.rest_16_), channel_id=1, source_target_pairs={{0,4},{1,5},{2,6},{3,7},{4,0},{5,1},{6,2},{7,3},{8,12},{9,13},{10,... | collective-permute-start | bytes 2359304 | tf_op jit(solution)/shard_map/ppermute | solution.py:870
  108.6 2.6 copy-start.18
  109.9 1.3 copy-start.19
  149.5 18.1 %collective-permute-start.19 = (bf16[128,2048]{1,0:T(8,128)(2,1)}, bf16[128,2048]{1,0:T(8,128)(2,1)S(1)}, u32[]{:S(2)}, u32[]{:S(2)}) collective-permute-start(bf16[128,2048]{1,0:T(8,128)(2,1)} %get-tuple-element.89), channel_id=1, source_target_pairs={{0,31},{1,0},{2,1},{3,2},{4,3},{5,4},{6,5},{7,6},{8,7},{9,8},{10,9... | collective-permute-start | bytes 1572872 | tf_op jit(solution)/shard_map/ppermute | solution.py:865
  167.6 0.8 copy-start.21
  168.3 97.6 %reduce-scatter.5.cloned.1.call-start = ((), (), s32[]{:S(2)}) async-start(), calls=%async_computation.3 | async-start | bytes 1310720 | tf_op jit(solution)/shard_map/reduce_scatter | solution.py:993
  214.5 8.1 %collective-permute-start.20 = (bf16[16,2432]{1,0:T(8,128)(2,1)}, bf16[16,2432]{1,0:T(8,128)(2,1)S(1)}, u32[]{:S(2)}, u32[]{:S(2)}) collective-permute-start(bf16[16,2432]{1,0:T(8,128)(2,1)} %get-tuple-element.95), channel_id=1, source_target_pairs={{0,31},{1,0},{2,1},{3,2},{4,3},{5,4},{6,5},{7,6},{8,7},{9,8},{10,9... | collective-permute-start | bytes 233480 | tf_op jit(solution)/shard_map/ppermute | solution.py:865
  222.6 7.8 %copy-start.22 = (bf16[16,2432]{1,0:T(8,128)(2,1)}, bf16[16,2432]{1,0:T(8,128)(2,1)S(1)}, u32[]{:S(2)}) copy-start(bf16[16,2432]{1,0:T(8,128)(2,1)S(1)} %collective-permute-done.20.ahead_ref) | copy-start | bytes 233476
  222.6 7.8 %collective-permute-start.21 = (bf16[4,4,304,256]{3,2,1,0:T(8,128)(2,1)}, bf16[4,4,304,256]{3,2,1,0:T(8,128)(2,1)S(1)}, u32[]{:S(2)}, u32[]{:S(2)}) collective-permute-start(bf16[4,4,304,256]{3,2,1,0:T(8,128)(2,1)} %conv_grad.3), channel_id=1, source_target_pairs={{0,4},{1,5},{2,6},{3,7},{4,0},{5,1},{6,2},{7,3},{8,12},{9,13},{10,... | collective-permute-start | bytes 7471112 | tf_op jit(solution)/shard_map/ppermute | solution.py:870
  236.4 64.1 %all-gather.7.cloned.1.call-start = ((), (), s32[]{:S(2)}) async-start(), calls=%async_computation.5 | async-start | bytes 2359296 | tf_op jit(solution)/shard_map/all_gather | solution.py:996
  236.7 33.7 %collective-permute-start.24 = (bf16[4,304,256]{2,1,0:T(8,128)(2,1)S(1)}, bf16[4,304,256]{2,1,0:T(8,128)(2,1)S(1)}, u32[]{:S(2)}, u32[]{:S(2)}) collective-permute-start(bf16[4,304,256]{2,1,0:T(8,128)(2,1)S(1)} %get-tuple-element.145), channel_id=1, source_target_pairs={{0,24},{1,25},{2,26},{3,27},{4,28},{5,29},{6,30},{7,31},{8,16},{9,... | collective-permute-start | bytes 1867784 | tf_op jit(solution)/shard_map/ppermute | solution.py:870
  238.2 32.2 %collective-permute-start.23 = (bf16[4,304,256]{2,1,0:T(8,128)(2,1)S(1)}, bf16[4,304,256]{2,1,0:T(8,128)(2,1)}, u32[]{:S(2)}, u32[]{:S(2)}) collective-permute-start(bf16[4,304,256]{2,1,0:T(8,128)(2,1)S(1)} %get-tuple-element.146), channel_id=1, source_target_pairs={{0,16},{1,17},{2,18},{3,19},{4,20},{5,21},{6,22},{7,23},{8,24},{9,... | collective-permute-start | bytes 1867784 | tf_op jit(solution)/shard_map/ppermute | solution.py:870
  239.6 30.8 %collective-permute-start.22 = (bf16[4,304,256]{2,1,0:T(8,128)(2,1)S(1)}, bf16[4,304,256]{2,1,0:T(8,128)(2,1)}, u32[]{:S(2)}, u32[]{:S(2)}) collective-permute-start(bf16[4,304,256]{2,1,0:T(8,128)(2,1)S(1)} %get-tuple-element.147), channel_id=1, source_target_pairs={{0,8},{1,9},{2,10},{3,11},{4,12},{5,13},{6,14},{7,15},{8,0},{9,1},... | collective-permute-start | bytes 1867784 | tf_op jit(solution)/shard_map/ppermute | solution.py:870
  240.3 25.7 %copy-start.17 = (f32[8,2304]{1,0:T(8,128)S(1)}, f32[8,2304]{1,0:T(8,128)}, u32[]{:S(2)}) copy-start(f32[8,2304]{1,0:T(8,128)} %get-tuple-element.107) | copy-start | bytes 221188
  272.1 13.5 %collective-permute-start.26 = (bf16[336,256]{1,0:T(8,128)(2,1)S(1)}, bf16[336,256]{1,0:T(8,128)(2,1)S(1)}, u32[]{:S(2)}, u32[]{:S(2)}) collective-permute-start(bf16[336,256]{1,0:T(8,128)(2,1)S(1)} %pad_maximum_fusion.4), channel_id=1, source_target_pairs={{0,2},{1,3},{2,0},{3,1},{4,6},{5,7},{6,4},{7,5},{8,10},{9,11},{10,... | collective-permute-start | bytes 516104 | tf_op jit(solution)/shard_map/ppermute | solution.py:870
  273.2 12.4 %collective-permute-start.27 = (bf16[336,256]{1,0:T(8,128)(2,1)S(1)}, bf16[336,256]{1,0:T(8,128)(2,1)S(1)}, u32[]{:S(2)}, u32[]{:S(2)}) collective-permute-start(bf16[336,256]{1,0:T(8,128)(2,1)S(1)} %pad_maximum_fusion.5), channel_id=1, source_target_pairs={{0,3},{1,2},{2,1},{3,0},{4,7},{5,6},{6,5},{7,4},{8,11},{9,10},{10,... | collective-permute-start | bytes 516104 | tf_op jit(solution)/shard_map/ppermute | solution.py:870
  274.1 13.0 %collective-permute-start.25 = (bf16[336,256]{1,0:T(8,128)(2,1)S(1)}, bf16[336,256]{1,0:T(8,128)(2,1)S(1)}, u32[]{:S(2)}, u32[]{:S(2)}) collective-permute-start(bf16[336,256]{1,0:T(8,128)(2,1)S(1)} %pad_maximum_fusion.3), channel_id=1, source_target_pairs={{0,1},{1,0},{2,3},{3,2},{4,5},{5,4},{6,7},{7,6},{8,9},{9,8},{10,11... | collective-permute-start | bytes 516104 | tf_op jit(solution)/shard_map/ppermute | solution.py:870
  287.2 18.9 %copy-start.5 = (bf16[336,256]{1,0:T(8,128)(2,1)}, bf16[336,256]{1,0:T(8,128)(2,1)S(1)}, u32[]{:S(2)}) copy-start(bf16[336,256]{1,0:T(8,128)(2,1)S(1)} %pad_maximum_fusion.6.rest_0_) | copy-start | bytes 516100
  287.2 11.0 %collective-permute-start.33 = (bf16[336,256]{1,0:T(8,128)(2,1)S(1)}, bf16[336,256]{1,0:T(8,128)(2,1)S(1)}, u32[]{:S(2)}, u32[]{:S(2)}) collective-permute-start(bf16[336,256]{1,0:T(8,128)(2,1)S(1)} %pad_maximum_fusion.6.rest_0_), channel_id=1, source_target_pairs={{0,24},{1,25},{2,26},{3,27},{4,28},{5,29},{6,30},{7,31},{8,16},{9,... | collective-permute-start | bytes 516104 | tf_op jit(solution)/shard_map/ppermute | solution.py:870
  289.6 10.4 %collective-permute-start.31 = (bf16[336,256]{1,0:T(8,128)(2,1)S(1)}, bf16[336,256]{1,0:T(8,128)(2,1)S(1)}, u32[]{:S(2)}, u32[]{:S(2)}) collective-permute-start(bf16[336,256]{1,0:T(8,128)(2,1)S(1)} %pad_maximum_fusion.6.rest_0_), channel_id=1, source_target_pairs={{0,16},{1,17},{2,18},{3,19},{4,20},{5,21},{6,22},{7,23},{8,24},{9,... | collective-permute-start | bytes 516104 | tf_op jit(solution)/shard_map/ppermute | solution.py:870
  290.2 9.8 %collective-permute-start.29 = (bf16[336,256]{1,0:T(8,128)(2,1)S(1)}, bf16[336,256]{1,0:T(8,128)(2,1)S(1)}, u32[]{:S(2)}, u32[]{:S(2)}) collective-permute-start(bf16[336,256]{1,0:T(8,128)(2,1)S(1)} %pad_maximum_fusion.6.rest_0_), channel_id=1, source_target_pairs={{0,8},{1,9},{2,10},{3,11},{4,12},{5,13},{6,14},{7,15},{8,0},{9,1},... | collective-permute-start | bytes 516104 | tf_op jit(solution)/shard_map/ppermute | solution.py:870
  290.7 15.3 %collective-permute-start.28 = (bf16[336,256]{1,0:T(8,128)(2,1)S(1)}, bf16[336,256]{1,0:T(8,128)(2,1)S(1)}, u32[]{:S(2)}, u32[]{:S(2)}) collective-permute-start(bf16[336,256]{1,0:T(8,128)(2,1)S(1)} %pad_maximum_fusion.6.rest_0_), channel_id=1, source_target_pairs={{0,4},{1,5},{2,6},{3,7},{4,0},{5,1},{6,2},{7,3},{8,12},{9,13},{10,... | collective-permute-start | bytes 516104 | tf_op jit(solution)/shard_map/ppermute | solution.py:870
  298.1 7.9 %copy-start.9 = (bf16[336,256]{1,0:T(8,128)(2,1)}, bf16[336,256]{1,0:T(8,128)(2,1)S(1)}, u32[]{:S(2)}) copy-start(bf16[336,256]{1,0:T(8,128)(2,1)S(1)} %collective-permute-done.33.rest_6_) | copy-start | bytes 516100
  298.1 7.9 %collective-permute-start.34 = (bf16[336,256]{1,0:T(8,128)(2,1)S(1)}, bf16[336,256]{1,0:T(8,128)(2,1)S(1)}, u32[]{:S(2)}, u32[]{:S(2)}) collective-permute-start(bf16[336,256]{1,0:T(8,128)(2,1)S(1)} %collective-permute-done.33.rest_6_), channel_id=1, source_target_pairs={{0,4},{1,5},{2,6},{3,7},{4,0},{5,1},{6,2},{7,3},{8,12},{9,13},{10,... | collective-permute-start | bytes 516104 | tf_op jit(solution)/shard_map/ppermute | solution.py:870
  300.0 6.1 %copy-start.10 = (bf16[336,256]{1,0:T(8,128)(2,1)}, bf16[336,256]{1,0:T(8,128)(2,1)S(1)}, u32[]{:S(2)}) copy-start(bf16[336,256]{1,0:T(8,128)(2,1)S(1)} %collective-permute-done.31.rest_4_) | copy-start | bytes 516100
  300.0 6.0 %collective-permute-start.32 = (bf16[336,256]{1,0:T(8,128)(2,1)S(1)}, bf16[336,256]{1,0:T(8,128)(2,1)S(1)}, u32[]{:S(2)}, u32[]{:S(2)}) collective-permute-start(bf16[336,256]{1,0:T(8,128)(2,1)S(1)} %collective-permute-done.31.rest_4_), channel_id=1, source_target_pairs={{0,4},{1,5},{2,6},{3,7},{4,0},{5,1},{6,2},{7,3},{8,12},{9,13},{10,... | collective-permute-start | bytes 516104 | tf_op jit(solution)/shard_map/ppermute | solution.py:870
  300.0 6.1 %copy-start.11 = (bf16[336,256]{1,0:T(8,128)(2,1)}, bf16[336,256]{1,0:T(8,128)(2,1)S(1)}, u32[]{:S(2)}) copy-start(bf16[336,256]{1,0:T(8,128)(2,1)S(1)} %collective-permute-done.29.rest_2_) | copy-start | bytes 516100
  300.0 6.0 %collective-permute-start.30 = (bf16[336,256]{1,0:T(8,128)(2,1)S(1)}, bf16[336,256]{1,0:T(8,128)(2,1)S(1)}, u32[]{:S(2)}, u32[]{:S(2)}) collective-permute-start(bf16[336,256]{1,0:T(8,128)(2,1)S(1)} %collective-permute-done.29.rest_2_), channel_id=1, source_target_pairs={{0,4},{1,5},{2,6},{3,7},{4,0},{5,1},{6,2},{7,3},{8,12},{9,13},{10,... | collective-permute-start | bytes 516104 | tf_op jit(solution)/shard_map/ppermute | solution.py:870
  306.0 0.7 copy-start.12
  306.0 0.7 copy-start.13
  306.0 0.7 copy-start.14
  306.1 0.8 copy-start.15
Sparse Core Ops, SparseCore 0:
  24.7 28.4 all-gather.4
  167.7 68.6 reduce-scatter.2
  238.8 27.1 reduce-scatter.4
  267.7 32.6 all-gather.6

commit v2 on v1

--- a/solution.py
+++ b/solution.py
@@ -613,28 +613,30 @@
         gt_ref[rows] = (inv * v - x * (inv * inv * inv * mean) + dy_ref[rows].astype(F32)).astype(BF)
 
 
-def finish_wide_kernel(cont, wide_ref, gin_ref, gout_ref, buf, sems):
-    i = pl.program_id(0)
-    reps, rows, m = wide_ref.shape
-    part = buf.shape[1] // reps
-    for r in range(reps):
-        buf[i, r * part : (r + 1) * part, :] = wide_ref[r, rows - part :, :].astype(F32)
-
-    def copy(step):
-        to = pl.ds(pl.multiple_of(step * reps * part, 16), reps * part)
-        return pltpu.make_async_copy(buf.at[step], gin_ref.at[to], sems.at[step])
-
-    copy(i).start()
-    lines = (rows - part) * m // D
-    for r in range(reps):
+def finish_wide_kernel(nb, count, cont, *rest):
+    pieces = rest[:count]
+    gin_ref, gout_ref, buf, lines, sems = rest[count:]
+    part, m = buf.shape[1:]
+    rows = lines.shape[1]
+
+    def copies(i):
+        place = cont[nb + 2] ^ i
+        first = pl.ds(pl.multiple_of(place * part, 16), part)
+        second = pl.ds(pl.multiple_of(place * rows, 16), rows)
+        return [
+            pltpu.make_async_copy(buf.at[i], gin_ref.at[first], sems.at[0, i]),
+            pltpu.make_async_copy(lines.at[i], gout_ref.at[second], sems.at[1, i]),
+        ]
+
+    for i, piece in enumerate(pieces):
+        buf[i] = piece[rows * D // m :].astype(F32)
         for u in range(D // m):
-            block = wide_ref[r, u * lines : (u + 1) * lines, :]
-            gout_ref[r * lines : (r + 1) * lines, u * m : (u + 1) * m] = block.astype(F32)
-
-    @pl.when(i == pl.num_programs(0) - 1)
-    def _():
-        for step in range(buf.shape[0]):
-            copy(step).wait()
+            lines[i, :, u * m : (u + 1) * m] = piece[u * rows : (u + 1) * rows].astype(F32)
+        for c in copies(i):
+            c.start()
+    for i in range(count):
+        for c in copies(i):
+            c.wait()
 
 
 def finish_conv_kernel(nb, count, part, cont, *rest):
@@ -660,12 +662,11 @@
         buf[i] = piece[0:part].astype(F32)
         each(i, lambda c: c.start())
     m = buf.shape[2]
-    half = small_ref.shape[1] // m
+    half = small_ref.shape[0]
     small = jnp.zeros((half, m), F32)
     for piece in pieces:
         small = small + (piece[part : part + half].astype(F32) + piece[part + half :].astype(F32))
-    for r in range(half):
-        small_ref[:, r * m : (r + 1) * m] = small[r : r + 1]
+    small_ref[...] = small
     for i in range(count):
         each(i, lambda c: c.wait())
 
@@ -832,29 +833,30 @@
     )(cont, x, dy, gp, dgate, ahead, ng, *wc, *wg)
 
 
-def finish_wide(cont, wide):
-    reps, rows, m = wide.shape
-    shards = D // m
-    steps = 4
+def finish_wide(cont, nb, pieces):
+    rows, m = pieces[0].shape
+    count = len(pieces)
+    part = DI // count
+    lines = DI * m // D // count
     return call(
-        finish_wide_kernel, steps,
-        [pl.BlockSpec((reps // steps, rows, m), lambda i, c: (i, 0, 0))],
-        [pl.BlockSpec(memory_space=pl.ANY), pl.BlockSpec((DI // shards // steps, D), lambda i, c: (i, 0))],
-        [((DI + CH + H, m), F32), ((DI // shards, D), F32)],
-        [pltpu.VMEM((steps, DI // steps, m), F32), pltpu.SemaphoreType.DMA((steps,))],
+        partial(finish_wide_kernel, nb, count), 1,
+        [whole(rows, m)] * count,
+        anywhere(2),
+        [((DI + CH + H, m), F32), ((lines * count, D), F32)],
+        [pltpu.VMEM((count, part, m), F32), pltpu.VMEM((count, lines, D), F32), pltpu.SemaphoreType.DMA((2, count))],
         1_000_000, 8 << 20, "finish_wide",
-    )(cont, wide)
+    )(cont, *pieces)
 
 
 def finish_conv(cont, nb, pieces, gin, part):
     rows, m = pieces[0].shape
     count = len(pieces)
-    flat = (rows - part) // 2 * m
+    half = (rows - part) // 2
     return call(
         partial(finish_conv_kernel, nb, count, part), 1,
         [*[whole(rows, m)] * count, pl.BlockSpec(memory_space=pl.ANY)],
-        [pl.BlockSpec(memory_space=pl.ANY), fixed(1, flat)],
-        [(gin.shape, F32), ((1, flat), F32)],
+        [pl.BlockSpec(memory_space=pl.ANY), fixed(half, m)],
+        [(gin.shape, F32), ((half, m), F32)],
         [pltpu.VMEM((count, part, m), F32), pltpu.SemaphoreType.DMA((count,))],
         1_000_000, 5 << 20, "finish_conv", {1 + count: 0},
     )(cont, *pieces, gin)
@@ -901,8 +903,8 @@
 def two_halves(v, m):
     rows = -(-v.size // (16 * m)) * 16
     v = jnp.pad(v, (0, rows * m - v.size)).reshape(rows, m)
-    hi = v.astype(BF)
-    return jnp.concatenate([hi, (v - hi.astype(F32)).astype(BF)], 0)
+    hi = lax.reduce_precision(v, 8, 7)
+    return jnp.concatenate([hi, v - hi], 0).astype(BF)
 
 
 def one_value(v):
@@ -992,8 +994,9 @@
     gp = after(gp, w, wide)
     wide = lax.psum_scatter(after(wide, w), "shard", scatter_dimension=0, tiled=True)[0]
     grad_tokens, grad_norm = input_grad(cont, tokens, cotangent, gp, dgate, ahead, ng, wc, wg, shards)
-    csum, hsum, sums, grad_norm, wide = lax.optimization_barrier((csum, hsum, sums, grad_norm, wide))
-    wide = lax.all_gather(wide, "rep", axis=0)
+    csum, hsum, sums, grad_norm = lax.optimization_barrier((csum, hsum, sums, grad_norm))
+    csum, wide = lax.optimization_barrier((csum, wide))
+    wide = over_cores(over_reps(wide))
     packed = jnp.concatenate(
         [csum[0:CONVW].reshape(CONVW, shards, -1).transpose(1, 0, 2).reshape(shards, -1), csum[4].reshape(shards, -1),
          sums[0].reshape(shards, -1), grad_norm.sum(0).reshape(shards, -1), hsum[0, :H].reshape(shards, -1),
@@ -1008,7 +1011,7 @@
     rest = sum(one_value(v[part:]) for v in w)
     w = jnp.concatenate([total_of(*[v[:part] for v in w]), two_halves(rest.reshape(-1), m)], 0)
     pieces = over_cores(over_reps(w))
-    gin, grad_out = finish_wide(cont, wide)
+    gin, grad_out = finish_wide(cont, nb, wide)
     grad_in, small = finish_conv(cont, nb, pieces, gin, part)
     grad_in = grad_in.T
     own = small.reshape(-1)

time: 325 us -> 324 us (level)
  starting transfers between devices: 30.6 us -> 35.6 us
  waiting for transfers between devices: 52.1 us -> 47.4 us
    ppermute x31 -> x38, starting transfers between devices: 25.1 us -> 30 us  [swap(): return lax.ppermute(v, BOTH, [(i, i ^ mask) for i in range(n)])]
    slice x5 -> x4, local copies, waits for them, and re-layouts: 5.91 us -> 2.47 us  [local(): got.append(own[at:at + size])]
    unnamed x56 -> x73, local copies, waits for them, and re-layouts: 5.89 us -> 8 us
    ppermute x31 -> x38, waiting for transfers between devices: 28 us -> 26.2 us  [swap(): return lax.ppermute(v, BOTH, [(i, i ^ mask) for i in range(n)])]
  transfers between devices with their start and end apart: 39 -> 45, of which waited for: 14 -> 15; matrix products, arithmetic and copies ran while one was open for 9% -> 8% of each run, Pallas kernels for 44% -> 44%
where the time goes in v2:
time: 324 us; the launch traced here: 323 us
  Pallas kernels  185 us (57%)
  waiting for transfers between devices  47.4 us (15%)
  starting transfers between devices  35.6 us (11%)
  local copies, waits for them, and re-layouts  26.9 us (8%)
  between operations  14.6 us (5%)
  other arithmetic  13 us (4%)
    pallas_call x1, Pallas kernels, back(): call(back_kernel, nb, [rows_of(2 * NS, nb, DI // (2 * NS)), rows_of(DI, n...  46.1 us
    pallas_call x1, Pallas kernels, gating(): call(partial(gate_kernel, count), nb, [rows_of(D), rows_of(D), rows_of(D)...  38.2 us
    ppermute x38, starting transfers between devices, swap(): return lax.ppermute(v, BOTH, [(i, i ^ mask) for i in range(n)])  30 us
    ppermute x38, waiting for transfers between devices, swap(): return lax.ppermute(v, BOTH, [(i, i ^ mask) for i in range(n)])  26.2 us
    pallas_call x1, Pallas kernels, front(): call(partial(front_kernel, count), nb, [rows_of(D), whole(16, D), whole(1...  25.9 us
    pallas_call x1, Pallas kernels, input_grad(): call(partial(input_grad_kernel, convs, gates), nb, [rows_of(D), rows_of(D...  21.4 us
    pallas_call x2, Pallas kernels, conv_grad(): call(partial(conv_grad_kernel, nb), shards, [pl.BlockSpec((rows, m), lamb...  15.5 us
    pallas_call x1, Pallas kernels, wide_grad(): call(wide_grad_kernel, shards, [pl.BlockSpec((rows, block), lambda k, c:...  15.2 us
  transfers between devices with their start and end apart: 45, of which 15 were waited for; matrix products, arithmetic and copies ran while one was open for 8% of the time, Pallas kernels for 44%

profile of v2, /device:TPU:0, one launch (start us, length us, event | category | flops | bytes accessed | tf_op | source)
XLA Modules:
  0.0 322.5 jit_solution(15851828955208960907)
XLA Ops:
  7.2 0.9 slice_reduce_fusion.10
  8.1 0.9 pad_add_fusion
  9.6 1.4 slice.261
  11.7 5.0 %collective-permute-start.3 = (bf16[320,256]{1,0:T(8,128)(2,1)}, bf16[320,256]{1,0:T(8,128)(2,1)}, u32[]{:S(2)}, u32[]{:S(2)}) collective-permute-start(bf16[320,256]{1,0:T(8,128)(2,1)} %pad_maximum_fusion.7), channel_id=1, source_target_pairs={{0,3},{1,2},{2,1},{3,0},{4,7},{5,6},{6,5},{7,4},{8,11},{9,10},{10,... | collective-permute-start | bytes 491528 | tf_op jit(solution)/shard_map/ppermute | solution.py:872
  17.3 1.4 slice.193
  18.7 1.5 collective-permute-start
  20.1 1.3 slice.273.rest_0_.rest_9_
  21.5 1.0 slice_bitcast_fusion.3
  22.4 1.2 pad_maximum_fusion.rest_9_
  23.7 0.8 pad_maximum_fusion.2
  24.7 0.8 select_reduce_fusion
  26.3 0.7 stack.50
  27.0 1.1 pad.61.rest_0_
  28.2 3.4 %collective-permute-done.2 = bf16[320,256]{1,0:T(8,128)(2,1)} collective-permute-done((bf16[320,256]{1,0:T(8,128)(2,1)}, bf16[320,256]{1,0:T(8,128)(2,1)}, u32[]{:S(2)}, u32[]{:S(2)}) %collective-permute-start.2) | collective-permute-done | bytes 163872 | tf_op jit(solution)/shard_map/ppermute | solution.py:872
  31.6 1.2 pad_maximum_fusion.1.rest_1_
  32.8 2.5 collective-permute-start.7
  36.4 0.7 slice_bitcast_fusion.9
  37.1 0.7 slice_bitcast_fusion.10
  37.8 0.7 slice_bitcast_fusion.11
  39.8 13.5 %all-gather.3.cloned.1.call-done = bf16[2048,256]{1,0:T(8,128)(2,1)} async-done(((bf16[512,256]{1,0:T(8,128)(2,1)}), bf16[2048,256]{1,0:T(8,128)(2,1)}) %all-gather.3.cloned.1.call-update) | async-done | bytes 1048592 | tf_op jit(solution)/shard_map/all_gather | solution.py:957
  53.2 1.8 gather_fusion.1
  55.2 1.3 collective-permute-done.6.rest_5_
  56.8 0.7 maximum_maximum_fusion.cw_ref
  58.7 1.7 collective-permute-start.15
  60.3 1.3 collective-permute-start.14
  63.1 25.9 %front.1 = (bf16[1024,1024]{1,0:T(8,128)(2,1)}, bf16[1024,2304]{1,0:T(8,128)(2,1)}, bf16[1024,2048]{1,0:T(8,128)(2,1)}, bf16[1024,2304]{1,0:T(8,128)(2,1)}, bf16...) custom-call(s32[7]{0:T(128)} %pad_add_fusion.1.cont, ...), custom_call_target="tpu_custom_call" | custom-call | flops 1000000 | bytes 1048576 | tf_op jit(solution)/shard_map/front/pallas_call | solution.py:720
  89.5 14.3 %scan.1.y_ref = f32[1024,2048]{1,0:T(8,128)} custom-call(s32[7]{0:T(128)} %pad_add_fusion.1.cont, bf16[1024,2304]{1,0:T(8,128)(2,1)} %get-tuple-element.72.kq_ref.inner_ref, bf16[1024,2048]{1,0:T(8,128)(2,1)} %get-tuple-element.73.vp_ref, f32[1024,128]{1,0:T(8,128)} %get-tuple-element.74.tot_ref, f32[4,128,256]{2,1,0:T(8,128)} %get-tuple-element.75.tott_ref), custom_call_target="tpu_custom_call" | custom-call | flops 1000000 | bytes 1048576 | tf_op jit(solution)/shard_map/scan/pallas_call | solution.py:737
  103.8 2.5 collective-permute-done.11.sin_ref
  108.7 1.3 collective-permute-done.16.rest_4_.rest_13_
  110.1 1.1 collective-permute-done.18.rest_8_.rest_17_
  111.2 38.2 %gating.1 = (bf16[1024,1024]{1,0:T(8,128)(2,1)}, bf16[1024,2048]{1,0:T(8,128)(2,1)}, bf16[1024,2048]{1,0:T(8,128)(2,1)}, bf16[1024,2048]{1,0:T(8,128)(2,1)}, f32...) custom-call(s32[7]{0:T(128)} %pad_add_fusion.1.cont, ...), custom_call_target="tpu_custom_call" | custom-call | flops 35000000512 | bytes 41943040 | tf_op jit(solution)/shard_map/gating/pallas_call | solution.py:752
  149.4 2.8 collective-permute-start.19
  152.3 15.2 %wide_grad.1 = bf16[8,4,512,256]{3,2,1,0:T(8,128)(2,1)} custom-call(s32[7]{0:T(128)} %pad_add_fusion.1.cont, bf16[1024,2048]{1,0:T(8,128)(2,1)} %get-tuple-element.98.gn_ref, bf16[1024,1024]{1,0:T(8,128)(2,1)} %dy_ref.5, bf16[1024,1024]{1,0:T(8,128)(2,1)} %get-tuple-element.71.normed_ref, bf16[1024,2048]{1,0:T(8,128)(2,1)} %get-tuple-element.99.dgate_ref), custom_call_target="tpu_custom_call" | custom-call | flops 8600000512 | bytes 25165824 | tf_op jit(solution)/shard_map/wide_grad/pallas_call | solution.py:793
  167.5 0.8 copy-done.29
  168.3 46.1 %back.1 = (bf16[1024,2432]{1,0:T(8,128)(2,1)}, bf16[2432,1024]{1,0:T(8,128)(2,1)}, bf16[16,2432]{1,0:T(8,128)(2,1)}, bf16[2432,128]{1,0:T(8,128)(2,1)}, f32[8,2304]{1,0:T(8,128)}, /*index=5*/f32[8,128]{1,0:T(8,128)}) custom-call(s32[7]{0:T(128)} %pad_add_fusion.1.cont, bf16[1024,2304]{1,0:T(8,128)(2,1)} %get-tuple-element.72.kq_ref.inner_ref, ...), custom_call_target="tpu_custom_call" | custom-call | flops 60000002048 | bytes 31457280 | tf_op jit(solution)/shard_map/back/pallas_call | solution.py:772
  214.4 0.7 collective-permute-start.20
  215.1 7.7 %conv_grad.3 = bf16[4,4,304,256]{3,2,1,0:T(8,128)(2,1)} custom-call(s32[7]{0:T(128)} %pad_add_fusion.1.cont, bf16[1024,1024]{1,0:T(8,128)(2,1)} %get-tuple-element.71.normed_ref, bf16[2432,1024]{1,0:T(8,128)(2,1)} %get-tuple-element.93.turned_ref, bf16[128,1024]{1,0:T(8,128)(2,1)} %get-tuple-element.94.nh_ref, ...), custom_call_target="tpu_custom_call" | custom-call | flops 5000000000 | bytes 8388608 | tf_op jit(solution)/shard_map/conv_grad/pallas_call | solution.py:808
  222.9 7.7 %conv_grad.2 = bf16[4,4,304,256]{3,2,1,0:T(8,128)(2,1)} custom-call(s32[7]{0:T(128)} %pad_add_fusion.1.cont, bf16[1024,1024]{1,0:T(8,128)(2,1)} %get-tuple-element.71.normed_ref, bf16[2432,1024]{1,0:T(8,128)(2,1)} %get-tuple-element.93.turned_ref, bf16[128,1024]{1,0:T(8,128)(2,1)} %get-tuple-element.94.nh_ref, ...), custom_call_target="tpu_custom_call" | custom-call | flops 5000000000 | bytes 8388608 | tf_op jit(solution)/shard_map/conv_grad/pallas_call | solution.py:808
  230.6 2.3 fusion.3
  232.9 3.5 %reduce-scatter.3.cloned.1.call-done = bf16[1,4,512,256]{3,2,1,0:T(8,128)(2,1)} async-done(((bf16[8,4,512,256]{3,2,1,0:T(8,128)(2,1)}), bf16[1,4,512,256]{3,2,1,0:T(8,128)(2,1)}) %reduce-scatter.3.cloned.1.call-update) | async-done | bytes 1048592 | tf_op jit(solution)/shard_map/reduce_scatter | solution.py:987
  236.4 1.5 collective-permute-start.24
  237.9 1.4 collective-permute-start.23
  239.9 21.4 %input_grad.1 = (bf16[1024,1024]{1,0:T(8,128)(2,1)}, f32[8,1024]{1,0:T(8,128)}) custom-call(s32[7]{0:T(128)} %pad_add_fusion.1.cont, bf16[1024,1024]{1,0:T(8,128)(2,1)} %x_ref.5, bf16[1024,1024]{1,0:T(8,128)(2,1)} %dy_ref.5, bf16[1024,2432]{1,0:T(8,128)(2,1)} %get-tuple-element.101.gp_ref, bf16[1024,2048]{1,0:T(8,128)(2,1)} %get-tuple-element.99.dgate_ref, ...), custom_call_target="tpu_custom_call" | custom-call | flops 10000000000 | bytes 25165824 | tf_op jit(solution)/shard_map/input_grad/pallas_call | solution.py:824
  261.3 0.8 slice_reduce_fusion.11
  262.3 0.8 reduce_sum.28
  263.1 1.0 slice_reduce_fusion.5
  264.3 1.6 reduce-scatter.5.cloned.1.call-done
  267.5 1.6 add_convert_fusion
  269.2 1.6 collective-permute-start.26
  270.8 1.5 collective-permute-start.27
  272.9 2.4 collective-permute-start.40
  275.8 8.2 %collective-permute-done.26 = bf16[336,256]{1,0:T(8,128)(2,1)S(1)} collective-permute-done((bf16[336,256]{1,0:T(8,128)(2,1)S(1)}, bf16[336,256]{1,0:T(8,128)(2,1)S(1)}, u32[]{:S(2)}, u32[]{:S(2)}) %collective-permute-start.26) | collective-permute-done | bytes 172064 | tf_op jit(solution)/shard_map/ppermute | solution.py:872
  284.0 1.4 collective-permute-start.36
  285.6 1.5 collective-permute-start.33
  287.6 5.5 %collective-permute-done.36.rest_2_ = bf16[512,256]{1,0:T(8,128)(2,1)S(1)} collective-permute-done((bf16[512,256]{1,0:T(8,128)(2,1)S(1)}, bf16[512,256]{1,0:T(8,128)(2,1)S(1)}, u32[]{:S(2)}, u32[]{:S(2)}) %collective-permute-start.36) | collective-permute-done | bytes 262176 | tf_op jit(solution)/shard_map/ppermute | solution.py:872
  293.2 1.5 collective-permute-start.31
  295.2 2.6 collective-permute-done.33.rest_6_
  297.8 1.3 collective-permute-done.31.rest_4_
  299.1 1.0 collective-permute-done.29.rest_2_
  301.3 0.7 copy-done.16
  302.0 4.3 %finish_wide.1 = (f32[4384,256]{1,0:T(8,128)}, f32[512,1024]{1,0:T(8,128)}) custom-call(s32[7]{0:T(128)} %pad_add_fusion.1.cont, bf16[512,256]{1,0:T(8,128)(2,1)} %bitcast.76, bf16[512,256]{1,0:T(8,128)(2,1)} %copy-done.13, bf16[512,256]{1,0:T(8,128)(2,1)} %copy-done.12, bf16[512,256]{1,0:T(8,128)(2,1)} %copy-done.16, bf16[512,256]{1,0:T(8,128)(2,1)} %copy-done.11, ...), custom_call_target="tpu_custom_call" | custom-call | flops 1000000 | bytes 8388608 | tf_op jit(solution)/shard_map/finish_wide/pallas_call | solution.py:841
  307.2 4.2 %finish_conv.1 = (f32[4384,256]{1,0:T(8,128)}, f32[16,256]{1,0:T(8,128)}) custom-call(s32[7]{0:T(128)} %pad_add_fusion.1.cont, bf16[336,256]{1,0:T(8,128)(2,1)} %copy-done.5, bf16[336,256]{1,0:T(8,128)(2,1)} %copy-done.20, bf16[336,256]{1,0:T(8,128)(2,1)} %copy-done.19, bf16[336,256]{1,0:T(8,128)(2,1)} %copy-done.23, ...), custom_call_target="tpu_custom_call", output_to_operand_aliasing={{0}: (9, {})} | custom-call | flops 1000000 | bytes 5242880 | tf_op jit(solution)/shard_map/finish_conv/pallas_call | solution.py:855
  311.4 0.7 copy.33
  314.6 1.4 reshape.203
  (212 shorter events, 20.6 us)
Async XLA Ops:
  7.2 46.1 %all-gather.3.cloned.1.call-start = ((), (), s32[]{:S(2)}) async-start(), calls=%async_computation.4 | async-start | bytes 1310720 | tf_op jit(solution)/shard_map/all_gather | solution.py:957
  10.9 10.5 %copy-start.3 = (bf16[512,1024]{1,0:T(8,128)(2,1)S(1)}, bf16[512,1024]{1,0:T(8,128)(2,1)}, u32[]{:S(2)}) copy-start(bf16[512,1024]{1,0:T(8,128)(2,1)} %param.24) | copy-start | bytes 3145732
  11.7 16.5 %collective-permute-start.3 = (bf16[320,256]{1,0:T(8,128)(2,1)}, bf16[320,256]{1,0:T(8,128)(2,1)}, u32[]{:S(2)}, u32[]{:S(2)}) collective-permute-start(bf16[320,256]{1,0:T(8,128)(2,1)} %pad_maximum_fusion.7), channel_id=1, source_target_pairs={{0,3},{1,2},{2,1},{3,0},{4,7},{5,6},{6,5},{7,4},{8,11},{9,10},{10,... | collective-permute-start | bytes 491528 | tf_op jit(solution)/shard_map/ppermute | solution.py:872
  16.7 14.9 %collective-permute-start.2 = (bf16[320,256]{1,0:T(8,128)(2,1)}, bf16[320,256]{1,0:T(8,128)(2,1)}, u32[]{:S(2)}, u32[]{:S(2)}) collective-permute-start(bf16[320,256]{1,0:T(8,128)(2,1)} %pad_maximum_fusion.7), channel_id=1, source_target_pairs={{0,2},{1,3},{2,0},{3,1},{4,6},{5,7},{6,4},{7,5},{8,10},{9,11},{10,... | collective-permute-start | bytes 491528 | tf_op jit(solution)/shard_map/ppermute | solution.py:872
  16.7 14.9 %collective-permute-start.1 = (bf16[320,256]{1,0:T(8,128)(2,1)}, bf16[320,256]{1,0:T(8,128)(2,1)}, u32[]{:S(2)}, u32[]{:S(2)}) collective-permute-start(bf16[320,256]{1,0:T(8,128)(2,1)} %pad_maximum_fusion.7), channel_id=1, source_target_pairs={{0,1},{1,0},{2,3},{3,2},{4,5},{5,4},{6,7},{7,6},{8,9},{9,8},{10,11... | collective-permute-start | bytes 491528 | tf_op jit(solution)/shard_map/ppermute | solution.py:872
  18.7 40.0 %collective-permute-start = (bf16[16,1024]{1,0:T(8,128)(2,1)}, bf16[16,1024]{1,0:T(8,128)(2,1)}, u32[]{:S(2)}, u32[]{:S(2)}) collective-permute-start(bf16[16,1024]{1,0:T(8,128)(2,1)} %slice.193), channel_id=1, source_target_pairs={{0,1},{1,2},{2,3},{3,4},{4,5},{5,6},{6,7},{7,8},{8,9},{9,10},{10,1... | collective-permute-start | bytes 98312 | tf_op jit(solution)/shard_map/ppermute | solution.py:867
  21.4 2.3 copy-start.1
  23.7 9.1 %copy-start.2 = (bf16[4,512,256]{2,1,0:T(8,128)(2,1)}, bf16[4,512,256]{2,1,0:T(8,128)(2,1)S(1)}, u32[]{:S(2)}) copy-start(bf16[4,512,256]{2,1,0:T(8,128)(2,1)S(1)} %pad_maximum_fusion.rest_9_) | copy-start | bytes 3145732
  24.6 211.8 %reduce-scatter.3.cloned.1.call-start = ((), (), s32[]{:S(2)}) async-start(), calls=%async_computation.2 | async-start | bytes 9437184 | tf_op jit(solution)/shard_map/reduce_scatter | solution.py:987
  32.8 24.7 %copy-start = (bf16[3,320,256]{2,1,0:T(8,128)(2,1)}, bf16[3,320,256]{2,1,0:T(8,128)(2,1)S(1)}, u32[]{:S(2)}) copy-start(bf16[3,320,256]{2,1,0:T(8,128)(2,1)S(1)} %pad_maximum_fusion.1.rest_1_) | copy-start | bytes 1474564
  32.8 22.4 %collective-permute-start.7 = (bf16[3,320,256]{2,1,0:T(8,128)(2,1)S(1)}, bf16[3,320,256]{2,1,0:T(8,128)(2,1)S(1)}, u32[]{:S(2)}, u32[]{:S(2)}) collective-permute-start(bf16[3,320,256]{2,1,0:T(8,128)(2,1)S(1)} %pad_maximum_fusion.1.rest_1_), channel_id=1, source_target_pairs={{0,24},{1,25},{2,26},{3,27},{4,28},{5,29},{6,30},{7,31},{8,16},{9,... | collective-permute-start | bytes 1474568 | tf_op jit(solution)/shard_map/ppermute | solution.py:872
  35.3 21.2 %collective-permute-start.6 = (bf16[3,320,256]{2,1,0:T(8,128)(2,1)S(1)}, bf16[3,320,256]{2,1,0:T(8,128)(2,1)S(1)}, u32[]{:S(2)}, u32[]{:S(2)}) collective-permute-start(bf16[3,320,256]{2,1,0:T(8,128)(2,1)S(1)} %pad_maximum_fusion.1.rest_1_), channel_id=1, source_target_pairs={{0,16},{1,17},{2,18},{3,19},{4,20},{5,21},{6,22},{7,23},{8,24},{9,... | collective-permute-start | bytes 1474568 | tf_op jit(solution)/shard_map/ppermute | solution.py:872
  35.8 20.9 %collective-permute-start.5 = (bf16[3,320,256]{2,1,0:T(8,128)(2,1)S(1)}, bf16[3,320,256]{2,1,0:T(8,128)(2,1)}, u32[]{:S(2)}, u32[]{:S(2)}) collective-permute-start(bf16[3,320,256]{2,1,0:T(8,128)(2,1)S(1)} %pad_maximum_fusion.1.rest_1_), channel_id=1, source_target_pairs={{0,8},{1,9},{2,10},{3,11},{4,12},{5,13},{6,14},{7,15},{8,0},{9,1},... | collective-permute-start | bytes 1474568 | tf_op jit(solution)/shard_map/ppermute | solution.py:872
  39.4 21.0 %collective-permute-start.4 = (bf16[3,320,256]{2,1,0:T(8,128)(2,1)S(1)}, bf16[3,320,256]{2,1,0:T(8,128)(2,1)}, u32[]{:S(2)}, u32[]{:S(2)}) collective-permute-start(bf16[3,320,256]{2,1,0:T(8,128)(2,1)S(1)} %pad_maximum_fusion.1.rest_1_), channel_id=1, source_target_pairs={{0,4},{1,5},{2,6},{3,7},{4,0},{5,1},{6,2},{7,3},{8,12},{9,13},{10,... | collective-permute-start | bytes 1474568 | tf_op jit(solution)/shard_map/ppermute | solution.py:872
  55.2 34.3 %copy-start.4 = (bf16[3,512,256]{2,1,0:T(8,128)(2,1)}, bf16[3,512,256]{2,1,0:T(8,128)(2,1)S(1)}, u32[]{:S(2)}) copy-start(bf16[3,512,256]{2,1,0:T(8,128)(2,1)S(1)} %broadcast_select_fusion.rest_1_.rest_10_) | copy-start | bytes 2359300
  55.2 7.8 %copy-start.6 = (bf16[3,320,256]{2,1,0:T(8,128)(2,1)}, bf16[3,320,256]{2,1,0:T(8,128)(2,1)S(1)}, u32[]{:S(2)}) copy-start(bf16[3,320,256]{2,1,0:T(8,128)(2,1)S(1)} %collective-permute-done.7.rest_7_) | copy-start | bytes 1474564
  56.6 6.5 %copy-start.7 = (bf16[3,320,256]{2,1,0:T(8,128)(2,1)}, bf16[3,320,256]{2,1,0:T(8,128)(2,1)S(1)}, u32[]{:S(2)}) copy-start(bf16[3,320,256]{2,1,0:T(8,128)(2,1)S(1)} %collective-permute-done.6.rest_5_) | copy-start | bytes 1474564
  56.8 4.9 %collective-permute-start.8 = (bf16[3,320,256]{2,1,0:T(8,128)(2,1)}, bf16[3,320,256]{2,1,0:T(8,128)(2,1)S(1)}, u32[]{:S(2)}, u32[]{:S(2)}) collective-permute-start(bf16[3,320,256]{2,1,0:T(8,128)(2,1)} %collective-permute-done.5.rest_3_), channel_id=1, source_target_pairs={{0,4},{1,5},{2,6},{3,7},{4,0},{5,1},{6,2},{7,3},{8,12},{9,13},{10,... | collective-permute-start | bytes 1474568 | tf_op jit(solution)/shard_map/ppermute | solution.py:872
  57.5 5.5 %collective-permute-start.9 = (bf16[3,320,256]{2,1,0:T(8,128)(2,1)S(1)}, bf16[3,320,256]{2,1,0:T(8,128)(2,1)}, u32[]{:S(2)}, u32[]{:S(2)}) collective-permute-start(bf16[3,320,256]{2,1,0:T(8,128)(2,1)S(1)} %collective-permute-done.6.rest_5_), channel_id=1, source_target_pairs={{0,4},{1,5},{2,6},{3,7},{4,0},{5,1},{6,2},{7,3},{8,12},{9,13},{10,... | collective-permute-start | bytes 1474568 | tf_op jit(solution)/shard_map/ppermute | solution.py:872
  58.0 5.0 %collective-permute-start.10 = (bf16[3,320,256]{2,1,0:T(8,128)(2,1)S(1)}, bf16[3,320,256]{2,1,0:T(8,128)(2,1)}, u32[]{:S(2)}, u32[]{:S(2)}) collective-permute-start(bf16[3,320,256]{2,1,0:T(8,128)(2,1)S(1)} %collective-permute-done.7.rest_7_), channel_id=1, source_target_pairs={{0,4},{1,5},{2,6},{3,7},{4,0},{5,1},{6,2},{7,3},{8,12},{9,13},{10,... | collective-permute-start | bytes 1474568 | tf_op jit(solution)/shard_map/ppermute | solution.py:872
  58.7 45.1 %collective-permute-start.15 = (bf16[3,512,256]{2,1,0:T(8,128)(2,1)S(1)}, bf16[3,512,256]{2,1,0:T(8,128)(2,1)}, u32[]{:S(2)}, u32[]{:S(2)}) collective-permute-start(bf16[3,512,256]{2,1,0:T(8,128)(2,1)S(1)} %broadcast_select_fusion.rest_1_.rest_10_), channel_id=1, source_target_pairs={{0,24},{1,25},{2,26},{3,27},{4,28},{5,29},{6,30},{7,31},{8,16},{9,... | collective-permute-start | bytes 2359304 | tf_op jit(solution)/shard_map/ppermute | solution.py:872
  60.3 43.5 %collective-permute-start.14 = (bf16[3,512,256]{2,1,0:T(8,128)(2,1)S(1)}, bf16[3,512,256]{2,1,0:T(8,128)(2,1)}, u32[]{:S(2)}, u32[]{:S(2)}) collective-permute-start(bf16[3,512,256]{2,1,0:T(8,128)(2,1)S(1)} %broadcast_select_fusion.rest_1_.rest_10_), channel_id=1, source_target_pairs={{0,16},{1,17},{2,18},{3,19},{4,20},{5,21},{6,22},{7,23},{8,24},{9,... | collective-permute-start | bytes 2359304 | tf_op jit(solution)/shard_map/ppermute | solution.py:872
  61.6 42.2 %collective-permute-start.13 = (bf16[3,512,256]{2,1,0:T(8,128)(2,1)S(1)}, bf16[3,512,256]{2,1,0:T(8,128)(2,1)}, u32[]{:S(2)}, u32[]{:S(2)}) collective-permute-start(bf16[3,512,256]{2,1,0:T(8,128)(2,1)S(1)} %broadcast_select_fusion.rest_1_.rest_10_), channel_id=1, source_target_pairs={{0,8},{1,9},{2,10},{3,11},{4,12},{5,13},{6,14},{7,15},{8,0},{9,1},... | collective-permute-start | bytes 2359304 | tf_op jit(solution)/shard_map/ppermute | solution.py:872
  89.0 17.3 %collective-permute-start.11 = (bf16[128,2048]{1,0:T(8,128)(2,1)}, bf16[128,2048]{1,0:T(8,128)(2,1)S(1)}, u32[]{:S(2)}, u32[]{:S(2)}) collective-permute-start(bf16[128,2048]{1,0:T(8,128)(2,1)} %get-tuple-element.77), channel_id=1, source_target_pairs={{0,1},{1,2},{2,3},{3,4},{4,5},{5,6},{6,7},{7,8},{8,9},{9,10},{10,1... | collective-permute-start | bytes 1572872 | tf_op jit(solution)/shard_map/ppermute | solution.py:867
  89.5 19.1 %collective-permute-start.12 = (bf16[3,512,256]{2,1,0:T(8,128)(2,1)S(1)}, bf16[3,512,256]{2,1,0:T(8,128)(2,1)S(1)}, u32[]{:S(2)}, u32[]{:S(2)}) collective-permute-start(bf16[3,512,256]{2,1,0:T(8,128)(2,1)S(1)} %broadcast_select_fusion.rest_1_.rest_10_), channel_id=1, source_target_pairs={{0,4},{1,5},{2,6},{3,7},{4,0},{5,1},{6,2},{7,3},{8,12},{9,13},{10,... | collective-permute-start | bytes 2359304 | tf_op jit(solution)/shard_map/ppermute | solution.py:872
  106.3 3.6 %collective-permute-start.16 = (bf16[3,512,256]{2,1,0:T(8,128)(2,1)}, bf16[3,512,256]{2,1,0:T(8,128)(2,1)S(1)}, u32[]{:S(2)}, u32[]{:S(2)}) collective-permute-start(bf16[3,512,256]{2,1,0:T(8,128)(2,1)} %collective-permute-done.13.rest_3_.rest_12_), channel_id=1, source_target_pairs={{0,4},{1,5},{2,6},{3,7},{4,0},{5,1},{6,2},{7,3},{8,12},{9,13},{10,... | collective-permute-start | bytes 2359304 | tf_op jit(solution)/shard_map/ppermute | solution.py:872
  106.3 3.7 %collective-permute-start.17 = (bf16[3,512,256]{2,1,0:T(8,128)(2,1)}, bf16[3,512,256]{2,1,0:T(8,128)(2,1)}, u32[]{:S(2)}, u32[]{:S(2)}) collective-permute-start(bf16[3,512,256]{2,1,0:T(8,128)(2,1)} %collective-permute-done.14.rest_5_.rest_14_), channel_id=1, source_target_pairs={{0,4},{1,5},{2,6},{3,7},{4,0},{5,1},{6,2},{7,3},{8,12},{9,13},{10,... | collective-permute-start | bytes 2359304 | tf_op jit(solution)/shard_map/ppermute | solution.py:872
  106.8 4.4 %collective-permute-start.18 = (bf16[3,512,256]{2,1,0:T(8,128)(2,1)}, bf16[3,512,256]{2,1,0:T(8,128)(2,1)}, u32[]{:S(2)}, u32[]{:S(2)}) collective-permute-start(bf16[3,512,256]{2,1,0:T(8,128)(2,1)} %collective-permute-done.15.rest_7_.rest_16_), channel_id=1, source_target_pairs={{0,4},{1,5},{2,6},{3,7},{4,0},{5,1},{6,2},{7,3},{8,12},{9,13},{10,... | collective-permute-start | bytes 2359304 | tf_op jit(solution)/shard_map/ppermute | solution.py:872
  108.7 2.6 copy-start.26
  149.4 18.0 %collective-permute-start.19 = (bf16[128,2048]{1,0:T(8,128)(2,1)}, bf16[128,2048]{1,0:T(8,128)(2,1)S(1)}, u32[]{:S(2)}, u32[]{:S(2)}) collective-permute-start(bf16[128,2048]{1,0:T(8,128)(2,1)} %get-tuple-element.90), channel_id=1, source_target_pairs={{0,31},{1,0},{2,1},{3,2},{4,3},{5,4},{6,5},{7,6},{8,7},{9,8},{10,9... | collective-permute-start | bytes 1572872 | tf_op jit(solution)/shard_map/ppermute | solution.py:867
  168.3 97.7 %reduce-scatter.5.cloned.1.call-start = ((), (), s32[]{:S(2)}) async-start(), calls=%async_computation.3 | async-start | bytes 1310720 | tf_op jit(solution)/shard_map/reduce_scatter | solution.py:995
  214.4 8.4 %collective-permute-start.20 = (bf16[16,2432]{1,0:T(8,128)(2,1)}, bf16[16,2432]{1,0:T(8,128)(2,1)S(1)}, u32[]{:S(2)}, u32[]{:S(2)}) collective-permute-start(bf16[16,2432]{1,0:T(8,128)(2,1)} %get-tuple-element.96), channel_id=1, source_target_pairs={{0,31},{1,0},{2,1},{3,2},{4,3},{5,4},{6,5},{7,6},{8,7},{9,8},{10,9... | collective-permute-start | bytes 233480 | tf_op jit(solution)/shard_map/ppermute | solution.py:867
  222.8 7.8 %copy-start.30 = (bf16[16,2432]{1,0:T(8,128)(2,1)}, bf16[16,2432]{1,0:T(8,128)(2,1)S(1)}, u32[]{:S(2)}) copy-start(bf16[16,2432]{1,0:T(8,128)(2,1)S(1)} %collective-permute-done.20.ahead_ref) | copy-start | bytes 233476
  222.8 7.8 %collective-permute-start.21 = (bf16[4,4,304,256]{3,2,1,0:T(8,128)(2,1)}, bf16[4,4,304,256]{3,2,1,0:T(8,128)(2,1)S(1)}, u32[]{:S(2)}, u32[]{:S(2)}) collective-permute-start(bf16[4,4,304,256]{3,2,1,0:T(8,128)(2,1)} %conv_grad.3), channel_id=1, source_target_pairs={{0,4},{1,5},{2,6},{3,7},{4,0},{5,1},{6,2},{7,3},{8,12},{9,13},{10,... | collective-permute-start | bytes 7471112 | tf_op jit(solution)/shard_map/ppermute | solution.py:872
  236.4 31.0 %collective-permute-start.24 = (bf16[4,304,256]{2,1,0:T(8,128)(2,1)S(1)}, bf16[4,304,256]{2,1,0:T(8,128)(2,1)S(1)}, u32[]{:S(2)}, u32[]{:S(2)}) collective-permute-start(bf16[4,304,256]{2,1,0:T(8,128)(2,1)S(1)} %get-tuple-element.139), channel_id=1, source_target_pairs={{0,24},{1,25},{2,26},{3,27},{4,28},{5,29},{6,30},{7,31},{8,16},{9,... | collective-permute-start | bytes 1867784 | tf_op jit(solution)/shard_map/ppermute | solution.py:872
  237.9 29.5 %collective-permute-start.23 = (bf16[4,304,256]{2,1,0:T(8,128)(2,1)S(1)}, bf16[4,304,256]{2,1,0:T(8,128)(2,1)}, u32[]{:S(2)}, u32[]{:S(2)}) collective-permute-start(bf16[4,304,256]{2,1,0:T(8,128)(2,1)S(1)} %get-tuple-element.140), channel_id=1, source_target_pairs={{0,16},{1,17},{2,18},{3,19},{4,20},{5,21},{6,22},{7,23},{8,24},{9,... | collective-permute-start | bytes 1867784 | tf_op jit(solution)/shard_map/ppermute | solution.py:872
  239.3 28.2 %collective-permute-start.22 = (bf16[4,304,256]{2,1,0:T(8,128)(2,1)S(1)}, bf16[4,304,256]{2,1,0:T(8,128)(2,1)}, u32[]{:S(2)}, u32[]{:S(2)}) collective-permute-start(bf16[4,304,256]{2,1,0:T(8,128)(2,1)S(1)} %get-tuple-element.141), channel_id=1, source_target_pairs={{0,8},{1,9},{2,10},{3,11},{4,12},{5,13},{6,14},{7,15},{8,0},{9,1},... | collective-permute-start | bytes 1867784 | tf_op jit(solution)/shard_map/ppermute | solution.py:872
  239.9 26.0 %copy-start.25 = (f32[8,2304]{1,0:T(8,128)S(1)}, f32[8,2304]{1,0:T(8,128)}, u32[]{:S(2)}) copy-start(f32[8,2304]{1,0:T(8,128)} %get-tuple-element.109) | copy-start | bytes 221188
  267.4 5.4 %copy-start.9 = (bf16[1,512,256]{2,1,0:T(8,128)(2,1)S(1)}, bf16[1,512,256]{2,1,0:T(8,128)(2,1)}, u32[]{:S(2)}) copy-start(bf16[1,512,256]{2,1,0:T(8,128)(2,1)} %reduce-scatter.5.cloned.1.call-done) | copy-start | bytes 786436
  269.2 14.8 %collective-permute-start.26 = (bf16[336,256]{1,0:T(8,128)(2,1)S(1)}, bf16[336,256]{1,0:T(8,128)(2,1)S(1)}, u32[]{:S(2)}, u32[]{:S(2)}) collective-permute-start(bf16[336,256]{1,0:T(8,128)(2,1)S(1)} %pad_maximum_fusion.4), channel_id=1, source_target_pairs={{0,2},{1,3},{2,0},{3,1},{4,6},{5,7},{6,4},{7,5},{8,10},{9,11},{10,... | collective-permute-start | bytes 516104 | tf_op jit(solution)/shard_map/ppermute | solution.py:872
  270.8 14.6 %collective-permute-start.27 = (bf16[336,256]{1,0:T(8,128)(2,1)S(1)}, bf16[336,256]{1,0:T(8,128)(2,1)S(1)}, u32[]{:S(2)}, u32[]{:S(2)}) collective-permute-start(bf16[336,256]{1,0:T(8,128)(2,1)S(1)} %pad_maximum_fusion.5), channel_id=1, source_target_pairs={{0,3},{1,2},{2,1},{3,0},{4,7},{5,6},{6,5},{7,4},{8,11},{9,10},{10,... | collective-permute-start | bytes 516104 | tf_op jit(solution)/shard_map/ppermute | solution.py:872
  272.3 13.1 %collective-permute-start.25 = (bf16[336,256]{1,0:T(8,128)(2,1)S(1)}, bf16[336,256]{1,0:T(8,128)(2,1)S(1)}, u32[]{:S(2)}, u32[]{:S(2)}) collective-permute-start(bf16[336,256]{1,0:T(8,128)(2,1)S(1)} %pad_maximum_fusion.3), channel_id=1, source_target_pairs={{0,1},{1,0},{2,3},{3,2},{4,5},{5,4},{6,7},{7,6},{8,9},{9,8},{10,11... | collective-permute-start | bytes 516104 | tf_op jit(solution)/shard_map/ppermute | solution.py:872
  272.9 14.2 %collective-permute-start.40 = (bf16[512,256]{1,0:T(8,128)(2,1)S(1)}, bf16[512,256]{1,0:T(8,128)(2,1)S(1)}, u32[]{:S(2)}, u32[]{:S(2)}) collective-permute-start(bf16[512,256]{1,0:T(8,128)(2,1)S(1)} %bitcast.77), channel_id=1, source_target_pairs={{0,24},{1,25},{2,26},{3,27},{4,28},{5,29},{6,30},{7,31},{8,16},{9,... | collective-permute-start | bytes 786440 | tf_op jit(solution)/shard_map/ppermute | solution.py:872
  275.3 12.1 %collective-permute-start.38 = (bf16[512,256]{1,0:T(8,128)(2,1)S(1)}, bf16[512,256]{1,0:T(8,128)(2,1)S(1)}, u32[]{:S(2)}, u32[]{:S(2)}) collective-permute-start(bf16[512,256]{1,0:T(8,128)(2,1)S(1)} %bitcast.78), channel_id=1, source_target_pairs={{0,16},{1,17},{2,18},{3,19},{4,20},{5,21},{6,22},{7,23},{8,24},{9,... | collective-permute-start | bytes 786440 | tf_op jit(solution)/shard_map/ppermute | solution.py:872
  284.0 9.1 %collective-permute-start.36 = (bf16[512,256]{1,0:T(8,128)(2,1)S(1)}, bf16[512,256]{1,0:T(8,128)(2,1)S(1)}, u32[]{:S(2)}, u32[]{:S(2)}) collective-permute-start(bf16[512,256]{1,0:T(8,128)(2,1)S(1)} %bitcast.79), channel_id=1, source_target_pairs={{0,8},{1,9},{2,10},{3,11},{4,12},{5,13},{6,14},{7,15},{8,0},{9,1},... | collective-permute-start | bytes 786440 | tf_op jit(solution)/shard_map/ppermute | solution.py:872
  285.4 9.3 %collective-permute-start.35 = (bf16[512,256]{1,0:T(8,128)(2,1)S(1)}, bf16[512,256]{1,0:T(8,128)(2,1)S(1)}, u32[]{:S(2)}, u32[]{:S(2)}) collective-permute-start(bf16[512,256]{1,0:T(8,128)(2,1)S(1)} %bitcast.80), channel_id=1, source_target_pairs={{0,4},{1,5},{2,6},{3,7},{4,0},{5,1},{6,2},{7,3},{8,12},{9,13},{10,... | collective-permute-start | bytes 786440 | tf_op jit(solution)/shard_map/ppermute | solution.py:872
  285.6 20.9 %copy-start.5 = (bf16[336,256]{1,0:T(8,128)(2,1)}, bf16[336,256]{1,0:T(8,128)(2,1)S(1)}, u32[]{:S(2)}) copy-start(bf16[336,256]{1,0:T(8,128)(2,1)S(1)} %pad_maximum_fusion.6.rest_0_) | copy-start | bytes 516100
  285.6 12.2 %collective-permute-start.33 = (bf16[336,256]{1,0:T(8,128)(2,1)S(1)}, bf16[336,256]{1,0:T(8,128)(2,1)S(1)}, u32[]{:S(2)}, u32[]{:S(2)}) collective-permute-start(bf16[336,256]{1,0:T(8,128)(2,1)S(1)} %pad_maximum_fusion.6.rest_0_), channel_id=1, source_target_pairs={{0,24},{1,25},{2,26},{3,27},{4,28},{5,29},{6,30},{7,31},{8,16},{9,... | collective-permute-start | bytes 516104 | tf_op jit(solution)/shard_map/ppermute | solution.py:872
  287.1 13.6 %copy-start.10 = (bf16[512,256]{1,0:T(8,128)(2,1)}, bf16[512,256]{1,0:T(8,128)(2,1)S(1)}, u32[]{:S(2)}) copy-start(bf16[512,256]{1,0:T(8,128)(2,1)S(1)} %collective-permute-done.40.rest_6_) | copy-start | bytes 786436
  287.1 13.0 %collective-permute-start.41 = (bf16[512,256]{1,0:T(8,128)(2,1)S(1)}, bf16[512,256]{1,0:T(8,128)(2,1)S(1)}, u32[]{:S(2)}, u32[]{:S(2)}) collective-permute-start(bf16[512,256]{1,0:T(8,128)(2,1)S(1)} %collective-permute-done.40.rest_6_), channel_id=1, source_target_pairs={{0,4},{1,5},{2,6},{3,7},{4,0},{5,1},{6,2},{7,3},{8,12},{9,13},{10,... | collective-permute-start | bytes 786440 | tf_op jit(solution)/shard_map/ppermute | solution.py:872
  287.3 13.3 %copy-start.11 = (bf16[512,256]{1,0:T(8,128)(2,1)}, bf16[512,256]{1,0:T(8,128)(2,1)S(1)}, u32[]{:S(2)}) copy-start(bf16[512,256]{1,0:T(8,128)(2,1)S(1)} %collective-permute-done.38.rest_4_) | copy-start | bytes 786436
  287.3 13.2 %collective-permute-start.39 = (bf16[512,256]{1,0:T(8,128)(2,1)S(1)}, bf16[512,256]{1,0:T(8,128)(2,1)S(1)}, u32[]{:S(2)}, u32[]{:S(2)}) collective-permute-start(bf16[512,256]{1,0:T(8,128)(2,1)S(1)} %collective-permute-done.38.rest_4_), channel_id=1, source_target_pairs={{0,4},{1,5},{2,6},{3,7},{4,0},{5,1},{6,2},{7,3},{8,12},{9,13},{10,... | collective-permute-start | bytes 786440 | tf_op jit(solution)/shard_map/ppermute | solution.py:872
  293.2 7.5 %copy-start.12 = (bf16[512,256]{1,0:T(8,128)(2,1)}, bf16[512,256]{1,0:T(8,128)(2,1)S(1)}, u32[]{:S(2)}) copy-start(bf16[512,256]{1,0:T(8,128)(2,1)S(1)} %collective-permute-done.36.rest_2_) | copy-start | bytes 786436
  293.2 5.9 %collective-permute-start.31 = (bf16[336,256]{1,0:T(8,128)(2,1)S(1)}, bf16[336,256]{1,0:T(8,128)(2,1)S(1)}, u32[]{:S(2)}, u32[]{:S(2)}) collective-permute-start(bf16[336,256]{1,0:T(8,128)(2,1)S(1)} %pad_maximum_fusion.6.rest_0_), channel_id=1, source_target_pairs={{0,16},{1,17},{2,18},{3,19},{4,20},{5,21},{6,22},{7,23},{8,24},{9,... | collective-permute-start | bytes 516104 | tf_op jit(solution)/shard_map/ppermute | solution.py:872
  294.6 6.0 %copy-start.13 = (bf16[512,256]{1,0:T(8,128)(2,1)}, bf16[512,256]{1,0:T(8,128)(2,1)S(1)}, u32[]{:S(2)}) copy-start(bf16[512,256]{1,0:T(8,128)(2,1)S(1)} %collective-permute-done.35.rest_1_) | copy-start | bytes 786436
  294.6 5.4 %collective-permute-start.29 = (bf16[336,256]{1,0:T(8,128)(2,1)S(1)}, bf16[336,256]{1,0:T(8,128)(2,1)S(1)}, u32[]{:S(2)}, u32[]{:S(2)}) collective-permute-start(bf16[336,256]{1,0:T(8,128)(2,1)S(1)} %pad_maximum_fusion.6.rest_0_), channel_id=1, source_target_pairs={{0,8},{1,9},{2,10},{3,11},{4,12},{5,13},{6,14},{7,15},{8,0},{9,1},... | collective-permute-start | bytes 516104 | tf_op jit(solution)/shard_map/ppermute | solution.py:872
  297.8 8.7 %copy-start.17 = (bf16[336,256]{1,0:T(8,128)(2,1)}, bf16[336,256]{1,0:T(8,128)(2,1)S(1)}, u32[]{:S(2)}) copy-start(bf16[336,256]{1,0:T(8,128)(2,1)S(1)} %collective-permute-done.33.rest_6_) | copy-start | bytes 516100
  297.8 2.9 collective-permute-start.37
  299.1 7.4 %copy-start.18 = (bf16[336,256]{1,0:T(8,128)(2,1)}, bf16[336,256]{1,0:T(8,128)(2,1)S(1)}, u32[]{:S(2)}) copy-start(bf16[336,256]{1,0:T(8,128)(2,1)S(1)} %collective-permute-done.31.rest_4_) | copy-start | bytes 516100
  299.1 7.2 %collective-permute-start.28 = (bf16[336,256]{1,0:T(8,128)(2,1)S(1)}, bf16[336,256]{1,0:T(8,128)(2,1)S(1)}, u32[]{:S(2)}, u32[]{:S(2)}) collective-permute-start(bf16[336,256]{1,0:T(8,128)(2,1)S(1)} %pad_maximum_fusion.6.rest_0_), channel_id=1, source_target_pairs={{0,4},{1,5},{2,6},{3,7},{4,0},{5,1},{6,2},{7,3},{8,12},{9,13},{10,... | collective-permute-start | bytes 516104 | tf_op jit(solution)/shard_map/ppermute | solution.py:872
  300.1 6.4 %copy-start.19 = (bf16[336,256]{1,0:T(8,128)(2,1)}, bf16[336,256]{1,0:T(8,128)(2,1)S(1)}, u32[]{:S(2)}) copy-start(bf16[336,256]{1,0:T(8,128)(2,1)S(1)} %collective-permute-done.29.rest_2_) | copy-start | bytes 516100
  300.1 6.3 %collective-permute-start.34 = (bf16[336,256]{1,0:T(8,128)(2,1)S(1)}, bf16[336,256]{1,0:T(8,128)(2,1)S(1)}, u32[]{:S(2)}, u32[]{:S(2)}) collective-permute-start(bf16[336,256]{1,0:T(8,128)(2,1)S(1)} %collective-permute-done.33.rest_6_), channel_id=1, source_target_pairs={{0,4},{1,5},{2,6},{3,7},{4,0},{5,1},{6,2},{7,3},{8,12},{9,13},{10,... | collective-permute-start | bytes 516104 | tf_op jit(solution)/shard_map/ppermute | solution.py:872
  300.1 6.3 %collective-permute-start.32 = (bf16[336,256]{1,0:T(8,128)(2,1)S(1)}, bf16[336,256]{1,0:T(8,128)(2,1)S(1)}, u32[]{:S(2)}, u32[]{:S(2)}) collective-permute-start(bf16[336,256]{1,0:T(8,128)(2,1)S(1)} %collective-permute-done.31.rest_4_), channel_id=1, source_target_pairs={{0,4},{1,5},{2,6},{3,7},{4,0},{5,1},{6,2},{7,3},{8,12},{9,13},{10,... | collective-permute-start | bytes 516104 | tf_op jit(solution)/shard_map/ppermute | solution.py:872
  300.6 5.8 %collective-permute-start.30 = (bf16[336,256]{1,0:T(8,128)(2,1)S(1)}, bf16[336,256]{1,0:T(8,128)(2,1)S(1)}, u32[]{:S(2)}, u32[]{:S(2)}) collective-permute-start(bf16[336,256]{1,0:T(8,128)(2,1)S(1)} %collective-permute-done.29.rest_2_), channel_id=1, source_target_pairs={{0,4},{1,5},{2,6},{3,7},{4,0},{5,1},{6,2},{7,3},{8,12},{9,13},{10,... | collective-permute-start | bytes 516104 | tf_op jit(solution)/shard_map/ppermute | solution.py:872
  (12 other events, 10.1 us)
Sparse Core Ops, SparseCore 0:
  24.7 28.4 all-gather.2
  167.6 68.6 reduce-scatter.2
  238.8 27.1 reduce-scatter.4

commit v3 on v2

--- a/solution.py
+++ b/solution.py
@@ -978,7 +978,7 @@
     normed, inner, vp, cs, cin, stp, sig, tot, tott, sloc, fin, nh, ch = front(cont, tokens, halo, ng, wc, cw, sp, shards)
     sin = shift(fin, 1)
     y = scan(cont, inner, vp, tot, tott)
-    wg = [wgs, *over_cores(gate_plane[:1] + after(gate_plane[1:], y, sin))]
+    wg = [wgs, *over_cores(gate_plane[:1] + after(gate_plane[1:-1], y) + after(gate_plane[-1:], y, sin))]
     output, gn, dgate, dmix, yd, sc, dlead, sums = gating(
         cont, tokens, cotangent, normed, inner, y, tot, sloc, sin, wg, wo_own, gg, sk, shards
     )

time: 324 us -> 324 us (level)
  transfers between devices with their start and end apart: 45 -> 45, of which waited for: 15 -> 13; matrix products, arithmetic and copies ran while one was open for 8% -> 8% of each run, Pallas kernels for 44% -> 44%
where the time goes in v3:
time: 324 us; the launch traced here: 323 us
  Pallas kernels  185 us (57%)
  waiting for transfers between devices  44.4 us (14%)
  starting transfers between devices  37.2 us (11%)
  local copies, waits for them, and re-layouts  28.2 us (9%)
  between operations  14.6 us (5%)
  other arithmetic  13 us (4%)
    pallas_call x1, Pallas kernels, back(): call(back_kernel, nb, [rows_of(2 * NS, nb, DI // (2 * NS)), rows_of(DI, n...  46 us
    pallas_call x1, Pallas kernels, gating(): call(partial(gate_kernel, count), nb, [rows_of(D), rows_of(D), rows_of(D)...  38.2 us
    ppermute x38, starting transfers between devices, swap(): return lax.ppermute(v, BOTH, [(i, i ^ mask) for i in range(n)])  30.2 us
    pallas_call x1, Pallas kernels, front(): call(partial(front_kernel, count), nb, [rows_of(D), whole(16, D), whole(1...  25.9 us
    ppermute x38, waiting for transfers between devices, swap(): return lax.ppermute(v, BOTH, [(i, i ^ mask) for i in range(n)])  23.9 us
    pallas_call x1, Pallas kernels, input_grad(): call(partial(input_grad_kernel, convs, gates), nb, [rows_of(D), rows_of(D...  21.4 us
    pallas_call x2, Pallas kernels, conv_grad(): call(partial(conv_grad_kernel, nb), shards, [pl.BlockSpec((rows, m), lamb...  15.5 us
    pallas_call x1, Pallas kernels, wide_grad(): call(wide_grad_kernel, shards, [pl.BlockSpec((rows, block), lambda k, c:...  15.2 us
  transfers between devices with their start and end apart: 45, of which 13 were waited for; matrix products, arithmetic and copies ran while one was open for 8% of the time, Pallas kernels for 44%

profile of v3, /device:TPU:0, one launch (start us, length us, event | category | flops | bytes accessed | tf_op | source)
XLA Modules:
  0.0 322.5 jit_solution(13704733335187942586)
XLA Ops:
  7.2 0.9 slice_reduce_fusion.10
  8.1 0.9 pad_add_fusion
  9.6 1.4 slice.261
  11.7 5.0 %collective-permute-start.3 = (bf16[320,256]{1,0:T(8,128)(2,1)}, bf16[320,256]{1,0:T(8,128)(2,1)}, u32[]{:S(2)}, u32[]{:S(2)}) collective-permute-start(bf16[320,256]{1,0:T(8,128)(2,1)} %pad_maximum_fusion.7), channel_id=1, source_target_pairs={{0,3},{1,2},{2,1},{3,0},{4,7},{5,6},{6,5},{7,4},{8,11},{9,10},{10,... | collective-permute-start | bytes 491528 | tf_op jit(solution)/shard_map/ppermute | solution.py:872
  17.3 1.4 slice.193
  18.7 1.5 collective-permute-start
  20.1 1.3 slice.273.rest_0_.rest_9_
  21.5 1.0 slice_bitcast_fusion.3
  22.4 1.2 pad_maximum_fusion.rest_9_
  23.7 0.8 pad_maximum_fusion.2
  24.7 0.8 select_reduce_fusion
  26.3 0.7 stack.50
  27.0 1.1 pad.61.rest_0_
  28.2 3.4 %collective-permute-done.2 = bf16[320,256]{1,0:T(8,128)(2,1)} collective-permute-done((bf16[320,256]{1,0:T(8,128)(2,1)}, bf16[320,256]{1,0:T(8,128)(2,1)}, u32[]{:S(2)}, u32[]{:S(2)}) %collective-permute-start.2) | collective-permute-done | bytes 163872 | tf_op jit(solution)/shard_map/ppermute | solution.py:872
  31.6 1.2 pad_maximum_fusion.1.rest_1_
  32.8 2.5 collective-permute-start.7
  36.4 0.7 slice_bitcast_fusion.9
  37.1 0.7 slice_bitcast_fusion.10
  37.8 0.7 slice_bitcast_fusion.11
  39.8 13.5 %all-gather.3.cloned.1.call-done = bf16[2048,256]{1,0:T(8,128)(2,1)} async-done(((bf16[512,256]{1,0:T(8,128)(2,1)}), bf16[2048,256]{1,0:T(8,128)(2,1)}) %all-gather.3.cloned.1.call-update) | async-done | bytes 1048592 | tf_op jit(solution)/shard_map/all_gather | solution.py:957
  53.2 1.8 gather_fusion.1
  55.2 1.3 collective-permute-done.6.rest_5_
  56.8 0.7 maximum_maximum_fusion.cw_ref
  58.7 1.7 collective-permute-start.17
  60.3 1.3 collective-permute-start.14
  63.1 25.9 %front.1 = (bf16[1024,1024]{1,0:T(8,128)(2,1)}, bf16[1024,2304]{1,0:T(8,128)(2,1)}, bf16[1024,2048]{1,0:T(8,128)(2,1)}, bf16[1024,2304]{1,0:T(8,128)(2,1)}, bf16...) custom-call(s32[7]{0:T(128)} %pad_add_fusion.1.cont, ...), custom_call_target="tpu_custom_call" | custom-call | flops 1000000 | bytes 1048576 | tf_op jit(solution)/shard_map/front/pallas_call | solution.py:720
  89.5 14.3 %scan.1.y_ref = f32[1024,2048]{1,0:T(8,128)} custom-call(s32[7]{0:T(128)} %pad_add_fusion.1.cont, bf16[1024,2304]{1,0:T(8,128)(2,1)} %get-tuple-element.72.kq_ref.inner_ref, bf16[1024,2048]{1,0:T(8,128)(2,1)} %get-tuple-element.73.vp_ref, f32[1024,128]{1,0:T(8,128)} %get-tuple-element.74.tot_ref, f32[4,128,256]{2,1,0:T(8,128)} %get-tuple-element.75.tott_ref), custom_call_target="tpu_custom_call" | custom-call | flops 1000000 | bytes 1048576 | tf_op jit(solution)/shard_map/scan/pallas_call | solution.py:737
  104.4 1.9 collective-permute-done.11.sin_ref
  106.3 0.8 copy-done.28
  108.0 0.7 broadcast_in_dim.71.sk_ref
  109.8 38.2 %gating.1 = (bf16[1024,1024]{1,0:T(8,128)(2,1)}, bf16[1024,2048]{1,0:T(8,128)(2,1)}, bf16[1024,2048]{1,0:T(8,128)(2,1)}, bf16[1024,2048]{1,0:T(8,128)(2,1)}, f32...) custom-call(s32[7]{0:T(128)} %pad_add_fusion.1.cont, ...), custom_call_target="tpu_custom_call" | custom-call | flops 35000000512 | bytes 41943040 | tf_op jit(solution)/shard_map/gating/pallas_call | solution.py:752
  148.0 4.2 %collective-permute-start.19 = (bf16[128,2048]{1,0:T(8,128)(2,1)}, bf16[128,2048]{1,0:T(8,128)(2,1)S(1)}, u32[]{:S(2)}, u32[]{:S(2)}) collective-permute-start(bf16[128,2048]{1,0:T(8,128)(2,1)} %get-tuple-element.90), channel_id=1, source_target_pairs={{0,31},{1,0},{2,1},{3,2},{4,3},{5,4},{6,5},{7,6},{8,7},{9,8},{10,9... | collective-permute-start | bytes 1572872 | tf_op jit(solution)/shard_map/ppermute | solution.py:867
  152.2 15.2 %wide_grad.1 = bf16[8,4,512,256]{3,2,1,0:T(8,128)(2,1)} custom-call(s32[7]{0:T(128)} %pad_add_fusion.1.cont, bf16[1024,2048]{1,0:T(8,128)(2,1)} %get-tuple-element.98.gn_ref, bf16[1024,1024]{1,0:T(8,128)(2,1)} %dy_ref.5, bf16[1024,1024]{1,0:T(8,128)(2,1)} %get-tuple-element.71.normed_ref, bf16[1024,2048]{1,0:T(8,128)(2,1)} %get-tuple-element.99.dgate_ref), custom_call_target="tpu_custom_call" | custom-call | flops 8600000512 | bytes 25165824 | tf_op jit(solution)/shard_map/wide_grad/pallas_call | solution.py:793
  167.5 0.8 copy-done.29
  168.2 46.0 %back.1 = (bf16[1024,2432]{1,0:T(8,128)(2,1)}, bf16[2432,1024]{1,0:T(8,128)(2,1)}, bf16[16,2432]{1,0:T(8,128)(2,1)}, bf16[2432,128]{1,0:T(8,128)(2,1)}, f32[8,2304]{1,0:T(8,128)}, /*index=5*/f32[8,128]{1,0:T(8,128)}) custom-call(s32[7]{0:T(128)} %pad_add_fusion.1.cont, bf16[1024,2304]{1,0:T(8,128)(2,1)} %get-tuple-element.72.kq_ref.inner_ref, ...), custom_call_target="tpu_custom_call" | custom-call | flops 60000002048 | bytes 31457280 | tf_op jit(solution)/shard_map/back/pallas_call | solution.py:772
  214.3 0.8 collective-permute-start.20
  215.1 7.7 %conv_grad.3 = bf16[4,4,304,256]{3,2,1,0:T(8,128)(2,1)} custom-call(s32[7]{0:T(128)} %pad_add_fusion.1.cont, bf16[1024,1024]{1,0:T(8,128)(2,1)} %get-tuple-element.71.normed_ref, bf16[2432,1024]{1,0:T(8,128)(2,1)} %get-tuple-element.93.turned_ref, bf16[128,1024]{1,0:T(8,128)(2,1)} %get-tuple-element.94.nh_ref, ...), custom_call_target="tpu_custom_call" | custom-call | flops 5000000000 | bytes 8388608 | tf_op jit(solution)/shard_map/conv_grad/pallas_call | solution.py:808
  222.9 7.8 %conv_grad.2 = bf16[4,4,304,256]{3,2,1,0:T(8,128)(2,1)} custom-call(s32[7]{0:T(128)} %pad_add_fusion.1.cont, bf16[1024,1024]{1,0:T(8,128)(2,1)} %get-tuple-element.71.normed_ref, bf16[2432,1024]{1,0:T(8,128)(2,1)} %get-tuple-element.93.turned_ref, bf16[128,1024]{1,0:T(8,128)(2,1)} %get-tuple-element.94.nh_ref, ...), custom_call_target="tpu_custom_call" | custom-call | flops 5000000000 | bytes 8388608 | tf_op jit(solution)/shard_map/conv_grad/pallas_call | solution.py:808
  230.6 2.3 fusion.3
  232.9 3.5 %reduce-scatter.3.cloned.1.call-done = bf16[1,4,512,256]{3,2,1,0:T(8,128)(2,1)} async-done(((bf16[8,4,512,256]{3,2,1,0:T(8,128)(2,1)}), bf16[1,4,512,256]{3,2,1,0:T(8,128)(2,1)}) %reduce-scatter.3.cloned.1.call-update) | async-done | bytes 1048592 | tf_op jit(solution)/shard_map/reduce_scatter | solution.py:987
  236.4 1.5 collective-permute-start.24
  237.9 1.4 collective-permute-start.23
  239.9 21.4 %input_grad.1 = (bf16[1024,1024]{1,0:T(8,128)(2,1)}, f32[8,1024]{1,0:T(8,128)}) custom-call(s32[7]{0:T(128)} %pad_add_fusion.1.cont, bf16[1024,1024]{1,0:T(8,128)(2,1)} %x_ref.5, bf16[1024,1024]{1,0:T(8,128)(2,1)} %dy_ref.5, bf16[1024,2432]{1,0:T(8,128)(2,1)} %get-tuple-element.101.gp_ref, bf16[1024,2048]{1,0:T(8,128)(2,1)} %get-tuple-element.99.dgate_ref, ...), custom_call_target="tpu_custom_call" | custom-call | flops 10000000000 | bytes 25165824 | tf_op jit(solution)/shard_map/input_grad/pallas_call | solution.py:824
  261.3 0.8 slice_reduce_fusion.11
  262.3 0.8 reduce_sum.28
  263.0 1.0 slice_reduce_fusion.5
  264.3 1.6 reduce-scatter.5.cloned.1.call-done
  267.4 1.6 add_convert_fusion
  269.1 1.6 collective-permute-start.26
  270.8 1.5 collective-permute-start.27
  272.9 2.4 collective-permute-start.40
  275.8 8.2 %collective-permute-done.26 = bf16[336,256]{1,0:T(8,128)(2,1)S(1)} collective-permute-done((bf16[336,256]{1,0:T(8,128)(2,1)S(1)}, bf16[336,256]{1,0:T(8,128)(2,1)S(1)}, u32[]{:S(2)}, u32[]{:S(2)}) %collective-permute-start.26) | collective-permute-done | bytes 172064 | tf_op jit(solution)/shard_map/ppermute | solution.py:872
  284.0 1.4 collective-permute-start.36
  285.6 1.5 collective-permute-start.33
  287.6 5.5 %collective-permute-done.36.rest_2_ = bf16[512,256]{1,0:T(8,128)(2,1)S(1)} collective-permute-done((bf16[512,256]{1,0:T(8,128)(2,1)S(1)}, bf16[512,256]{1,0:T(8,128)(2,1)S(1)}, u32[]{:S(2)}, u32[]{:S(2)}) %collective-permute-start.36) | collective-permute-done | bytes 262176 | tf_op jit(solution)/shard_map/ppermute | solution.py:872
  293.1 1.5 collective-permute-start.31
  295.2 2.6 collective-permute-done.33.rest_6_
  297.8 1.3 collective-permute-done.31.rest_4_
  299.1 1.0 collective-permute-done.29.rest_2_
  301.3 0.7 copy-done.16
  302.0 4.3 %finish_wide.1 = (f32[4384,256]{1,0:T(8,128)}, f32[512,1024]{1,0:T(8,128)}) custom-call(s32[7]{0:T(128)} %pad_add_fusion.1.cont, bf16[512,256]{1,0:T(8,128)(2,1)} %bitcast.76, bf16[512,256]{1,0:T(8,128)(2,1)} %copy-done.13, bf16[512,256]{1,0:T(8,128)(2,1)} %copy-done.12, bf16[512,256]{1,0:T(8,128)(2,1)} %copy-done.16, bf16[512,256]{1,0:T(8,128)(2,1)} %copy-done.11, ...), custom_call_target="tpu_custom_call" | custom-call | flops 1000000 | bytes 8388608 | tf_op jit(solution)/shard_map/finish_wide/pallas_call | solution.py:841
  307.2 4.2 %finish_conv.1 = (f32[4384,256]{1,0:T(8,128)}, f32[16,256]{1,0:T(8,128)}) custom-call(s32[7]{0:T(128)} %pad_add_fusion.1.cont, bf16[336,256]{1,0:T(8,128)(2,1)} %copy-done.5, bf16[336,256]{1,0:T(8,128)(2,1)} %copy-done.20, bf16[336,256]{1,0:T(8,128)(2,1)} %copy-done.19, bf16[336,256]{1,0:T(8,128)(2,1)} %copy-done.23, ...), custom_call_target="tpu_custom_call", output_to_operand_aliasing={{0}: (9, {})} | custom-call | flops 1000000 | bytes 5242880 | tf_op jit(solution)/shard_map/finish_conv/pallas_call | solution.py:855
  311.4 0.7 copy.33
  314.6 1.4 reshape.203
  (212 shorter events, 20.7 us)
Async XLA Ops:
  7.2 46.1 %all-gather.3.cloned.1.call-start = ((), (), s32[]{:S(2)}) async-start(), calls=%async_computation.4 | async-start | bytes 1310720 | tf_op jit(solution)/shard_map/all_gather | solution.py:957
  10.9 10.5 %copy-start.3 = (bf16[512,1024]{1,0:T(8,128)(2,1)S(1)}, bf16[512,1024]{1,0:T(8,128)(2,1)}, u32[]{:S(2)}) copy-start(bf16[512,1024]{1,0:T(8,128)(2,1)} %param.24) | copy-start | bytes 3145732
  11.7 16.5 %collective-permute-start.3 = (bf16[320,256]{1,0:T(8,128)(2,1)}, bf16[320,256]{1,0:T(8,128)(2,1)}, u32[]{:S(2)}, u32[]{:S(2)}) collective-permute-start(bf16[320,256]{1,0:T(8,128)(2,1)} %pad_maximum_fusion.7), channel_id=1, source_target_pairs={{0,3},{1,2},{2,1},{3,0},{4,7},{5,6},{6,5},{7,4},{8,11},{9,10},{10,... | collective-permute-start | bytes 491528 | tf_op jit(solution)/shard_map/ppermute | solution.py:872
  16.7 14.9 %collective-permute-start.2 = (bf16[320,256]{1,0:T(8,128)(2,1)}, bf16[320,256]{1,0:T(8,128)(2,1)}, u32[]{:S(2)}, u32[]{:S(2)}) collective-permute-start(bf16[320,256]{1,0:T(8,128)(2,1)} %pad_maximum_fusion.7), channel_id=1, source_target_pairs={{0,2},{1,3},{2,0},{3,1},{4,6},{5,7},{6,4},{7,5},{8,10},{9,11},{10,... | collective-permute-start | bytes 491528 | tf_op jit(solution)/shard_map/ppermute | solution.py:872
  16.7 14.9 %collective-permute-start.1 = (bf16[320,256]{1,0:T(8,128)(2,1)}, bf16[320,256]{1,0:T(8,128)(2,1)}, u32[]{:S(2)}, u32[]{:S(2)}) collective-permute-start(bf16[320,256]{1,0:T(8,128)(2,1)} %pad_maximum_fusion.7), channel_id=1, source_target_pairs={{0,1},{1,0},{2,3},{3,2},{4,5},{5,4},{6,7},{7,6},{8,9},{9,8},{10,11... | collective-permute-start | bytes 491528 | tf_op jit(solution)/shard_map/ppermute | solution.py:872
  18.7 40.0 %collective-permute-start = (bf16[16,1024]{1,0:T(8,128)(2,1)}, bf16[16,1024]{1,0:T(8,128)(2,1)}, u32[]{:S(2)}, u32[]{:S(2)}) collective-permute-start(bf16[16,1024]{1,0:T(8,128)(2,1)} %slice.193), channel_id=1, source_target_pairs={{0,1},{1,2},{2,3},{3,4},{4,5},{5,6},{6,7},{7,8},{8,9},{9,10},{10,1... | collective-permute-start | bytes 98312 | tf_op jit(solution)/shard_map/ppermute | solution.py:867
  21.4 2.3 copy-start.1
  23.7 9.1 %copy-start.2 = (bf16[4,512,256]{2,1,0:T(8,128)(2,1)}, bf16[4,512,256]{2,1,0:T(8,128)(2,1)S(1)}, u32[]{:S(2)}) copy-start(bf16[4,512,256]{2,1,0:T(8,128)(2,1)S(1)} %pad_maximum_fusion.rest_9_) | copy-start | bytes 3145732
  24.6 211.8 %reduce-scatter.3.cloned.1.call-start = ((), (), s32[]{:S(2)}) async-start(), calls=%async_computation.2 | async-start | bytes 9437184 | tf_op jit(solution)/shard_map/reduce_scatter | solution.py:987
  32.8 24.7 %copy-start = (bf16[3,320,256]{2,1,0:T(8,128)(2,1)}, bf16[3,320,256]{2,1,0:T(8,128)(2,1)S(1)}, u32[]{:S(2)}) copy-start(bf16[3,320,256]{2,1,0:T(8,128)(2,1)S(1)} %pad_maximum_fusion.1.rest_1_) | copy-start | bytes 1474564
  32.8 22.4 %collective-permute-start.7 = (bf16[3,320,256]{2,1,0:T(8,128)(2,1)S(1)}, bf16[3,320,256]{2,1,0:T(8,128)(2,1)S(1)}, u32[]{:S(2)}, u32[]{:S(2)}) collective-permute-start(bf16[3,320,256]{2,1,0:T(8,128)(2,1)S(1)} %pad_maximum_fusion.1.rest_1_), channel_id=1, source_target_pairs={{0,24},{1,25},{2,26},{3,27},{4,28},{5,29},{6,30},{7,31},{8,16},{9,... | collective-permute-start | bytes 1474568 | tf_op jit(solution)/shard_map/ppermute | solution.py:872
  35.3 21.2 %collective-permute-start.6 = (bf16[3,320,256]{2,1,0:T(8,128)(2,1)S(1)}, bf16[3,320,256]{2,1,0:T(8,128)(2,1)S(1)}, u32[]{:S(2)}, u32[]{:S(2)}) collective-permute-start(bf16[3,320,256]{2,1,0:T(8,128)(2,1)S(1)} %pad_maximum_fusion.1.rest_1_), channel_id=1, source_target_pairs={{0,16},{1,17},{2,18},{3,19},{4,20},{5,21},{6,22},{7,23},{8,24},{9,... | collective-permute-start | bytes 1474568 | tf_op jit(solution)/shard_map/ppermute | solution.py:872
  35.8 20.9 %collective-permute-start.5 = (bf16[3,320,256]{2,1,0:T(8,128)(2,1)S(1)}, bf16[3,320,256]{2,1,0:T(8,128)(2,1)}, u32[]{:S(2)}, u32[]{:S(2)}) collective-permute-start(bf16[3,320,256]{2,1,0:T(8,128)(2,1)S(1)} %pad_maximum_fusion.1.rest_1_), channel_id=1, source_target_pairs={{0,8},{1,9},{2,10},{3,11},{4,12},{5,13},{6,14},{7,15},{8,0},{9,1},... | collective-permute-start | bytes 1474568 | tf_op jit(solution)/shard_map/ppermute | solution.py:872
  39.4 21.0 %collective-permute-start.4 = (bf16[3,320,256]{2,1,0:T(8,128)(2,1)S(1)}, bf16[3,320,256]{2,1,0:T(8,128)(2,1)}, u32[]{:S(2)}, u32[]{:S(2)}) collective-permute-start(bf16[3,320,256]{2,1,0:T(8,128)(2,1)S(1)} %pad_maximum_fusion.1.rest_1_), channel_id=1, source_target_pairs={{0,4},{1,5},{2,6},{3,7},{4,0},{5,1},{6,2},{7,3},{8,12},{9,13},{10,... | collective-permute-start | bytes 1474568 | tf_op jit(solution)/shard_map/ppermute | solution.py:872
  55.2 34.3 %copy-start.4 = (bf16[3,512,256]{2,1,0:T(8,128)(2,1)}, bf16[3,512,256]{2,1,0:T(8,128)(2,1)S(1)}, u32[]{:S(2)}) copy-start(bf16[3,512,256]{2,1,0:T(8,128)(2,1)S(1)} %broadcast_select_fusion.rest_1_.rest_10_) | copy-start | bytes 2359300
  55.2 7.8 %copy-start.6 = (bf16[3,320,256]{2,1,0:T(8,128)(2,1)}, bf16[3,320,256]{2,1,0:T(8,128)(2,1)S(1)}, u32[]{:S(2)}) copy-start(bf16[3,320,256]{2,1,0:T(8,128)(2,1)S(1)} %collective-permute-done.7.rest_7_) | copy-start | bytes 1474564
  56.6 6.5 %copy-start.7 = (bf16[3,320,256]{2,1,0:T(8,128)(2,1)}, bf16[3,320,256]{2,1,0:T(8,128)(2,1)S(1)}, u32[]{:S(2)}) copy-start(bf16[3,320,256]{2,1,0:T(8,128)(2,1)S(1)} %collective-permute-done.6.rest_5_) | copy-start | bytes 1474564
  56.8 4.9 %collective-permute-start.8 = (bf16[3,320,256]{2,1,0:T(8,128)(2,1)}, bf16[3,320,256]{2,1,0:T(8,128)(2,1)S(1)}, u32[]{:S(2)}, u32[]{:S(2)}) collective-permute-start(bf16[3,320,256]{2,1,0:T(8,128)(2,1)} %collective-permute-done.5.rest_3_), channel_id=1, source_target_pairs={{0,4},{1,5},{2,6},{3,7},{4,0},{5,1},{6,2},{7,3},{8,12},{9,13},{10,... | collective-permute-start | bytes 1474568 | tf_op jit(solution)/shard_map/ppermute | solution.py:872
  57.5 5.5 %collective-permute-start.9 = (bf16[3,320,256]{2,1,0:T(8,128)(2,1)S(1)}, bf16[3,320,256]{2,1,0:T(8,128)(2,1)}, u32[]{:S(2)}, u32[]{:S(2)}) collective-permute-start(bf16[3,320,256]{2,1,0:T(8,128)(2,1)S(1)} %collective-permute-done.6.rest_5_), channel_id=1, source_target_pairs={{0,4},{1,5},{2,6},{3,7},{4,0},{5,1},{6,2},{7,3},{8,12},{9,13},{10,... | collective-permute-start | bytes 1474568 | tf_op jit(solution)/shard_map/ppermute | solution.py:872
  58.0 5.0 %collective-permute-start.10 = (bf16[3,320,256]{2,1,0:T(8,128)(2,1)S(1)}, bf16[3,320,256]{2,1,0:T(8,128)(2,1)}, u32[]{:S(2)}, u32[]{:S(2)}) collective-permute-start(bf16[3,320,256]{2,1,0:T(8,128)(2,1)S(1)} %collective-permute-done.7.rest_7_), channel_id=1, source_target_pairs={{0,4},{1,5},{2,6},{3,7},{4,0},{5,1},{6,2},{7,3},{8,12},{9,13},{10,... | collective-permute-start | bytes 1474568 | tf_op jit(solution)/shard_map/ppermute | solution.py:872
  58.7 45.8 %collective-permute-start.17 = (bf16[3,512,256]{2,1,0:T(8,128)(2,1)S(1)}, bf16[3,512,256]{2,1,0:T(8,128)(2,1)}, u32[]{:S(2)}, u32[]{:S(2)}) collective-permute-start(bf16[3,512,256]{2,1,0:T(8,128)(2,1)S(1)} %broadcast_select_fusion.rest_1_.rest_10_), channel_id=1, source_target_pairs={{0,24},{1,25},{2,26},{3,27},{4,28},{5,29},{6,30},{7,31},{8,16},{9,... | collective-permute-start | bytes 2359304 | tf_op jit(solution)/shard_map/ppermute | solution.py:872
  60.3 43.5 %collective-permute-start.14 = (bf16[3,512,256]{2,1,0:T(8,128)(2,1)S(1)}, bf16[3,512,256]{2,1,0:T(8,128)(2,1)}, u32[]{:S(2)}, u32[]{:S(2)}) collective-permute-start(bf16[3,512,256]{2,1,0:T(8,128)(2,1)S(1)} %broadcast_select_fusion.rest_1_.rest_10_), channel_id=1, source_target_pairs={{0,16},{1,17},{2,18},{3,19},{4,20},{5,21},{6,22},{7,23},{8,24},{9,... | collective-permute-start | bytes 2359304 | tf_op jit(solution)/shard_map/ppermute | solution.py:872
  61.6 1.4 copy-start.8
  61.6 42.2 %collective-permute-start.13 = (bf16[3,512,256]{2,1,0:T(8,128)(2,1)S(1)}, bf16[3,512,256]{2,1,0:T(8,128)(2,1)}, u32[]{:S(2)}, u32[]{:S(2)}) collective-permute-start(bf16[3,512,256]{2,1,0:T(8,128)(2,1)S(1)} %broadcast_select_fusion.rest_1_.rest_10_), channel_id=1, source_target_pairs={{0,8},{1,9},{2,10},{3,11},{4,12},{5,13},{6,14},{7,15},{8,0},{9,1},... | collective-permute-start | bytes 2359304 | tf_op jit(solution)/shard_map/ppermute | solution.py:872
  89.0 17.3 %collective-permute-start.11 = (bf16[128,2048]{1,0:T(8,128)(2,1)}, bf16[128,2048]{1,0:T(8,128)(2,1)S(1)}, u32[]{:S(2)}, u32[]{:S(2)}) collective-permute-start(bf16[128,2048]{1,0:T(8,128)(2,1)} %get-tuple-element.77), channel_id=1, source_target_pairs={{0,1},{1,2},{2,3},{3,4},{4,5},{5,6},{6,7},{7,8},{8,9},{9,10},{10,1... | collective-permute-start | bytes 1572872 | tf_op jit(solution)/shard_map/ppermute | solution.py:867
  89.5 19.1 %collective-permute-start.12 = (bf16[3,512,256]{2,1,0:T(8,128)(2,1)S(1)}, bf16[3,512,256]{2,1,0:T(8,128)(2,1)S(1)}, u32[]{:S(2)}, u32[]{:S(2)}) collective-permute-start(bf16[3,512,256]{2,1,0:T(8,128)(2,1)S(1)} %broadcast_select_fusion.rest_1_.rest_10_), channel_id=1, source_target_pairs={{0,4},{1,5},{2,6},{3,7},{4,0},{5,1},{6,2},{7,3},{8,12},{9,13},{10,... | collective-permute-start | bytes 2359304 | tf_op jit(solution)/shard_map/ppermute | solution.py:872
  103.8 4.9 %collective-permute-start.15 = (bf16[3,512,256]{2,1,0:T(8,128)(2,1)}, bf16[3,512,256]{2,1,0:T(8,128)(2,1)S(1)}, u32[]{:S(2)}, u32[]{:S(2)}) collective-permute-start(bf16[3,512,256]{2,1,0:T(8,128)(2,1)} %collective-permute-done.13.rest_3_.rest_12_), channel_id=1, source_target_pairs={{0,4},{1,5},{2,6},{3,7},{4,0},{5,1},{6,2},{7,3},{8,12},{9,13},{10,... | collective-permute-start | bytes 2359304 | tf_op jit(solution)/shard_map/ppermute | solution.py:872
  104.4 4.3 %collective-permute-start.16 = (bf16[3,512,256]{2,1,0:T(8,128)(2,1)}, bf16[3,512,256]{2,1,0:T(8,128)(2,1)}, u32[]{:S(2)}, u32[]{:S(2)}) collective-permute-start(bf16[3,512,256]{2,1,0:T(8,128)(2,1)} %collective-permute-done.14.rest_5_.rest_14_), channel_id=1, source_target_pairs={{0,4},{1,5},{2,6},{3,7},{4,0},{5,1},{6,2},{7,3},{8,12},{9,13},{10,... | collective-permute-start | bytes 2359304 | tf_op jit(solution)/shard_map/ppermute | solution.py:872
  106.3 2.6 collective-permute-start.18
  148.0 19.4 %collective-permute-start.19 = (bf16[128,2048]{1,0:T(8,128)(2,1)}, bf16[128,2048]{1,0:T(8,128)(2,1)S(1)}, u32[]{:S(2)}, u32[]{:S(2)}) collective-permute-start(bf16[128,2048]{1,0:T(8,128)(2,1)} %get-tuple-element.90), channel_id=1, source_target_pairs={{0,31},{1,0},{2,1},{3,2},{4,3},{5,4},{6,5},{7,6},{8,7},{9,8},{10,9... | collective-permute-start | bytes 1572872 | tf_op jit(solution)/shard_map/ppermute | solution.py:867
  168.2 97.7 %reduce-scatter.5.cloned.1.call-start = ((), (), s32[]{:S(2)}) async-start(), calls=%async_computation.3 | async-start | bytes 1310720 | tf_op jit(solution)/shard_map/reduce_scatter | solution.py:995
  214.3 8.5 %collective-permute-start.20 = (bf16[16,2432]{1,0:T(8,128)(2,1)}, bf16[16,2432]{1,0:T(8,128)(2,1)S(1)}, u32[]{:S(2)}, u32[]{:S(2)}) collective-permute-start(bf16[16,2432]{1,0:T(8,128)(2,1)} %get-tuple-element.96), channel_id=1, source_target_pairs={{0,31},{1,0},{2,1},{3,2},{4,3},{5,4},{6,5},{7,6},{8,7},{9,8},{10,9... | collective-permute-start | bytes 233480 | tf_op jit(solution)/shard_map/ppermute | solution.py:867
  222.8 7.8 %copy-start.30 = (bf16[16,2432]{1,0:T(8,128)(2,1)}, bf16[16,2432]{1,0:T(8,128)(2,1)S(1)}, u32[]{:S(2)}) copy-start(bf16[16,2432]{1,0:T(8,128)(2,1)S(1)} %collective-permute-done.20.ahead_ref) | copy-start | bytes 233476
  222.8 7.8 %collective-permute-start.21 = (bf16[4,4,304,256]{3,2,1,0:T(8,128)(2,1)}, bf16[4,4,304,256]{3,2,1,0:T(8,128)(2,1)S(1)}, u32[]{:S(2)}, u32[]{:S(2)}) collective-permute-start(bf16[4,4,304,256]{3,2,1,0:T(8,128)(2,1)} %conv_grad.3), channel_id=1, source_target_pairs={{0,4},{1,5},{2,6},{3,7},{4,0},{5,1},{6,2},{7,3},{8,12},{9,13},{10,... | collective-permute-start | bytes 7471112 | tf_op jit(solution)/shard_map/ppermute | solution.py:872
  236.4 31.0 %collective-permute-start.24 = (bf16[4,304,256]{2,1,0:T(8,128)(2,1)S(1)}, bf16[4,304,256]{2,1,0:T(8,128)(2,1)S(1)}, u32[]{:S(2)}, u32[]{:S(2)}) collective-permute-start(bf16[4,304,256]{2,1,0:T(8,128)(2,1)S(1)} %get-tuple-element.139), channel_id=1, source_target_pairs={{0,24},{1,25},{2,26},{3,27},{4,28},{5,29},{6,30},{7,31},{8,16},{9,... | collective-permute-start | bytes 1867784 | tf_op jit(solution)/shard_map/ppermute | solution.py:872
  237.9 29.5 %collective-permute-start.23 = (bf16[4,304,256]{2,1,0:T(8,128)(2,1)S(1)}, bf16[4,304,256]{2,1,0:T(8,128)(2,1)}, u32[]{:S(2)}, u32[]{:S(2)}) collective-permute-start(bf16[4,304,256]{2,1,0:T(8,128)(2,1)S(1)} %get-tuple-element.140), channel_id=1, source_target_pairs={{0,16},{1,17},{2,18},{3,19},{4,20},{5,21},{6,22},{7,23},{8,24},{9,... | collective-permute-start | bytes 1867784 | tf_op jit(solution)/shard_map/ppermute | solution.py:872
  239.3 28.1 %collective-permute-start.22 = (bf16[4,304,256]{2,1,0:T(8,128)(2,1)S(1)}, bf16[4,304,256]{2,1,0:T(8,128)(2,1)}, u32[]{:S(2)}, u32[]{:S(2)}) collective-permute-start(bf16[4,304,256]{2,1,0:T(8,128)(2,1)S(1)} %get-tuple-element.141), channel_id=1, source_target_pairs={{0,8},{1,9},{2,10},{3,11},{4,12},{5,13},{6,14},{7,15},{8,0},{9,1},... | collective-permute-start | bytes 1867784 | tf_op jit(solution)/shard_map/ppermute | solution.py:872
  239.9 26.0 %copy-start.25 = (f32[8,2304]{1,0:T(8,128)S(1)}, f32[8,2304]{1,0:T(8,128)}, u32[]{:S(2)}) copy-start(f32[8,2304]{1,0:T(8,128)} %get-tuple-element.109) | copy-start | bytes 221188
  267.4 5.4 %copy-start.9 = (bf16[1,512,256]{2,1,0:T(8,128)(2,1)S(1)}, bf16[1,512,256]{2,1,0:T(8,128)(2,1)}, u32[]{:S(2)}) copy-start(bf16[1,512,256]{2,1,0:T(8,128)(2,1)} %reduce-scatter.5.cloned.1.call-done) | copy-start | bytes 786436
  269.1 14.9 %collective-permute-start.26 = (bf16[336,256]{1,0:T(8,128)(2,1)S(1)}, bf16[336,256]{1,0:T(8,128)(2,1)S(1)}, u32[]{:S(2)}, u32[]{:S(2)}) collective-permute-start(bf16[336,256]{1,0:T(8,128)(2,1)S(1)} %pad_maximum_fusion.4), channel_id=1, source_target_pairs={{0,2},{1,3},{2,0},{3,1},{4,6},{5,7},{6,4},{7,5},{8,10},{9,11},{10,... | collective-permute-start | bytes 516104 | tf_op jit(solution)/shard_map/ppermute | solution.py:872
  270.8 14.6 %collective-permute-start.27 = (bf16[336,256]{1,0:T(8,128)(2,1)S(1)}, bf16[336,256]{1,0:T(8,128)(2,1)S(1)}, u32[]{:S(2)}, u32[]{:S(2)}) collective-permute-start(bf16[336,256]{1,0:T(8,128)(2,1)S(1)} %pad_maximum_fusion.5), channel_id=1, source_target_pairs={{0,3},{1,2},{2,1},{3,0},{4,7},{5,6},{6,5},{7,4},{8,11},{9,10},{10,... | collective-permute-start | bytes 516104 | tf_op jit(solution)/shard_map/ppermute | solution.py:872
  272.3 13.1 %collective-permute-start.25 = (bf16[336,256]{1,0:T(8,128)(2,1)S(1)}, bf16[336,256]{1,0:T(8,128)(2,1)S(1)}, u32[]{:S(2)}, u32[]{:S(2)}) collective-permute-start(bf16[336,256]{1,0:T(8,128)(2,1)S(1)} %pad_maximum_fusion.3), channel_id=1, source_target_pairs={{0,1},{1,0},{2,3},{3,2},{4,5},{5,4},{6,7},{7,6},{8,9},{9,8},{10,11... | collective-permute-start | bytes 516104 | tf_op jit(solution)/shard_map/ppermute | solution.py:872
  272.9 14.2 %collective-permute-start.40 = (bf16[512,256]{1,0:T(8,128)(2,1)S(1)}, bf16[512,256]{1,0:T(8,128)(2,1)S(1)}, u32[]{:S(2)}, u32[]{:S(2)}) collective-permute-start(bf16[512,256]{1,0:T(8,128)(2,1)S(1)} %bitcast.77), channel_id=1, source_target_pairs={{0,24},{1,25},{2,26},{3,27},{4,28},{5,29},{6,30},{7,31},{8,16},{9,... | collective-permute-start | bytes 786440 | tf_op jit(solution)/shard_map/ppermute | solution.py:872
  275.2 12.1 %collective-permute-start.38 = (bf16[512,256]{1,0:T(8,128)(2,1)S(1)}, bf16[512,256]{1,0:T(8,128)(2,1)S(1)}, u32[]{:S(2)}, u32[]{:S(2)}) collective-permute-start(bf16[512,256]{1,0:T(8,128)(2,1)S(1)} %bitcast.78), channel_id=1, source_target_pairs={{0,16},{1,17},{2,18},{3,19},{4,20},{5,21},{6,22},{7,23},{8,24},{9,... | collective-permute-start | bytes 786440 | tf_op jit(solution)/shard_map/ppermute | solution.py:872
  284.0 9.1 %collective-permute-start.36 = (bf16[512,256]{1,0:T(8,128)(2,1)S(1)}, bf16[512,256]{1,0:T(8,128)(2,1)S(1)}, u32[]{:S(2)}, u32[]{:S(2)}) collective-permute-start(bf16[512,256]{1,0:T(8,128)(2,1)S(1)} %bitcast.79), channel_id=1, source_target_pairs={{0,8},{1,9},{2,10},{3,11},{4,12},{5,13},{6,14},{7,15},{8,0},{9,1},... | collective-permute-start | bytes 786440 | tf_op jit(solution)/shard_map/ppermute | solution.py:872
  285.4 9.2 %collective-permute-start.35 = (bf16[512,256]{1,0:T(8,128)(2,1)S(1)}, bf16[512,256]{1,0:T(8,128)(2,1)S(1)}, u32[]{:S(2)}, u32[]{:S(2)}) collective-permute-start(bf16[512,256]{1,0:T(8,128)(2,1)S(1)} %bitcast.80), channel_id=1, source_target_pairs={{0,4},{1,5},{2,6},{3,7},{4,0},{5,1},{6,2},{7,3},{8,12},{9,13},{10,... | collective-permute-start | bytes 786440 | tf_op jit(solution)/shard_map/ppermute | solution.py:872
  285.6 20.9 %copy-start.5 = (bf16[336,256]{1,0:T(8,128)(2,1)}, bf16[336,256]{1,0:T(8,128)(2,1)S(1)}, u32[]{:S(2)}) copy-start(bf16[336,256]{1,0:T(8,128)(2,1)S(1)} %pad_maximum_fusion.6.rest_0_) | copy-start | bytes 516100
  285.6 12.2 %collective-permute-start.33 = (bf16[336,256]{1,0:T(8,128)(2,1)S(1)}, bf16[336,256]{1,0:T(8,128)(2,1)S(1)}, u32[]{:S(2)}, u32[]{:S(2)}) collective-permute-start(bf16[336,256]{1,0:T(8,128)(2,1)S(1)} %pad_maximum_fusion.6.rest_0_), channel_id=1, source_target_pairs={{0,24},{1,25},{2,26},{3,27},{4,28},{5,29},{6,30},{7,31},{8,16},{9,... | collective-permute-start | bytes 516104 | tf_op jit(solution)/shard_map/ppermute | solution.py:872
  287.1 13.6 %copy-start.10 = (bf16[512,256]{1,0:T(8,128)(2,1)}, bf16[512,256]{1,0:T(8,128)(2,1)S(1)}, u32[]{:S(2)}) copy-start(bf16[512,256]{1,0:T(8,128)(2,1)S(1)} %collective-permute-done.40.rest_6_) | copy-start | bytes 786436
  287.1 13.0 %collective-permute-start.41 = (bf16[512,256]{1,0:T(8,128)(2,1)S(1)}, bf16[512,256]{1,0:T(8,128)(2,1)S(1)}, u32[]{:S(2)}, u32[]{:S(2)}) collective-permute-start(bf16[512,256]{1,0:T(8,128)(2,1)S(1)} %collective-permute-done.40.rest_6_), channel_id=1, source_target_pairs={{0,4},{1,5},{2,6},{3,7},{4,0},{5,1},{6,2},{7,3},{8,12},{9,13},{10,... | collective-permute-start | bytes 786440 | tf_op jit(solution)/shard_map/ppermute | solution.py:872
  287.3 13.3 %copy-start.11 = (bf16[512,256]{1,0:T(8,128)(2,1)}, bf16[512,256]{1,0:T(8,128)(2,1)S(1)}, u32[]{:S(2)}) copy-start(bf16[512,256]{1,0:T(8,128)(2,1)S(1)} %collective-permute-done.38.rest_4_) | copy-start | bytes 786436
  287.3 13.2 %collective-permute-start.39 = (bf16[512,256]{1,0:T(8,128)(2,1)S(1)}, bf16[512,256]{1,0:T(8,128)(2,1)S(1)}, u32[]{:S(2)}, u32[]{:S(2)}) collective-permute-start(bf16[512,256]{1,0:T(8,128)(2,1)S(1)} %collective-permute-done.38.rest_4_), channel_id=1, source_target_pairs={{0,4},{1,5},{2,6},{3,7},{4,0},{5,1},{6,2},{7,3},{8,12},{9,13},{10,... | collective-permute-start | bytes 786440 | tf_op jit(solution)/shard_map/ppermute | solution.py:872
  293.1 7.5 %copy-start.12 = (bf16[512,256]{1,0:T(8,128)(2,1)}, bf16[512,256]{1,0:T(8,128)(2,1)S(1)}, u32[]{:S(2)}) copy-start(bf16[512,256]{1,0:T(8,128)(2,1)S(1)} %collective-permute-done.36.rest_2_) | copy-start | bytes 786436
  293.1 5.9 %collective-permute-start.31 = (bf16[336,256]{1,0:T(8,128)(2,1)S(1)}, bf16[336,256]{1,0:T(8,128)(2,1)S(1)}, u32[]{:S(2)}, u32[]{:S(2)}) collective-permute-start(bf16[336,256]{1,0:T(8,128)(2,1)S(1)} %pad_maximum_fusion.6.rest_0_), channel_id=1, source_target_pairs={{0,16},{1,17},{2,18},{3,19},{4,20},{5,21},{6,22},{7,23},{8,24},{9,... | collective-permute-start | bytes 516104 | tf_op jit(solution)/shard_map/ppermute | solution.py:872
  294.6 6.0 %copy-start.13 = (bf16[512,256]{1,0:T(8,128)(2,1)}, bf16[512,256]{1,0:T(8,128)(2,1)S(1)}, u32[]{:S(2)}) copy-start(bf16[512,256]{1,0:T(8,128)(2,1)S(1)} %collective-permute-done.35.rest_1_) | copy-start | bytes 786436
  294.6 5.4 %collective-permute-start.29 = (bf16[336,256]{1,0:T(8,128)(2,1)S(1)}, bf16[336,256]{1,0:T(8,128)(2,1)S(1)}, u32[]{:S(2)}, u32[]{:S(2)}) collective-permute-start(bf16[336,256]{1,0:T(8,128)(2,1)S(1)} %pad_maximum_fusion.6.rest_0_), channel_id=1, source_target_pairs={{0,8},{1,9},{2,10},{3,11},{4,12},{5,13},{6,14},{7,15},{8,0},{9,1},... | collective-permute-start | bytes 516104 | tf_op jit(solution)/shard_map/ppermute | solution.py:872
  297.8 8.7 %copy-start.17 = (bf16[336,256]{1,0:T(8,128)(2,1)}, bf16[336,256]{1,0:T(8,128)(2,1)S(1)}, u32[]{:S(2)}) copy-start(bf16[336,256]{1,0:T(8,128)(2,1)S(1)} %collective-permute-done.33.rest_6_) | copy-start | bytes 516100
  297.8 2.9 collective-permute-start.37
  299.1 7.4 %copy-start.18 = (bf16[336,256]{1,0:T(8,128)(2,1)}, bf16[336,256]{1,0:T(8,128)(2,1)S(1)}, u32[]{:S(2)}) copy-start(bf16[336,256]{1,0:T(8,128)(2,1)S(1)} %collective-permute-done.31.rest_4_) | copy-start | bytes 516100
  299.1 7.2 %collective-permute-start.28 = (bf16[336,256]{1,0:T(8,128)(2,1)S(1)}, bf16[336,256]{1,0:T(8,128)(2,1)S(1)}, u32[]{:S(2)}, u32[]{:S(2)}) collective-permute-start(bf16[336,256]{1,0:T(8,128)(2,1)S(1)} %pad_maximum_fusion.6.rest_0_), channel_id=1, source_target_pairs={{0,4},{1,5},{2,6},{3,7},{4,0},{5,1},{6,2},{7,3},{8,12},{9,13},{10,... | collective-permute-start | bytes 516104 | tf_op jit(solution)/shard_map/ppermute | solution.py:872
  300.0 6.4 %copy-start.19 = (bf16[336,256]{1,0:T(8,128)(2,1)}, bf16[336,256]{1,0:T(8,128)(2,1)S(1)}, u32[]{:S(2)}) copy-start(bf16[336,256]{1,0:T(8,128)(2,1)S(1)} %collective-permute-done.29.rest_2_) | copy-start | bytes 516100
  300.0 6.3 %collective-permute-start.34 = (bf16[336,256]{1,0:T(8,128)(2,1)S(1)}, bf16[336,256]{1,0:T(8,128)(2,1)S(1)}, u32[]{:S(2)}, u32[]{:S(2)}) collective-permute-start(bf16[336,256]{1,0:T(8,128)(2,1)S(1)} %collective-permute-done.33.rest_6_), channel_id=1, source_target_pairs={{0,4},{1,5},{2,6},{3,7},{4,0},{5,1},{6,2},{7,3},{8,12},{9,13},{10,... | collective-permute-start | bytes 516104 | tf_op jit(solution)/shard_map/ppermute | solution.py:872
  300.1 6.3 %collective-permute-start.32 = (bf16[336,256]{1,0:T(8,128)(2,1)S(1)}, bf16[336,256]{1,0:T(8,128)(2,1)S(1)}, u32[]{:S(2)}, u32[]{:S(2)}) collective-permute-start(bf16[336,256]{1,0:T(8,128)(2,1)S(1)} %collective-permute-done.31.rest_4_), channel_id=1, source_target_pairs={{0,4},{1,5},{2,6},{3,7},{4,0},{5,1},{6,2},{7,3},{8,12},{9,13},{10,... | collective-permute-start | bytes 516104 | tf_op jit(solution)/shard_map/ppermute | solution.py:872
  300.6 5.8 %collective-permute-start.30 = (bf16[336,256]{1,0:T(8,128)(2,1)S(1)}, bf16[336,256]{1,0:T(8,128)(2,1)S(1)}, u32[]{:S(2)}, u32[]{:S(2)}) collective-permute-start(bf16[336,256]{1,0:T(8,128)(2,1)S(1)} %collective-permute-done.29.rest_2_), channel_id=1, source_target_pairs={{0,4},{1,5},{2,6},{3,7},{4,0},{5,1},{6,2},{7,3},{8,12},{9,13},{10,... | collective-permute-start | bytes 516104 | tf_op jit(solution)/shard_map/ppermute | solution.py:872
  (12 other events, 9.4 us)
Sparse Core Ops, SparseCore 0:
  24.7 28.4 all-gather.2
  167.6 68.6 reduce-scatter.2
  238.8 27.0 reduce-scatter.4
